TPU v7x, 32 devices: a whole 2x2x4 slice. The times are simulated.
32 devices in a mesh: dom: 16 (over z, x, core), split: 2 (over y).
Axes of the slice: x: 2, y: 2, z: 4, core: 2. Of those that a mesh axis runs over, the one named last changes fastest.
Arguments:
- modes_now: float32 [64, 1024, 128], P('split', 'dom'), may hold values from -6 to 6
- modes_prev: float32 [64, 1024, 128], P('split', 'dom'), may hold values from -6 to 6
- z_extent: int32 [16], P('dom'), may hold values from 16 to 64, as said below
- lower_nbr: int32 [16], P('dom'), may hold values from -1 to 15, as said below
- upper_nbr: int32 [16], P('dom'), may hold values from -1 to 15
- x_shift: int32 [16, 2], P('dom'), may hold values from -32 to 32, as said below
- y_shift: int32 [16, 2], P('dom'), may hold values from -32 to 32, as said below
Outputs:
- modes_next: float32 [64, 1024, 128], P('split', 'dom')
- modes_cur: float32 [64, 1024, 128], P('split', 'dom')
- pressure: float32 [64, 1024, 128], P('split', 'dom')
Inputs may be any that keep to these rules, and one draw needn't show every extreme that they name: `z_extent`: at least one cuboid reaches the full 64 slots. Cuboids form chains: if upper_nbr[a] = b then lower_nbr[b] = a, and no cuboid is its own neighbour. If upper_nbr[a] = b then x_shift[a, 1] = -x_shift[b, 0]; zero at walls. If upper_nbr[a] = b then y_shift[a, 1] = -y_shift[b, 0]; zero at walls.
All inputs are finite; a program needn't handle non-finite values.
Results may differ from a plain program's by a relative error of at most 0.0003.
Values sent between devices are 32-bit elements; how exact they have to be, the bound alone decides.
No kernel may reach another device: no remote copies, remote signals or barrier semaphores. Data moves between devices by JAX's collectives and lax.ppermute only.
A program may use at most 64 MiB of HBM per device.

v0:
```python
import functools
import math

import jax
import jax.numpy as jnp
import numpy as np
from jax import lax
from jax.experimental import pallas as pl
from jax.experimental.pallas import tpu as pltpu
from jax.sharding import PartitionSpec as P

HIGH = lax.Precision.HIGHEST
F32 = jnp.float32
BF16 = jnp.bfloat16
STENCIL = (-490.0 / 180.0, 270.0 / 180.0, -27.0 / 180.0, 2.0 / 180.0)
COURANT = 0.5
FACE = 3
ROWS = 2 * FACE
HEAD = 8
TERMS = 9
SERIES = [(-1) ** n * 2.0 / math.factorial(2 * n + 2) for n in range(TERMS)]
BASE = (COURANT * math.pi) ** 2
PAIRS = [(r, q) for r in range(ROWS) for q in range(r, ROWS)]
VMEM = pl.BlockSpec(memory_space=pltpu.VMEM)
SMEM = pl.BlockSpec(memory_space=pltpu.SMEM)
ANY = pl.BlockSpec(memory_space=pl.ANY)
LIMIT = 40 * 1024 * 1024


def static_table(count):
    kk = np.arange(count)[:, None]
    xx = np.arange(count)[None, :]
    scale = np.where(kk == 0, np.sqrt(1.0 / count), np.sqrt(2.0 / count))
    return scale * np.cos(np.pi * kk * (xx + 0.5) / count)


def halves(table):
    high = table.astype(np.float32).astype(BF16)
    low = (table.astype(np.float32) - high.astype(np.float32)).astype(BF16)
    return high, low


def inner_size(count):
    best = 1
    for n in range(1, count + 1):
        if count % n == 0 and n * n <= count:
            best = n
    return best


def tall_split(data):
    high = data.astype(BF16).astype(F32)
    return jnp.concatenate([high, high, data - high], axis=0).astype(BF16)


def wide_split(data):
    high = data.astype(BF16)
    return jnp.concatenate([high, (data - high.astype(F32)).astype(BF16)], axis=1)


def dot(left, right):
    return jnp.dot(left, right, preferred_element_type=F32)


def exact_dot(left, right):
    return jnp.dot(left, right, precision=HIGH, preferred_element_type=F32)


def exact_dot_t(left, right):
    return lax.dot_general(
        left, right, (((1,), (1,)), ((), ())), precision=HIGH, preferred_element_type=F32
    )


def along_y(data, ystack):
    width = data.shape[1]
    both = dot(wide_split(data), ystack)
    return both[:, :width] + both[:, width:]


def cosine_of(count, odd, lenf):
    prod = count * odd
    turn = 4.0 * lenf
    rest = prod - jnp.floor(prod / turn) * turn
    return jnp.cos(rest * (0.5 * jnp.pi / lenf))


def scale_of(kk, lenf):
    return jnp.where(kk == 0, jnp.sqrt(1.0 / lenf), jnp.sqrt(2.0 / lenf))


def face_rows(near, flip, shape, extent):
    kk = lax.broadcasted_iota(jnp.int32, shape, 0)
    kf = kk.astype(F32)
    lenf = jnp.full(shape, extent.astype(F32))
    table = scale_of(kk, lenf) * cosine_of(kf, 2.0 * near + 1.0, lenf)
    sign = jnp.where((flip > 0) & (kk % 2 == 1), -1.0, 1.0)
    return jnp.where(kk < extent, table * sign, 0.0)


def gain_of(square):
    total = jnp.full_like(square, SERIES[-1])
    for value in reversed(SERIES[:-1]):
        total = total * square + value
    return total


def plane_square(shape, extent):
    kk = lax.broadcasted_iota(jnp.int32, shape, 0)
    kf = kk.astype(F32) / jnp.full(shape, extent.astype(F32))
    kf = jnp.where(kk < extent, kf, 0.0)
    ky = lax.broadcasted_iota(jnp.int32, shape, 1).astype(F32) / shape[1]
    return BASE * (kf * kf + ky * ky)


def x_square(kx, full):
    frac = kx.astype(F32) / full
    return BASE * (frac * frac)


def stencil(face, order):
    rows = []
    for jj in range(FACE):
        total = None
        for mm in range(FACE - jj):
            term = STENCIL[jj + mm + 1] * face[order[mm]]
            total = term if total is None else total + term
        rows.append(total)
    return rows


def through(planes, across, along):
    full, width = planes[0].shape
    out = exact_dot(across, jnp.concatenate(planes, axis=1))
    out = jnp.concatenate([out[:, i * width : (i + 1) * width] for i in range(FACE)], axis=0)
    out = exact_dot_t(out, along)
    return [out[i * full : (i + 1) * full] for i in range(FACE)]


def gather_kx(out, pieces, own):
    count = len(pieces)
    slab = pieces[0].shape[0] // ROWS
    full = slab * count
    for k, piece in enumerate(pieces):
        at = pl.multiple_of(lax.rem(own + count - k, count) * slab, slab)
        for r in range(ROWS):
            out[pl.ds(r * full + at, slab), :] = piece[r * slab : (r + 1) * slab, :]


def plane(ref, r):
    full = ref.shape[0] // ROWS
    return ref[r * full : (r + 1) * full, :]


def call(kernel, out_shape, in_specs, scratch=(), flops=0, moved=0, name=None, out_specs=None):
    if out_specs is None:
        out_specs = [VMEM] * len(out_shape)
    return pl.pallas_call(
        kernel,
        out_shape=out_shape,
        in_specs=in_specs,
        out_specs=out_specs,
        scratch_shapes=list(scratch),
        compiler_params=pltpu.CompilerParams(vmem_limit_bytes=LIMIT),
        cost_estimate=pl.CostEstimate(flops=flops, bytes_accessed=moved, transcendentals=0),
        name=name,
    )


def shape_of(*dims, dtype=F32):
    return jax.ShapeDtypeStruct(dims, dtype)


def strip_kernel(extent, below, above, now, lanes, packet, rows):
    slab, zcap, width = now.shape
    table = face_rows(lanes[0:1, :], lanes[1:2, :], (zcap, width), extent[0])
    rows[...] = table
    for r in range(ROWS):
        weight = jnp.broadcast_to(table[:, r : r + 1], (zcap, width))
        packet[r * slab : (r + 1) * slab, :] = jnp.sum(now[...] * weight[None], axis=1)
    at = lax.broadcasted_iota(jnp.int32, (HEAD, width), 0)
    names = jnp.where(at < HEAD // 2, above[0], below[0])
    packet[ROWS * slab :, :] = names.astype(F32)


def ahead_kernel(
    extent, own, now, prev, rows, lanes, series, xparts, ystack,
    strip, free, zstack, coefs, field, *, full,
):
    slab, zcap, width = now.shape
    ext = extent[0]
    kk = lax.broadcasted_iota(jnp.int32, (zcap, zcap), 1)
    zz = lax.broadcasted_iota(jnp.int32, (zcap, zcap), 0)
    lenf = jnp.full((zcap, zcap), ext.astype(F32))
    ztable = scale_of(kk, lenf) * cosine_of(kk.astype(F32), 2.0 * zz.astype(F32) + 1.0, lenf)
    ztable = jnp.where((kk < ext) & (zz < ext), ztable, 0.0)
    high = ztable.astype(BF16).astype(F32)
    stacked = jnp.concatenate([high, ztable - high, high], axis=1).astype(BF16)
    zstack[...] = stacked

    kz = lax.broadcasted_iota(jnp.int32, (zcap, width), 0)
    bz = kz.astype(F32) / jnp.full((zcap, width), ext.astype(F32))
    bz = jnp.where(kz < ext, BASE * bz * bz, 0.0)
    total = jnp.zeros((zcap, width), F32)
    for j in reversed(range(TERMS)):
        total = total * bz + series[j : j + 1, :]
    pairs = face_rows(lanes[2:3, :], lanes[3:4, :], (zcap, width), ext)
    pairs = pairs * face_rows(lanes[4:5, :], lanes[5:6, :], (zcap, width), ext)
    coefs[...] = exact_dot(total.T[: coefs.shape[0]], pairs)

    keep = lax.broadcasted_iota(jnp.int32, (zcap, width), 0) < ext
    square = plane_square((zcap, width), ext)
    weights = [jnp.broadcast_to(rows[:, r : r + 1], (zcap, width)) for r in range(ROWS)]

    def body(i, _):
        frees = []
        for half in range(2):
            kx = 2 * i + half
            local = square + x_square(own[0] * slab + kx, full)
            twice = 2.0 - local * gain_of(local)
            first = jnp.where(keep, now[kx], 0.0)
            ahead = twice * first - jnp.where(keep, prev[kx], 0.0)
            for r in range(ROWS):
                strip[pl.ds(r * slab + kx, 1), :] = jnp.sum(
                    ahead * weights[r], axis=0, keepdims=True
                )
            frees.append(twice * ahead - first)
        wide = dot(stacked, tall_split(jnp.concatenate(frees, axis=1)))
        for half in range(2):
            at = pl.multiple_of((2 * i + half) * zcap, zcap)
            field[pl.ds(at, zcap), :] = wide[:, half * width : (half + 1) * width]
        return 0

    lax.fori_loop(0, slab // 2, body, 0)
    block = min(8, slab) * zcap

    def turn(i, _):
        at = pl.multiple_of(i * block, block)
        field[pl.ds(at, block), :] = along_y(field[pl.ds(at, block), :], ystack[...])
        return 0

    lax.fori_loop(0, slab * zcap // block, turn, 0)
    parts = full // slab
    across = xparts[own[0]]

    def spread(i, _):
        pair = [field[pl.ds(2 * i + half, slab, stride=zcap), :] for half in range(2)]
        wide = dot(across, tall_split(jnp.concatenate(pair, axis=1)))
        for k in range(parts):
            for half in range(2):
                free[k, pl.ds(2 * i + half, slab, stride=zcap), :] = wide[
                    k * slab : (k + 1) * slab, half * width : (half + 1) * width
                ]
        return 0

    lax.fori_loop(0, zcap // 2, spread, 0)


def relation_kernel(
    below, above, x_shift, y_shift, own, coefs, after, xplain, xtall, yplain, ytall, *rest, parts
):
    strips, (tx, uy, vx, wy, near, mixing, mine) = rest[:parts], rest[parts:]
    full, width = xplain.shape[0], yplain.shape[0]
    for f, (nbr, dx, dy) in enumerate(
        ((below, x_shift[0, 0], y_shift[0, 0]), (above, x_shift[0, 1], y_shift[0, 1]))
    ):
        has = jnp.where(nbr[0] >= 0, COURANT**2, 0.0).astype(F32)
        for count, move, plain, tall, take, keep, scale in (
            (full, dx, xplain, xtall, tx, vx, has),
            (width, dy, yplain, ytall, uy, wy, None),
        ):
            move = jnp.clip(move, -count, count)
            slid = tall[pl.ds(count + move, count), :]
            at = lax.broadcasted_iota(jnp.int32, (count, count), 0) + move
            kept = jnp.where((at >= 0) & (at < count), tall[count : 2 * count, :], 0.0)
            taken, stay = exact_dot(plain[...], slid), exact_dot(plain[...], kept)
            take[f] = taken if scale is None else taken * scale
            keep[f] = stay if scale is None else stay * scale
    gather_kx(mine, strips, own[0])
    near_planes(mine, vx, wy, near)
    shape = (full, width)
    ax = lax.broadcasted_iota(jnp.int32, shape, 0).astype(F32) / full
    ay = lax.broadcasted_iota(jnp.int32, shape, 1).astype(F32) / width
    square = BASE * (ax * ax + ay * ay)
    for p in range(len(PAIRS)):
        total = jnp.full(shape, coefs[TERMS - 1, p])
        for n in reversed(range(TERMS - 1)):
            total = total * square + coefs[n, p]
        mixing[p] = total


def near_planes(mine, vx, wy, near):
    full = vx.shape[1]
    low = through(stencil([plane(mine, r) for r in range(FACE)], (0, 1, 2)), vx[0], wy[0])
    upp = through(stencil([plane(mine, FACE + r) for r in range(FACE)], (2, 1, 0)), vx[1], wy[1])
    for r, value in enumerate(low + upp[::-1]):
        near[r * full : (r + 1) * full, :] = value


def force_planes(far, near, tx, uy, force):
    full = tx.shape[1]
    low = through(stencil([plane(far, r) for r in range(FACE)], (2, 1, 0)), tx[0], uy[0])
    upp = through(stencil([plane(far, FACE + r) for r in range(FACE)], (0, 1, 2)), tx[1], uy[1])
    for r, value in enumerate(low + upp[::-1]):
        force[r * full : (r + 1) * full, :] = value - plane(near, r)


def choose_kernel(group, *refs, width):
    held, out = refs[:width], refs[width:]
    rows = out[0].shape[0]
    half = rows // 2
    h, l = group[0] // width, lax.rem(group[0], width)
    for k in range(len(out)):
        dest = (lax.rem(h + k, len(out)) * width + l).astype(F32)
        for f in range(2):
            lo, hi = f * half, (f + 1) * half
            row = rows + (0 if f == 1 else HEAD // 2)
            chosen = held[0][lo:hi, :]
            for other in held[1:]:
                chosen = jnp.where(other[row : row + 1, :] == dest, other[lo:hi, :], chosen)
            out[k][lo:hi, :] = chosen


def pick_kernel(group, below, above, *refs, tall, width):
    got, out = refs[:-1], refs[-1]
    half = out.shape[0] // 2
    h = group[0] // width
    for f, nbr in enumerate((below, above)):
        lo = half if f == 0 else 0
        value = got[0][lo : lo + half, :]
        for k in range(1, tall):
            here = jnp.maximum(nbr[0], 0) // width == lax.rem(h + tall - k, tall)
            value = jnp.where(here, got[k][lo : lo + half, :], value)
        out[f * half : (f + 1) * half, :] = value


def middle_kernel(own, below, above, near, tx, uy, mixing, *rest, parts):
    far, ahead = rest[:parts], rest[parts : 2 * parts]
    packet, force, strip, spare = rest[2 * parts :]
    gather_kx(spare, far, own[0])
    force_planes(spare, near, tx, uy, force)
    gather_kx(strip, ahead, own[0])
    full = tx.shape[1]
    slab = full // parts
    for r in range(ROWS):
        total = plane(strip, r)
        for q in range(ROWS):
            total = total + mixing[PAIRS.index((min(r, q), max(r, q)))] * plane(force, q)
        strip[r * full : (r + 1) * full, :] = total
    at = pl.multiple_of(own[0] * slab, slab)
    for r in range(ROWS):
        packet[r * slab : (r + 1) * slab, :] = strip[pl.ds(r * full + at, slab), :]
    at = lax.broadcasted_iota(jnp.int32, (HEAD, packet.shape[1]), 0)
    names = jnp.where(at < HEAD // 2, above[0], below[0])
    packet[ROWS * slab :, :] = names.astype(F32)


def near_kernel(strip, vx, wy, near):
    near_planes(strip, vx, wy, near)


def lift(ext, own, force, rows, zstack, ystack, xown, store, field, turned, full, lead):
    zcap, width = rows.shape
    slab = turned.shape[0] // zcap
    square = plane_square((zcap, width), ext)
    weights = [jnp.broadcast_to(rows[:, r : r + 1], (zcap, width)) for r in range(ROWS)]

    def body(i, _):
        planes = []
        for half in range(2):
            kx = 2 * i + half
            local = square + x_square(kx, full)
            gain = gain_of(local)
            total = None
            for r in range(ROWS):
                term = weights[r] * force[pl.ds(r * full + kx, 1), :]
                total = term if total is None else total + term
            total = gain * total
            planes.append(lead(local, gain) * total if lead else total)
            store(kx, local, gain, total)
        wide = dot(zstack[...], tall_split(jnp.concatenate(planes, axis=1)))
        for half in range(2):
            at = pl.multiple_of((2 * i + half) * zcap, zcap)
            field[pl.ds(at, zcap), :] = wide[:, half * width : (half + 1) * width]
        return 0

    lax.fori_loop(0, full // 2, body, 0)
    across = xown[own]

    def spread(i, _):
        pair = [field[pl.ds(2 * i + half, full, stride=zcap), :] for half in range(2)]
        wide = dot(across, tall_split(jnp.concatenate(pair, axis=1)))
        for half in range(2):
            turned[pl.ds(2 * i + half, slab, stride=zcap), :] = wide[
                :, half * width : (half + 1) * width
            ]
        return 0

    lax.fori_loop(0, zcap // 2, spread, 0)


def between_kernel(
    extent, own, now, prev, force, rows, zstack, ystack, xown, free,
    current, onward, summed, field, turned, *, full,
):
    slab, zcap, width = now.shape
    keep = lax.broadcasted_iota(jnp.int32, (zcap, width), 0) < extent[0]

    def store(kx, local, gain, total):
        at = kx - own[0] * slab

        @pl.when((at >= 0) & (at < slab))
        def _():
            twice = 2.0 - local * gain
            first = jnp.where(keep, now[at], 0.0)
            value = twice * first - jnp.where(keep, prev[at], 0.0) + total
            current[at] = value
            onward[at] = twice * value - first

    lift(
        extent[0], own[0], force, rows, zstack, ystack, xown, store, field, turned, full,
        lambda local, gain: 2.0 - local * gain,
    )
    block = min(8, slab) * zcap

    def turn(i, _):
        at = pl.multiple_of(i * block, block)
        summed[pl.ds(at, block), :] = free[0, pl.ds(at, block), :] + along_y(
            turned[pl.ds(at, block), :], ystack[...]
        )
        return 0

    lax.fori_loop(0, slab * zcap // block, turn, 0)


def last_kernel(
    extent, own, near, tx, uy, onward, summed, rows, zstack, ystack, xown, *rest, full, parts
):
    far, given = rest[:parts], rest[parts : 2 * parts - 1]
    modes, pressure, spare, force, field, turned = rest[2 * parts - 1 :]
    slab, zcap, width = onward.shape
    gather_kx(spare, far, own[0])
    force_planes(spare, near, tx, uy, force)

    def store(kx, local, gain, total):
        at = kx - own[0] * slab

        @pl.when((at >= 0) & (at < slab))
        def _():
            modes[at] = onward[at] + total

    lift(
        extent[0], own[0], force, rows, zstack, ystack, xown, store, field, turned, full, None
    )
    block = min(8, slab) * zcap

    def turn(i, _):
        at = pl.multiple_of(i * block, block)
        value = summed[pl.ds(at, block), :]
        for piece in given:
            value = value + piece[pl.ds(at, block), :]
        pressure[pl.ds(at, block), :] = value + along_y(turned[pl.ds(at, block), :], ystack[...])
        return 0

    lax.fori_loop(0, slab * zcap // block, turn, 0)


def on_device(modes_now, modes_prev, z_extent, lower_nbr, upper_nbr, x_shift, y_shift):
    slab, zcap, width = modes_now.shape
    parts = lax.axis_size("split")
    count = lax.axis_size("dom")
    full = slab * parts
    own = lax.axis_index("split").astype(jnp.int32)[None]
    group = lax.axis_index("dom").astype(jnp.int32)[None]
    inner = inner_size(count)
    tall = count // inner
    size = ROWS * slab
    big = 4 * slab * zcap * width

    xtable, ytable = static_table(full), static_table(width)
    lanes = np.zeros((8, width), np.float32)
    for r in range(ROWS):
        lanes[0, r], lanes[1, r] = (r, 0) if r < FACE else (ROWS - 1 - r, 1)
    for p, (r, q) in enumerate(PAIRS):
        lanes[2, p], lanes[3, p] = lanes[0, r], lanes[1, r]
        lanes[4, p], lanes[5, p] = lanes[0, q], lanes[1, q]
    series = np.zeros((16, width), np.float32)
    for j in range(TERMS):
        for n in range(TERMS - j):
            series[j, n] = SERIES[n + j] * math.comb(n + j, n)
    yhigh, ylow = halves(ytable)
    ystack = np.block([[yhigh, ylow], [yhigh, np.zeros_like(yhigh)]])
    xhigh, xlow = halves(xtable.T)
    xown = np.stack(
        [
            np.concatenate([t[s * slab : (s + 1) * slab] for t in (xhigh, xlow, xhigh)], axis=1)
            for s in range(parts)
        ]
    )
    xparts = np.stack(
        [
            np.concatenate(
                [
                    np.concatenate(
                        [
                            t[(s + k) % parts * slab : ((s + k) % parts + 1) * slab,
                              s * slab : (s + 1) * slab]
                            for k in range(parts)
                        ],
                        axis=0,
                    )
                    for t in (xhigh, xlow, xhigh)
                ],
                axis=1,
            )
            for s in range(parts)
        ]
    )

    def tall_of(table):
        n = table.shape[0]
        return np.pad(table.T, ((n, n), (0, 0))).astype(np.float32)

    lanes, series, ystack, xown, xparts = map(jnp.asarray, (lanes, series, ystack, xown, xparts))
    xplain, xtall = jnp.asarray(xtable.astype(np.float32)), jnp.asarray(tall_of(xtable))
    yplain, ytall = jnp.asarray(ytable.astype(np.float32)), jnp.asarray(tall_of(ytable))

    def swap(piece):
        got = [piece]
        for k in range(1, parts):
            got.append(lax.ppermute(piece, "split", [(i, (i + k) % parts) for i in range(parts)]))
        return got

    def spread(packet):
        held = [packet]
        for k in range(1, inner):
            to = [(i, i // inner * inner + (i + k) % inner) for i in range(count)]
            held.append(lax.ppermute(packet, "dom", to))
        return call(
            functools.partial(choose_kernel, width=inner),
            [shape_of(size, width)] * tall,
            [SMEM] + [VMEM] * inner,
            moved=8 * size * width * 4,
            name="choose",
        )(group, *held)

    def deliver(chosen):
        got = [chosen[0]]
        for k in range(1, tall):
            to = [(i, (i + k * inner) % count) for i in range(count)]
            got.append(lax.ppermute(chosen[k], "dom", to))
        picked = call(
            functools.partial(pick_kernel, tall=tall, width=inner),
            [shape_of(size, width)],
            [SMEM] * 3 + [VMEM] * tall,
            moved=5 * size * width * 4,
            name="pick",
        )(group, lower_nbr, upper_nbr, *got)[0]
        return swap(picked)

    packet, rows = call(
        strip_kernel,
        [shape_of(size + HEAD, width), shape_of(zcap, width)],
        [SMEM] * 3 + [VMEM] * 2,
        moved=big,
        name="strip",
    )(z_extent, lower_nbr, upper_nbr, modes_now, lanes)
    chosen = spread(packet)
    mine = swap(packet[:size])

    ahead, free, zstack, coefs = call(
        functools.partial(ahead_kernel, full=full),
        [
            shape_of(size, width),
            shape_of(parts, slab * zcap, width),
            shape_of(zcap, 3 * zcap, dtype=BF16),
            shape_of(16, width),
        ],
        [SMEM] * 2 + [VMEM] * 7,
        scratch=[pltpu.VMEM((slab * zcap, width), F32)],
        flops=10**9,
        moved=4 * big,
        name="ahead",
    )(z_extent, own, modes_now, modes_prev, rows, lanes, series, xparts, ystack)
    aheads = swap(ahead)
    given = [
        lax.ppermute(free[k], "split", [(i, (i + k) % parts) for i in range(parts)])
        for k in range(1, parts)
    ]

    tx, uy, vx, wy, near1, mixing, _ = call(
        functools.partial(relation_kernel, parts=parts),
        [
            shape_of(2, full, full),
            shape_of(2, width, width),
            shape_of(2, full, full),
            shape_of(2, width, width),
            shape_of(ROWS * full, width),
            shape_of(len(PAIRS), full, width),
            shape_of(ROWS * full, width),
        ],
        [SMEM] * 6 + [ANY] + [VMEM] * (4 + parts),
        flops=10**8,
        moved=2 * big,
        name="relation",
    )(
        lower_nbr, upper_nbr, x_shift, y_shift, own, coefs, chosen[0],
        xplain, xtall, yplain, ytall, *mine,
    )

    packet2, force1, strip2 = call(
        functools.partial(middle_kernel, parts=parts),
        [
            shape_of(size + HEAD, width),
            shape_of(ROWS * full, width),
            shape_of(ROWS * full, width),
        ],
        [SMEM] * 3 + [VMEM] * (4 + 2 * parts),
        scratch=[pltpu.VMEM((ROWS * full, width), F32)],
        flops=10**8,
        moved=2 * big,
        name="middle",
    )(own, lower_nbr, upper_nbr, near1, tx, uy, mixing, *deliver(chosen), *aheads)

    chosen2 = spread(packet2)
    current, onward, summed = call(
        functools.partial(between_kernel, full=full),
        [
            shape_of(slab, zcap, width),
            shape_of(slab, zcap, width),
            shape_of(slab * zcap, width),
        ],
        [SMEM] * 2 + [VMEM] * 8,
        scratch=[
            pltpu.VMEM((full * zcap, width), F32),
            pltpu.VMEM((slab * zcap, width), F32),
        ],
        flops=10**9,
        moved=6 * big,
        name="between",
    )(z_extent, own, modes_now, modes_prev, force1, rows, zstack, ystack, xown, free)
    near2 = call(
        near_kernel,
        [shape_of(ROWS * full, width)],
        [VMEM] * 3,
        flops=10**7,
        moved=big,
        name="near",
    )(strip2, vx, wy)[0]

    modes, pressure = call(
        functools.partial(last_kernel, full=full, parts=parts),
        [shape_of(slab, zcap, width), shape_of(slab * zcap, width)],
        [SMEM] * 2 + [VMEM] * (9 + 2 * parts - 1),
        scratch=[
            pltpu.VMEM((ROWS * full, width), F32),
            pltpu.VMEM((ROWS * full, width), F32),
            pltpu.VMEM((full * zcap, width), F32),
            pltpu.VMEM((slab * zcap, width), F32),
        ],
        flops=10**9,
        moved=6 * big,
        name="last",
    )(
        z_extent, own, near2, tx, uy, onward, summed, rows, zstack, ystack, xown,
        *deliver(chosen2), *given,
    )
    return (modes, current, pressure.reshape(slab, zcap, width))


def solution(mesh):
    placed = (
        P("split", "dom", None),
        P("split", "dom", None),
        P("dom"),
        P("dom"),
        P("dom"),
        P("dom", None),
        P("dom", None),
    )
    return jax.shard_map(
        on_device,
        mesh=mesh,
        in_specs=placed,
        out_specs=(P("split", "dom", None), P("split", "dom", None), P("split", "dom", None)),
        check_vma=False,
    )
```

profile of v0, /device:TPU:0, one launch (start us, length us, event | category | flops | bytes accessed | tf_op | source)
XLA Modules:
  0.0 111.1 jit_solution(8564812169117581759)
XLA Ops:
  2.6 1.2 %copy-done = f32[32,64,128]{2,1,0:T(8,128)S(1)} copy-done((f32[32,64,128]{2,1,0:T(8,128)S(1)}, f32[32,64,128]{2,1,0:T(8,128)}, u32[]{:S(2)}) %copy-start) | copy-done | bytes 1048600
  5.5 1.2 %copy-done.2 = f32[32,64,128]{2,1,0:T(8,128)S(1)} copy-done((f32[32,64,128]{2,1,0:T(8,128)S(1)}, f32[32,64,128]{2,1,0:T(8,128)}, u32[]{:S(2)}) %copy-start.2) | copy-done | bytes 1048600
  9.7 11.6 %ahead.1 = (f32[192,128]{1,0:T(8,128)S(1)}, f32[2,2048,128]{2,1,0:T(8,128)S(1)}, bf16[64,192]{1,0:T(8,128)(2,1)S(1)}, f32[16,128]{1,0:T(8,128)S(1)}) custom-call(s32[1]{0:T(128)S(6)} %copy.19.extent, s32[1]{0:T(128)} %bitcast.own, f32[32,64,128]{2,1,0:T(8,128)S(1)} %copy-done, f32[32,64,128]{2,1,0:T(8,128)S(1)} %copy-done.2, ...), custom_call_target="tpu_custom_call" | custom-call | flops 1000000000 | bytes 4194304 | tf_op jit(solution)/shard_map/ahead/pallas_call | solution.py:571
  23.0 3.0 %collective-permute-start.16 = (f32[2048,128]{1,0:T(8,128)}, f32[2048,128]{1,0:T(8,128)S(1)}, u32[]{:S(2)}, u32[]{:S(2)}) collective-permute-start(f32[2048,128]{1,0:T(8,128)} %slice_bitcast_fusion), channel_id=1, source_target_pairs={{0,1},{1,0},{2,3},{3,2},{4,5},{5,4},{6,7},{7,6},{8,9},{9,8},{10,11... | collective-permute-start | bytes 3145736 | tf_op jit(solution)/shard_map/ppermute | solution.py:587
  26.0 1.5 %collective-permute-start.1 = (f32[200,128]{1,0:T(8,128)S(1)}, f32[200,128]{1,0:T(8,128)}, u32[]{:S(2)}, u32[]{:S(2)}) collective-permute-start(f32[200,128]{1,0:T(8,128)S(1)} %get-tuple-element.33.refs_0_), channel_id=1, source_target_pairs={{0,4},{2,6},{4,0},{6,2},{8,12},{10,14},{12,8},{14,10},{16,20},{18,... | collective-permute-start | bytes 307208 | tf_op jit(solution)/shard_map/ppermute | solution.py:538
  27.5 1.4 %collective-permute-start.2 = (f32[200,128]{1,0:T(8,128)S(1)}, f32[200,128]{1,0:T(8,128)}, u32[]{:S(2)}, u32[]{:S(2)}) collective-permute-start(f32[200,128]{1,0:T(8,128)S(1)} %get-tuple-element.33.refs_0_), channel_id=1, source_target_pairs={{0,6},{2,0},{4,2},{6,4},{8,14},{10,8},{12,10},{14,12},{16,22},{18,... | collective-permute-start | bytes 307208 | tf_op jit(solution)/shard_map/ppermute | solution.py:538
  29.0 1.8 %collective-permute-done.refs_1_ = f32[200,128]{1,0:T(8,128)} collective-permute-done((f32[200,128]{1,0:T(8,128)S(1)}, f32[200,128]{1,0:T(8,128)}, u32[]{:S(2)}, u32[]{:S(2)}) %collective-permute-start) | collective-permute-done | bytes 102432 | tf_op jit(solution)/shard_map/ppermute | solution.py:538
  33.5 1.6 %collective-permute-start.4 = (f32[192,128]{1,0:T(8,128)S(1)}, f32[192,128]{1,0:T(8,128)S(1)}, u32[]{:S(2)}, u32[]{:S(2)}) collective-permute-start(f32[192,128]{1,0:T(8,128)S(1)} %get-tuple-element.39), channel_id=1, source_target_pairs={{0,8},{2,10},{4,12},{6,14},{8,16},{10,18},{12,20},{14,22},{16,24},... | collective-permute-start | bytes 294920 | tf_op jit(solution)/shard_map/ppermute | solution.py:551
  35.1 2.6 %collective-permute-start.5 = (f32[192,128]{1,0:T(8,128)S(1)}, f32[192,128]{1,0:T(8,128)S(1)}, u32[]{:S(2)}, u32[]{:S(2)}) collective-permute-start(f32[192,128]{1,0:T(8,128)S(1)} %get-tuple-element.40), channel_id=1, source_target_pairs={{0,16},{2,18},{4,20},{6,22},{8,24},{10,26},{12,28},{14,30},{16,0},... | collective-permute-start | bytes 294920 | tf_op jit(solution)/shard_map/ppermute | solution.py:551
  37.7 1.3 %collective-permute-start.6 = (f32[192,128]{1,0:T(8,128)S(1)}, f32[192,128]{1,0:T(8,128)S(1)}, u32[]{:S(2)}, u32[]{:S(2)}) collective-permute-start(f32[192,128]{1,0:T(8,128)S(1)} %get-tuple-element.41), channel_id=1, source_target_pairs={{0,24},{2,26},{4,28},{6,30},{8,0},{10,2},{12,4},{14,6},{16,8},{18,... | collective-permute-start | bytes 294920 | tf_op jit(solution)/shard_map/ppermute | solution.py:551
  39.7 1.2 %collective-permute-done.4.refs_1_ = f32[192,128]{1,0:T(8,128)S(1)} collective-permute-done((f32[192,128]{1,0:T(8,128)S(1)}, f32[192,128]{1,0:T(8,128)S(1)}, u32[]{:S(2)}, u32[]{:S(2)}) %collective-permute-start.4) | collective-permute-done | bytes 98336 | tf_op jit(solution)/shard_map/ppermute | solution.py:551
  41.4 3.8 %collective-permute-done.5.refs_2_ = f32[192,128]{1,0:T(8,128)S(1)} collective-permute-done((f32[192,128]{1,0:T(8,128)S(1)}, f32[192,128]{1,0:T(8,128)S(1)}, u32[]{:S(2)}, u32[]{:S(2)}) %collective-permute-start.5) | collective-permute-done | bytes 98336 | tf_op jit(solution)/shard_map/ppermute | solution.py:551
  45.8 6.5 %collective-permute-done.3.rest_1_ = f32[192,128]{1,0:T(8,128)S(1)} collective-permute-done((f32[192,128]{1,0:T(8,128)S(1)}, f32[192,128]{1,0:T(8,128)S(1)}, u32[]{:S(2)}, u32[]{:S(2)}) %collective-permute-start.3) | collective-permute-done | bytes 98336 | tf_op jit(solution)/shard_map/ppermute | solution.py:531
  54.7 2.3 %relation.1 = (f32[2,64,64]{2,1,0:T(8,128)S(1)}, f32[2,128,128]{2,1,0:T(8,128)S(1)}, f32[2,64,64]{2,1,0:T(8,128)S(1)}, f32[2,128,128]{2,1,0:T(8,128)S(1)}, f32[3...) custom-call(s32[1]{0:T(128)S(6)} %copy.20.below, s32[1]{0:T(128)S(6)} %copy.21.above, ...), custom_call_target="tpu_custom_call" | custom-call | flops 100000000 | bytes 2097152 | tf_op jit(solution)/shard_map/relation/pallas_call | solution.py:591
  58.7 2.1 %collective-permute-start.10 = (f32[200,128]{1,0:T(8,128)S(1)}, f32[200,128]{1,0:T(8,128)S(1)}, u32[]{:S(2)}, u32[]{:S(2)}) collective-permute-start(f32[200,128]{1,0:T(8,128)S(1)} %get-tuple-element.51.refs_0_), channel_id=1, source_target_pairs={{0,4},{2,6},{4,0},{6,2},{8,12},{10,14},{12,8},{14,10},{16,20},{18,... | collective-permute-start | bytes 307208 | tf_op jit(solution)/shard_map/ppermute | solution.py:538
  61.3 2.6 %collective-permute-done.10.refs_2_ = f32[200,128]{1,0:T(8,128)S(1)} collective-permute-done((f32[200,128]{1,0:T(8,128)S(1)}, f32[200,128]{1,0:T(8,128)S(1)}, u32[]{:S(2)}, u32[]{:S(2)}) %collective-permute-start.10) | collective-permute-done | bytes 102432 | tf_op jit(solution)/shard_map/ppermute | solution.py:538
  65.7 2.0 %collective-permute-start.12 = (f32[192,128]{1,0:T(8,128)S(1)}, f32[192,128]{1,0:T(8,128)S(1)}, u32[]{:S(2)}, u32[]{:S(2)}) collective-permute-start(f32[192,128]{1,0:T(8,128)S(1)} %get-tuple-element.53), channel_id=1, source_target_pairs={{0,8},{2,10},{4,12},{6,14},{8,16},{10,18},{12,20},{14,22},{16,24},... | collective-permute-start | bytes 294920 | tf_op jit(solution)/shard_map/ppermute | solution.py:551
  67.7 2.6 %collective-permute-start.13 = (f32[192,128]{1,0:T(8,128)S(1)}, f32[192,128]{1,0:T(8,128)S(1)}, u32[]{:S(2)}, u32[]{:S(2)}) collective-permute-start(f32[192,128]{1,0:T(8,128)S(1)} %get-tuple-element.54), channel_id=1, source_target_pairs={{0,16},{2,18},{4,20},{6,22},{8,24},{10,26},{12,28},{14,30},{16,0},... | collective-permute-start | bytes 294920 | tf_op jit(solution)/shard_map/ppermute | solution.py:551
  70.2 1.4 %collective-permute-start.14 = (f32[192,128]{1,0:T(8,128)S(1)}, f32[192,128]{1,0:T(8,128)S(1)}, u32[]{:S(2)}, u32[]{:S(2)}) collective-permute-start(f32[192,128]{1,0:T(8,128)S(1)} %get-tuple-element.55), channel_id=1, source_target_pairs={{0,24},{2,26},{4,28},{6,30},{8,0},{10,2},{12,4},{14,6},{16,8},{18,... | collective-permute-start | bytes 294920 | tf_op jit(solution)/shard_map/ppermute | solution.py:551
  71.6 1.8 %collective-permute-done.12.refs_1_ = f32[192,128]{1,0:T(8,128)S(1)} collective-permute-done((f32[192,128]{1,0:T(8,128)S(1)}, f32[192,128]{1,0:T(8,128)S(1)}, u32[]{:S(2)}, u32[]{:S(2)}) %collective-permute-start.12) | collective-permute-done | bytes 98336 | tf_op jit(solution)/shard_map/ppermute | solution.py:551
  73.4 3.7 %collective-permute-done.13.refs_2_ = f32[192,128]{1,0:T(8,128)S(1)} collective-permute-done((f32[192,128]{1,0:T(8,128)S(1)}, f32[192,128]{1,0:T(8,128)S(1)}, u32[]{:S(2)}, u32[]{:S(2)}) %collective-permute-start.13) | collective-permute-done | bytes 98336 | tf_op jit(solution)/shard_map/ppermute | solution.py:551
  77.1 1.6 %collective-permute-start.15 = (f32[192,128]{1,0:T(8,128)S(1)}, f32[192,128]{1,0:T(8,128)S(1)}, u32[]{:S(2)}, u32[]{:S(2)}) collective-permute-start(f32[192,128]{1,0:T(8,128)S(1)} %pick.3.rest_0_), channel_id=1, source_target_pairs={{0,1},{1,0},{2,3},{3,2},{4,5},{5,4},{6,7},{7,6},{8,9},{9,8},{10,11... | collective-permute-start | bytes 294920 | tf_op jit(solution)/shard_map/ppermute | solution.py:531
  79.4 15.7 %between.1 = (f32[32,64,128]{2,1,0:T(8,128)}, f32[32,64,128]{2,1,0:T(8,128)S(1)}, f32[2048,128]{1,0:T(8,128)S(1)}) custom-call(s32[1]{0:T(128)S(6)} %copy.19.extent, s32[1]{0:T(128)} %bitcast.own, f32[32,64,128]{2,1,0:T(8,128)S(1)} %copy-done.1, f32[32,64,128]{2,1,0:T(8,128)S(1)} %copy-done.3, f32[384,128]{1,0:T(8,128)S(1)} %get-tuple-element.46.force, ...), custom_call_target="tpu_custom_call" | custom-call | flops 1000000000 | bytes 6291456 | tf_op jit(solution)/shard_map/between/pallas_call | solution.py:626
  95.1 16.0 %last.1 = (f32[32,64,128]{2,1,0:T(8,128)}, f32[2048,128]{1,0:T(8,128)}) custom-call(s32[1]{0:T(128)S(6)} %copy.19.extent, s32[1]{0:T(128)} %bitcast.own, f32[384,128]{1,0:T(8,128)S(1)} %near.1, f32[2,64,64]{2,1,0:T(8,128)S(1)} %get-tuple-element.36.tx, f32[2,128,128]{2,1,0:T(8,128)S(1)} %get-tuple-element.37.uy, ...), custom_call_target="tpu_custom_call" | custom-call | flops 1000000000 | bytes 6291456 | tf_op jit(solution)/shard_map/last/pallas_call | solution.py:651
  (61 shorter events, 17.9 us)
Async XLA Ops:
  22.0 30.3 %copy-start.6 = (f32[384,128]{1,0:T(8,128)S(1)}, f32[384,128]{1,0:T(8,128)}, u32[]{:S(2)}) copy-start(f32[384,128]{1,0:T(8,128)} %constant.34.clone.ytall) | copy-start | bytes 589828
  22.0 30.3 %copy-start.12 = (f32[64,64]{1,0:T(8,128)S(1)}, f32[64,64]{1,0:T(8,128)}, u32[]{:S(2)}) copy-start(f32[64,64]{1,0:T(8,128)} %constant.31.clone.xplain) | copy-start | bytes 49156
  22.0 30.3 %copy-start.15 = (s32[1,2]{1,0:T(1,128)S(1)}, s32[1,2]{1,0:T(1,128)}, u32[]{:S(2)}) copy-start(s32[1,2]{1,0:T(1,128)} %x_shift.1) | copy-start | bytes 28
  23.0 72.1 %collective-permute-start.16 = (f32[2048,128]{1,0:T(8,128)}, f32[2048,128]{1,0:T(8,128)S(1)}, u32[]{:S(2)}, u32[]{:S(2)}) collective-permute-start(f32[2048,128]{1,0:T(8,128)} %slice_bitcast_fusion), channel_id=1, source_target_pairs={{0,1},{1,0},{2,3},{3,2},{4,5},{5,4},{6,7},{7,6},{8,9},{9,8},{10,11... | collective-permute-start | bytes 3145736 | tf_op jit(solution)/shard_map/ppermute | solution.py:587
  26.0 4.7 %collective-permute-start = (f32[200,128]{1,0:T(8,128)S(1)}, f32[200,128]{1,0:T(8,128)}, u32[]{:S(2)}, u32[]{:S(2)}) collective-permute-start(f32[200,128]{1,0:T(8,128)S(1)} %get-tuple-element.33.refs_0_), channel_id=1, source_target_pairs={{0,2},{2,4},{4,6},{6,0},{8,10},{10,12},{12,14},{14,8},{16,18},{18,... | collective-permute-start | bytes 307208 | tf_op jit(solution)/shard_map/ppermute | solution.py:538
  26.0 5.8 %collective-permute-start.1 = (f32[200,128]{1,0:T(8,128)S(1)}, f32[200,128]{1,0:T(8,128)}, u32[]{:S(2)}, u32[]{:S(2)}) collective-permute-start(f32[200,128]{1,0:T(8,128)S(1)} %get-tuple-element.33.refs_0_), channel_id=1, source_target_pairs={{0,4},{2,6},{4,0},{6,2},{8,12},{10,14},{12,8},{14,10},{16,20},{18,... | collective-permute-start | bytes 307208 | tf_op jit(solution)/shard_map/ppermute | solution.py:538
  27.5 4.9 %collective-permute-start.2 = (f32[200,128]{1,0:T(8,128)S(1)}, f32[200,128]{1,0:T(8,128)}, u32[]{:S(2)}, u32[]{:S(2)}) collective-permute-start(f32[200,128]{1,0:T(8,128)S(1)} %get-tuple-element.33.refs_0_), channel_id=1, source_target_pairs={{0,6},{2,0},{4,2},{6,4},{8,14},{10,8},{12,10},{14,12},{16,22},{18,... | collective-permute-start | bytes 307208 | tf_op jit(solution)/shard_map/ppermute | solution.py:538
  33.5 7.4 %collective-permute-start.4 = (f32[192,128]{1,0:T(8,128)S(1)}, f32[192,128]{1,0:T(8,128)S(1)}, u32[]{:S(2)}, u32[]{:S(2)}) collective-permute-start(f32[192,128]{1,0:T(8,128)S(1)} %get-tuple-element.39), channel_id=1, source_target_pairs={{0,8},{2,10},{4,12},{6,14},{8,16},{10,18},{12,20},{14,22},{16,24},... | collective-permute-start | bytes 294920 | tf_op jit(solution)/shard_map/ppermute | solution.py:551
  35.1 10.1 %collective-permute-start.5 = (f32[192,128]{1,0:T(8,128)S(1)}, f32[192,128]{1,0:T(8,128)S(1)}, u32[]{:S(2)}, u32[]{:S(2)}) collective-permute-start(f32[192,128]{1,0:T(8,128)S(1)} %get-tuple-element.40), channel_id=1, source_target_pairs={{0,16},{2,18},{4,20},{6,22},{8,24},{10,26},{12,28},{14,30},{16,0},... | collective-permute-start | bytes 294920 | tf_op jit(solution)/shard_map/ppermute | solution.py:551
  37.7 7.5 %collective-permute-start.6 = (f32[192,128]{1,0:T(8,128)S(1)}, f32[192,128]{1,0:T(8,128)S(1)}, u32[]{:S(2)}, u32[]{:S(2)}) collective-permute-start(f32[192,128]{1,0:T(8,128)S(1)} %get-tuple-element.41), channel_id=1, source_target_pairs={{0,24},{2,26},{4,28},{6,30},{8,0},{10,2},{12,4},{14,6},{16,8},{18,... | collective-permute-start | bytes 294920 | tf_op jit(solution)/shard_map/ppermute | solution.py:551
  39.1 40.4 %copy-start.1 = (f32[32,64,128]{2,1,0:T(8,128)S(1)}, f32[32,64,128]{2,1,0:T(8,128)}, u32[]{:S(2)}) copy-start(f32[32,64,128]{2,1,0:T(8,128)} %now.5) | copy-start | bytes 3145732
  39.1 40.4 %copy-start.3 = (f32[32,64,128]{2,1,0:T(8,128)S(1)}, f32[32,64,128]{2,1,0:T(8,128)}, u32[]{:S(2)}) copy-start(f32[32,64,128]{2,1,0:T(8,128)} %prev.3) | copy-start | bytes 3145732
  39.1 40.4 %copy-start.5 = (bf16[256,256]{1,0:T(8,128)(2,1)S(1)}, bf16[256,256]{1,0:T(8,128)(2,1)}, u32[]{:S(2)}) copy-start(bf16[256,256]{1,0:T(8,128)(2,1)} %constant.28.clone.ystack) | copy-start | bytes 393220
  39.1 40.4 %copy-start.7 = (bf16[2,32,192]{2,1,0:T(8,128)(2,1)S(1)}, bf16[2,32,192]{2,1,0:T(8,128)(2,1)}, u32[]{:S(2)}) copy-start(bf16[2,32,192]{2,1,0:T(8,128)(2,1)} %constant.29.clone.xown) | copy-start | bytes 73732
  39.1 13.2 %collective-permute-start.3 = (f32[192,128]{1,0:T(8,128)S(1)}, f32[192,128]{1,0:T(8,128)S(1)}, u32[]{:S(2)}, u32[]{:S(2)}) collective-permute-start(f32[192,128]{1,0:T(8,128)S(1)} %slice.6.rest_0_), channel_id=1, source_target_pairs={{0,1},{1,0},{2,3},{3,2},{4,5},{5,4},{6,7},{7,6},{8,9},{9,8},{10,11... | collective-permute-start | bytes 294920 | tf_op jit(solution)/shard_map/ppermute | solution.py:531
  40.9 16.1 %collective-permute-start.8 = (f32[192,128]{1,0:T(8,128)}, f32[192,128]{1,0:T(8,128)S(1)}, u32[]{:S(2)}, u32[]{:S(2)}) collective-permute-start(f32[192,128]{1,0:T(8,128)} %copy-done.8), channel_id=1, source_target_pairs={{0,1},{1,0},{2,3},{3,2},{4,5},{5,4},{6,7},{7,6},{8,9},{9,8},{10,11... | collective-permute-start | bytes 294920 | tf_op jit(solution)/shard_map/ppermute | solution.py:531
  45.3 11.8 %collective-permute-start.7 = (f32[192,128]{1,0:T(8,128)S(1)}, f32[192,128]{1,0:T(8,128)S(1)}, u32[]{:S(2)}, u32[]{:S(2)}) collective-permute-start(f32[192,128]{1,0:T(8,128)S(1)} %pick.2.rest_0_), channel_id=1, source_target_pairs={{0,1},{1,0},{2,3},{3,2},{4,5},{5,4},{6,7},{7,6},{8,9},{9,8},{10,11... | collective-permute-start | bytes 294920 | tf_op jit(solution)/shard_map/ppermute | solution.py:531
  58.7 5.2 %collective-permute-start.10 = (f32[200,128]{1,0:T(8,128)S(1)}, f32[200,128]{1,0:T(8,128)S(1)}, u32[]{:S(2)}, u32[]{:S(2)}) collective-permute-start(f32[200,128]{1,0:T(8,128)S(1)} %get-tuple-element.51.refs_0_), channel_id=1, source_target_pairs={{0,4},{2,6},{4,0},{6,2},{8,12},{10,14},{12,8},{14,10},{16,20},{18,... | collective-permute-start | bytes 307208 | tf_op jit(solution)/shard_map/ppermute | solution.py:538
  60.8 4.2 %collective-permute-start.11 = (f32[200,128]{1,0:T(8,128)S(1)}, f32[200,128]{1,0:T(8,128)S(1)}, u32[]{:S(2)}, u32[]{:S(2)}) collective-permute-start(f32[200,128]{1,0:T(8,128)S(1)} %get-tuple-element.51.refs_0_), channel_id=1, source_target_pairs={{0,6},{2,0},{4,2},{6,4},{8,14},{10,8},{12,10},{14,12},{16,22},{18,... | collective-permute-start | bytes 307208 | tf_op jit(solution)/shard_map/ppermute | solution.py:538
  60.8 4.8 %collective-permute-start.9 = (f32[200,128]{1,0:T(8,128)S(1)}, f32[200,128]{1,0:T(8,128)S(1)}, u32[]{:S(2)}, u32[]{:S(2)}) collective-permute-start(f32[200,128]{1,0:T(8,128)S(1)} %get-tuple-element.51.refs_0_), channel_id=1, source_target_pairs={{0,2},{2,4},{4,6},{6,0},{8,10},{10,12},{12,14},{14,8},{16,18},{18,... | collective-permute-start | bytes 307208 | tf_op jit(solution)/shard_map/ppermute | solution.py:538
  65.7 7.7 %collective-permute-start.12 = (f32[192,128]{1,0:T(8,128)S(1)}, f32[192,128]{1,0:T(8,128)S(1)}, u32[]{:S(2)}, u32[]{:S(2)}) collective-permute-start(f32[192,128]{1,0:T(8,128)S(1)} %get-tuple-element.53), channel_id=1, source_target_pairs={{0,8},{2,10},{4,12},{6,14},{8,16},{10,18},{12,20},{14,22},{16,24},... | collective-permute-start | bytes 294920 | tf_op jit(solution)/shard_map/ppermute | solution.py:551
  67.7 9.4 %collective-permute-start.13 = (f32[192,128]{1,0:T(8,128)S(1)}, f32[192,128]{1,0:T(8,128)S(1)}, u32[]{:S(2)}, u32[]{:S(2)}) collective-permute-start(f32[192,128]{1,0:T(8,128)S(1)} %get-tuple-element.54), channel_id=1, source_target_pairs={{0,16},{2,18},{4,20},{6,22},{8,24},{10,26},{12,28},{14,30},{16,0},... | collective-permute-start | bytes 294920 | tf_op jit(solution)/shard_map/ppermute | solution.py:551
  70.2 6.8 %collective-permute-start.14 = (f32[192,128]{1,0:T(8,128)S(1)}, f32[192,128]{1,0:T(8,128)S(1)}, u32[]{:S(2)}, u32[]{:S(2)}) collective-permute-start(f32[192,128]{1,0:T(8,128)S(1)} %get-tuple-element.55), channel_id=1, source_target_pairs={{0,24},{2,26},{4,28},{6,30},{8,0},{10,2},{12,4},{14,6},{16,8},{18,... | collective-permute-start | bytes 294920 | tf_op jit(solution)/shard_map/ppermute | solution.py:551
  77.1 18.0 %collective-permute-start.15 = (f32[192,128]{1,0:T(8,128)S(1)}, f32[192,128]{1,0:T(8,128)S(1)}, u32[]{:S(2)}, u32[]{:S(2)}) collective-permute-start(f32[192,128]{1,0:T(8,128)S(1)} %pick.3.rest_0_), channel_id=1, source_target_pairs={{0,1},{1,0},{2,3},{3,2},{4,5},{5,4},{6,7},{7,6},{8,9},{9,8},{10,11... | collective-permute-start | bytes 294920 | tf_op jit(solution)/shard_map/ppermute | solution.py:531
  (12 other events, 10.1 us)
where the time goes:
time: 112 us; the launch traced here: 111 us
  Pallas kernels  49.1 us (44%)
  waiting for transfers between devices  24.8 us (22%)
  starting transfers between devices  23.3 us (21%)
  local copies, waits for them, and re-layouts  11.2 us (10%)
  between operations  2.76 us (2%)
    pallas_call x1, Pallas kernels, on_device(): call(functools.partial(last_kernel, full=full, parts=parts), [shape_of(sl...  16 us
    pallas_call x1, Pallas kernels, on_device(): call(functools.partial(between_kernel, full=full), [shape_of(slab, zcap,...  15.7 us
    pallas_call x1, Pallas kernels, on_device(): call(functools.partial(ahead_kernel, full=full), [shape_of(size, width),...  11.6 us
    ppermute x6, starting transfers between devices, deliver(): got.append(lax.ppermute(chosen[k], 'dom', to))  11.5 us
    ppermute x6, waiting for transfers between devices, deliver(): got.append(lax.ppermute(chosen[k], 'dom', to))  10.5 us
    unnamed x38, local copies, waits for them, and re-layouts  10.1 us
    ppermute x6, waiting for transfers between devices, spread(): held.append(lax.ppermute(packet, 'dom', to))  7.75 us
    ppermute x4, waiting for transfers between devices, swap(): lax.ppermute(piece, 'split', [(i, (i + k) % parts) for i in range(parts)])  6.5 us
  transfers between devices with their start and end apart: 17, of which 11 were waited for; matrix products, arithmetic and copies ran while one was open for 0% of the time, Pallas kernels for 19%

commit v1 on v0

--- a/solution.py
+++ b/solution.py
@@ -17,14 +17,14 @@
 FACE = 3
 ROWS = 2 * FACE
 HEAD = 8
-TERMS = 9
-SERIES = [(-1) ** n * 2.0 / math.factorial(2 * n + 2) for n in range(TERMS)]
+SERIES = [(-1) ** n * 2.0 / math.factorial(2 * n + 2) for n in range(10)]
+TERMS = 7
 BASE = (COURANT * math.pi) ** 2
 PAIRS = [(r, q) for r in range(ROWS) for q in range(r, ROWS)]
 VMEM = pl.BlockSpec(memory_space=pltpu.VMEM)
 SMEM = pl.BlockSpec(memory_space=pltpu.SMEM)
 ANY = pl.BlockSpec(memory_space=pl.ANY)
-LIMIT = 40 * 1024 * 1024
+LIMIT = 12 * 1024 * 1024
 
 
 def static_table(count):
@@ -171,9 +171,9 @@
     return jax.ShapeDtypeStruct(dims, dtype)
 
 
-def strip_kernel(extent, below, above, now, lanes, packet, rows):
+def strip_kernel(extent, below, above, now, consts, packet, rows):
     slab, zcap, width = now.shape
-    table = face_rows(lanes[0:1, :], lanes[1:2, :], (zcap, width), extent[0])
+    table = face_rows(consts[0:1, :], consts[1:2, :], (zcap, width), extent[0])
     rows[...] = table
     for r in range(ROWS):
         weight = jnp.broadcast_to(table[:, r : r + 1], (zcap, width))
@@ -183,9 +183,24 @@
     packet[ROWS * slab :, :] = names.astype(F32)
 
 
+def lane_series(consts, first, shape, extent):
+    kz = lax.broadcasted_iota(jnp.int32, shape, 0)
+    frac = kz.astype(F32) / jnp.full(shape, extent.astype(F32))
+    middle = jnp.where(kz < extent, BASE * frac * frac, 0.0) + BASE
+    total = jnp.zeros(shape, F32)
+    for j in reversed(range(len(SERIES))):
+        total = total * middle + consts[first + j : first + j + 1, :]
+    return total
+
+
+def stack_lanes(table, depth):
+    table = table[:, :depth]
+    high = table.astype(BF16).astype(F32)
+    return jnp.concatenate([high, table - high, high], axis=1).astype(BF16)
+
+
 def ahead_kernel(
-    extent, own, now, prev, rows, lanes, series, xparts, ystack,
-    strip, free, zstack, coefs, field, *, full,
+    extent, own, now, prev, rows, consts, strip, zstack, estack, hstack, coefs, *, full
 ):
     slab, zcap, width = now.shape
     ext = extent[0]
@@ -194,86 +209,58 @@
     lenf = jnp.full((zcap, zcap), ext.astype(F32))
     ztable = scale_of(kk, lenf) * cosine_of(kk.astype(F32), 2.0 * zz.astype(F32) + 1.0, lenf)
     ztable = jnp.where((kk < ext) & (zz < ext), ztable, 0.0)
-    high = ztable.astype(BF16).astype(F32)
-    stacked = jnp.concatenate([high, ztable - high, high], axis=1).astype(BF16)
-    zstack[...] = stacked
-
-    kz = lax.broadcasted_iota(jnp.int32, (zcap, width), 0)
-    bz = kz.astype(F32) / jnp.full((zcap, width), ext.astype(F32))
-    bz = jnp.where(kz < ext, BASE * bz * bz, 0.0)
-    total = jnp.zeros((zcap, width), F32)
-    for j in reversed(range(TERMS)):
-        total = total * bz + series[j : j + 1, :]
-    pairs = face_rows(lanes[2:3, :], lanes[3:4, :], (zcap, width), ext)
-    pairs = pairs * face_rows(lanes[4:5, :], lanes[5:6, :], (zcap, width), ext)
-    coefs[...] = exact_dot(total.T[: coefs.shape[0]], pairs)
-
-    keep = lax.broadcasted_iota(jnp.int32, (zcap, width), 0) < ext
-    square = plane_square((zcap, width), ext)
-    weights = [jnp.broadcast_to(rows[:, r : r + 1], (zcap, width)) for r in range(ROWS)]
+    zstack[...] = stack_lanes(ztable, zcap)
+
+    shape = (zcap, width)
+    pairs = face_rows(consts[2:3, :], consts[3:4, :], shape, ext)
+    pairs = pairs * face_rows(consts[4:5, :], consts[5:6, :], shape, ext)
+    coefs[...] = exact_dot(lane_series(consts, 8, shape, ext).T[: coefs.shape[0]], pairs)
+    terms = face_rows(consts[6:7, :], consts[7:8, :], shape, ext)
+    terms = terms * lane_series(consts, 24, shape, ext)
+    depth = estack.shape[1] // 3
+    estack[...] = stack_lanes(terms, depth)
+    hstack[...] = stack_lanes(exact_dot(ztable, terms), depth)
+
+    keep = lax.broadcasted_iota(jnp.int32, shape, 0) < ext
+    square = plane_square(shape, ext)
+    weights = [jnp.broadcast_to(rows[:, r : r + 1], shape) for r in range(ROWS)]
+    group = min(4, slab)
 
     def body(i, _):
-        frees = []
-        for half in range(2):
-            kx = 2 * i + half
+        for half in range(group):
+            kx = group * i + half
             local = square + x_square(own[0] * slab + kx, full)
             twice = 2.0 - local * gain_of(local)
-            first = jnp.where(keep, now[kx], 0.0)
-            ahead = twice * first - jnp.where(keep, prev[kx], 0.0)
+            ahead = twice * now[kx] - prev[kx]
+            ahead = jnp.where(keep, ahead, 0.0)
             for r in range(ROWS):
                 strip[pl.ds(r * slab + kx, 1), :] = jnp.sum(
                     ahead * weights[r], axis=0, keepdims=True
                 )
-            frees.append(twice * ahead - first)
-        wide = dot(stacked, tall_split(jnp.concatenate(frees, axis=1)))
-        for half in range(2):
-            at = pl.multiple_of((2 * i + half) * zcap, zcap)
-            field[pl.ds(at, zcap), :] = wide[:, half * width : (half + 1) * width]
         return 0
 
-    lax.fori_loop(0, slab // 2, body, 0)
-    block = min(8, slab) * zcap
-
-    def turn(i, _):
-        at = pl.multiple_of(i * block, block)
-        field[pl.ds(at, block), :] = along_y(field[pl.ds(at, block), :], ystack[...])
-        return 0
-
-    lax.fori_loop(0, slab * zcap // block, turn, 0)
-    parts = full // slab
-    across = xparts[own[0]]
-
-    def spread(i, _):
-        pair = [field[pl.ds(2 * i + half, slab, stride=zcap), :] for half in range(2)]
-        wide = dot(across, tall_split(jnp.concatenate(pair, axis=1)))
-        for k in range(parts):
-            for half in range(2):
-                free[k, pl.ds(2 * i + half, slab, stride=zcap), :] = wide[
-                    k * slab : (k + 1) * slab, half * width : (half + 1) * width
-                ]
-        return 0
-
-    lax.fori_loop(0, zcap // 2, spread, 0)
+    lax.fori_loop(0, slab // group, body, 0)
 
 
 def relation_kernel(
-    below, above, x_shift, y_shift, own, coefs, after, xplain, xtall, yplain, ytall, *rest, parts
+    below, above, x_shift, y_shift, own, coefs, after, xtall, ytall, *rest, parts
 ):
     strips, (tx, uy, vx, wy, near, mixing, mine) = rest[:parts], rest[parts:]
-    full, width = xplain.shape[0], yplain.shape[0]
+    full, width = xtall.shape[1], ytall.shape[1]
     for f, (nbr, dx, dy) in enumerate(
         ((below, x_shift[0, 0], y_shift[0, 0]), (above, x_shift[0, 1], y_shift[0, 1]))
     ):
         has = jnp.where(nbr[0] >= 0, COURANT**2, 0.0).astype(F32)
-        for count, move, plain, tall, take, keep, scale in (
-            (full, dx, xplain, xtall, tx, vx, has),
-            (width, dy, yplain, ytall, uy, wy, None),
+        for count, move, tall, take, keep, scale in (
+            (full, dx, xtall, tx, vx, has),
+            (width, dy, ytall, uy, wy, None),
         ):
             move = jnp.clip(move, -count, count)
             slid = tall[pl.ds(count + move, count), :]
             at = lax.broadcasted_iota(jnp.int32, (count, count), 0) + move
             kept = jnp.where((at >= 0) & (at < count), tall[count : 2 * count, :], 0.0)
-            taken, stay = exact_dot(plain[...], slid), exact_dot(plain[...], kept)
+            plain = tall[3 * count :, :]
+            taken, stay = exact_dot(plain, slid), exact_dot(plain, kept)
             take[f] = taken if scale is None else taken * scale
             keep[f] = stay if scale is None else stay * scale
     gather_kx(mine, strips, own[0])
@@ -281,7 +268,7 @@
     shape = (full, width)
     ax = lax.broadcasted_iota(jnp.int32, shape, 0).astype(F32) / full
     ay = lax.broadcasted_iota(jnp.int32, shape, 1).astype(F32) / width
-    square = BASE * (ax * ax + ay * ay)
+    square = BASE * (ax * ax + ay * ay) - BASE
     for p in range(len(PAIRS)):
         total = jnp.full(shape, coefs[TERMS - 1, p])
         for n in reversed(range(TERMS - 1)):
@@ -359,110 +346,105 @@
     near_planes(strip, vx, wy, near)
 
 
-def lift(ext, own, force, rows, zstack, ystack, xown, store, field, turned, full, lead):
-    zcap, width = rows.shape
-    slab = turned.shape[0] // zcap
-    square = plane_square((zcap, width), ext)
-    weights = [jnp.broadcast_to(rows[:, r : r + 1], (zcap, width)) for r in range(ROWS)]
+def between_kernel(
+    extent, own, now, prev, force, rows, zstack, ystack, xparts, current, onward, *rest, full,
+):
+    free, field = rest[:-1], rest[-1]
+    slab, zcap, width = now.shape
+    shape = (zcap, width)
+    keep = lax.broadcasted_iota(jnp.int32, shape, 0) < extent[0]
+    square = plane_square(shape, extent[0])
+    weights = [jnp.broadcast_to(rows[:, r : r + 1], shape) for r in range(ROWS)]
+    group = min(4, slab)
 
     def body(i, _):
         planes = []
-        for half in range(2):
-            kx = 2 * i + half
+        for half in range(group):
+            at = group * i + half
+            kx = own[0] * slab + at
             local = square + x_square(kx, full)
             gain = gain_of(local)
             total = None
             for r in range(ROWS):
                 term = weights[r] * force[pl.ds(r * full + kx, 1), :]
                 total = term if total is None else total + term
-            total = gain * total
-            planes.append(lead(local, gain) * total if lead else total)
-            store(kx, local, gain, total)
-        wide = dot(zstack[...], tall_split(jnp.concatenate(planes, axis=1)))
-        for half in range(2):
-            at = pl.multiple_of((2 * i + half) * zcap, zcap)
-            field[pl.ds(at, zcap), :] = wide[:, half * width : (half + 1) * width]
-        return 0
-
-    lax.fori_loop(0, full // 2, body, 0)
-    across = xown[own]
-
-    def spread(i, _):
-        pair = [field[pl.ds(2 * i + half, full, stride=zcap), :] for half in range(2)]
-        wide = dot(across, tall_split(jnp.concatenate(pair, axis=1)))
-        for half in range(2):
-            turned[pl.ds(2 * i + half, slab, stride=zcap), :] = wide[
-                :, half * width : (half + 1) * width
-            ]
-        return 0
-
-    lax.fori_loop(0, zcap // 2, spread, 0)
-
-
-def between_kernel(
-    extent, own, now, prev, force, rows, zstack, ystack, xown, free,
-    current, onward, summed, field, turned, *, full,
-):
-    slab, zcap, width = now.shape
-    keep = lax.broadcasted_iota(jnp.int32, (zcap, width), 0) < extent[0]
-
-    def store(kx, local, gain, total):
-        at = kx - own[0] * slab
-
-        @pl.when((at >= 0) & (at < slab))
-        def _():
             twice = 2.0 - local * gain
             first = jnp.where(keep, now[at], 0.0)
-            value = twice * first - jnp.where(keep, prev[at], 0.0) + total
+            value = twice * first - jnp.where(keep, prev[at], 0.0) + gain * total
             current[at] = value
-            onward[at] = twice * value - first
-
-    lift(
-        extent[0], own[0], force, rows, zstack, ystack, xown, store, field, turned, full,
-        lambda local, gain: 2.0 - local * gain,
-    )
-    block = min(8, slab) * zcap
-
-    def turn(i, _):
-        at = pl.multiple_of(i * block, block)
-        summed[pl.ds(at, block), :] = free[0, pl.ds(at, block), :] + along_y(
-            turned[pl.ds(at, block), :], ystack[...]
-        )
+            later = twice * value - first
+            onward[at] = later
+            planes.append(later)
+        for j in range(0, group, 2):
+            wide = dot(zstack[...], tall_split(jnp.concatenate(planes[j : j + 2], axis=1)))
+            for half in range(2):
+                at = pl.multiple_of((group * i + j + half) * zcap, zcap)
+                field[pl.ds(at, zcap), :] = wide[:, half * width : (half + 1) * width]
         return 0
 
-    lax.fori_loop(0, slab * zcap // block, turn, 0)
-
-
-def last_kernel(
-    extent, own, near, tx, uy, onward, summed, rows, zstack, ystack, xown, *rest, full, parts
-):
-    far, given = rest[:parts], rest[parts : 2 * parts - 1]
-    modes, pressure, spare, force, field, turned = rest[2 * parts - 1 :]
+    lax.fori_loop(0, slab // group, body, 0)
+    block = min(16, slab) * zcap
+    for i in range(slab * zcap // block):
+        span = slice(i * block, (i + 1) * block)
+        field[span, :] = along_y(field[span, :], ystack[...])
+    parts = full // slab
+    across = xparts[own[0]]
+    for i in range(0, zcap, 2):
+        pair = [field[pl.ds(i + half, slab, stride=zcap), :] for half in range(2)]
+        wide = dot(across, tall_split(jnp.concatenate(pair, axis=1)))
+        for k in range(parts):
+            for half in range(2):
+                free[k][pl.ds(i + half, slab, stride=zcap), :] = wide[
+                    k * slab : (k + 1) * slab, half * width : (half + 1) * width
+                ]
+
+
+def last_kernel(own, near, tx, uy, onward, estack, hstack, ystack, xown, *rest, full, parts):
+    far, given = rest[:parts], rest[parts : 2 * parts]
+    modes, pressure, spare, force, terms, turned = rest[2 * parts :]
     slab, zcap, width = onward.shape
+    depth = estack.shape[1] // 3
+    used = TERMS * ROWS
     gather_kx(spare, far, own[0])
     force_planes(spare, near, tx, uy, force)
-
-    def store(kx, local, gain, total):
-        at = kx - own[0] * slab
-
-        @pl.when((at >= 0) & (at < slab))
-        def _():
-            modes[at] = onward[at] + total
-
-    lift(
-        extent[0], own[0], force, rows, zstack, ystack, xown, store, field, turned, full, None
-    )
-    block = min(8, slab) * zcap
-
-    def turn(i, _):
-        at = pl.multiple_of(i * block, block)
-        value = summed[pl.ds(at, block), :]
-        for piece in given:
-            value = value + piece[pl.ds(at, block), :]
-        pressure[pl.ds(at, block), :] = value + along_y(turned[pl.ds(at, block), :], ystack[...])
-        return 0
-
-    lax.fori_loop(0, slab * zcap // block, turn, 0)
+    ax = lax.broadcasted_iota(jnp.int32, (full, width), 0).astype(F32) / full
+    ay = lax.broadcasted_iota(jnp.int32, (full, width), 1).astype(F32) / width
+    square = BASE * (ax * ax + ay * ay) - BASE
+    terms[used * full :, :] = jnp.zeros(((depth - used) * full, width), F32)
+    turned[used * slab :, :] = jnp.zeros(((depth - used) * slab, width), F32)
+    across = xown[own[0]]
+    planes = [plane(force, r) for r in range(ROWS)]
+    for n in range(TERMS):
+        if n:
+            planes = [value * square for value in planes]
+        for r in range(0, ROWS, 2):
+            at = n * ROWS + r
+            for half in range(2):
+                terms[(at + half) * full : (at + half + 1) * full, :] = planes[r + half]
+            wide = dot(across, tall_split(jnp.concatenate(planes[r : r + 2], axis=1)))
+            for half in range(2):
+                turned[(at + half) * slab : (at + half + 1) * slab, :] = wide[
+                    :, half * width : (half + 1) * width
+                ]
+    block = ROWS * slab
+    for n in range(TERMS):
+        span = slice(n * block, (n + 1) * block)
+        turned[span, :] = along_y(turned[span, :], ystack[...])
+    own_at = own[0] * slab
+    for i in range(0, slab, 2):
+        pair = [terms[pl.ds(own_at + i + half, depth, stride=full), :] for half in range(2)]
+        wide = dot(estack[...], tall_split(jnp.concatenate(pair, axis=1)))
+        for half in range(2):
+            modes[i + half] = onward[i + half] + wide[:, half * width : (half + 1) * width]
+    for i in range(0, slab, 2):
+        pair = [turned[pl.ds(i + half, depth, stride=slab), :] for half in range(2)]
+        wide = dot(hstack[...], tall_split(jnp.concatenate(pair, axis=1)))
+        for half in range(2):
+            span = slice((i + half) * zcap, (i + half + 1) * zcap)
+            value = wide[:, half * width : (half + 1) * width]
+            for piece in given:
+                value = value + piece[span, :]
+            pressure[span, :] = value
 
 
 def on_device(modes_now, modes_prev, z_extent, lower_nbr, upper_nbr, x_shift, y_shift):
@@ -478,16 +460,18 @@
     big = 4 * slab * zcap * width
 
     xtable, ytable = static_table(full), static_table(width)
-    lanes = np.zeros((8, width), np.float32)
+    consts = np.zeros((40, width), np.float32)
     for r in range(ROWS):
-        lanes[0, r], lanes[1, r] = (r, 0) if r < FACE else (ROWS - 1 - r, 1)
+        consts[0, r], consts[1, r] = (r, 0) if r < FACE else (ROWS - 1 - r, 1)
     for p, (r, q) in enumerate(PAIRS):
-        lanes[2, p], lanes[3, p] = lanes[0, r], lanes[1, r]
-        lanes[4, p], lanes[5, p] = lanes[0, q], lanes[1, q]
-    series = np.zeros((16, width), np.float32)
-    for j in range(TERMS):
-        for n in range(TERMS - j):
-            series[j, n] = SERIES[n + j] * math.comb(n + j, n)
+        consts[2:4, p], consts[4:6, p] = consts[0:2, r], consts[0:2, q]
+    for n in range(TERMS):
+        for j in range(len(SERIES) - n):
+            value = SERIES[n + j] * math.comb(n + j, n)
+            consts[8 + j, n] = value
+            consts[24 + j, n * ROWS : (n + 1) * ROWS] = value
+        consts[6:8, n * ROWS : (n + 1) * ROWS] = consts[0:2, :ROWS]
+    depth = -(-TERMS * ROWS // 16) * 16
     yhigh, ylow = halves(ytable)
     ystack = np.block([[yhigh, ylow], [yhigh, np.zeros_like(yhigh)]])
     xhigh, xlow = halves(xtable.T)
@@ -519,11 +503,11 @@
 
     def tall_of(table):
         n = table.shape[0]
-        return np.pad(table.T, ((n, n), (0, 0))).astype(np.float32)
-
-    lanes, series, ystack, xown, xparts = map(jnp.asarray, (lanes, series, ystack, xown, xparts))
-    xplain, xtall = jnp.asarray(xtable.astype(np.float32)), jnp.asarray(tall_of(xtable))
-    yplain, ytall = jnp.asarray(ytable.astype(np.float32)), jnp.asarray(tall_of(ytable))
+        tall = np.pad(table.T, ((n, n), (0, 0)))
+        return jnp.asarray(np.concatenate([tall, table], axis=0).astype(np.float32))
+
+    consts, ystack, xown, xparts = map(jnp.asarray, (consts, ystack, xown, xparts))
+    xtall, ytall = tall_of(xtable), tall_of(ytable)
 
     def swap(piece):
         got = [piece]
@@ -564,29 +548,25 @@
         [SMEM] * 3 + [VMEM] * 2,
         moved=big,
         name="strip",
-    )(z_extent, lower_nbr, upper_nbr, modes_now, lanes)
+    )(z_extent, lower_nbr, upper_nbr, modes_now, consts)
     chosen = spread(packet)
     mine = swap(packet[:size])
 
-    ahead, free, zstack, coefs = call(
+    ahead, zstack, estack, hstack, coefs = call(
         functools.partial(ahead_kernel, full=full),
         [
             shape_of(size, width),
-            shape_of(parts, slab * zcap, width),
             shape_of(zcap, 3 * zcap, dtype=BF16),
+            shape_of(zcap, 3 * depth, dtype=BF16),
+            shape_of(zcap, 3 * depth, dtype=BF16),
             shape_of(16, width),
         ],
-        [SMEM] * 2 + [VMEM] * 7,
-        scratch=[pltpu.VMEM((slab * zcap, width), F32)],
-        flops=10**9,
-        moved=4 * big,
+        [SMEM] * 2 + [VMEM] * 4,
+        flops=10**8,
+        moved=2 * big,
         name="ahead",
-    )(z_extent, own, modes_now, modes_prev, rows, lanes, series, xparts, ystack)
+    )(z_extent, own, modes_now, modes_prev, rows, consts)
     aheads = swap(ahead)
-    given = [
-        lax.ppermute(free[k], "split", [(i, (i + k) % parts) for i in range(parts)])
-        for k in range(1, parts)
-    ]
 
     tx, uy, vx, wy, near1, mixing, _ = call(
         functools.partial(relation_kernel, parts=parts),
@@ -599,14 +579,11 @@
             shape_of(len(PAIRS), full, width),
             shape_of(ROWS * full, width),
         ],
-        [SMEM] * 6 + [ANY] + [VMEM] * (4 + parts),
+        [SMEM] * 6 + [ANY] + [VMEM] * (2 + parts),
         flops=10**8,
         moved=2 * big,
         name="relation",
-    )(
-        lower_nbr, upper_nbr, x_shift, y_shift, own, coefs, chosen[0],
-        xplain, xtall, yplain, ytall, *mine,
-    )
+    )(lower_nbr, upper_nbr, x_shift, y_shift, own, coefs, chosen[0], xtall, ytall, *mine)
 
     packet2, force1, strip2 = call(
         functools.partial(middle_kernel, parts=parts),
@@ -623,22 +600,19 @@
     )(own, lower_nbr, upper_nbr, near1, tx, uy, mixing, *deliver(chosen), *aheads)
 
     chosen2 = spread(packet2)
-    current, onward, summed = call(
+    current, onward, *free = call(
         functools.partial(between_kernel, full=full),
-        [
-            shape_of(slab, zcap, width),
-            shape_of(slab, zcap, width),
-            shape_of(slab * zcap, width),
-        ],
-        [SMEM] * 2 + [VMEM] * 8,
-        scratch=[
-            pltpu.VMEM((full * zcap, width), F32),
-            pltpu.VMEM((slab * zcap, width), F32),
-        ],
+        [shape_of(slab, zcap, width)] * 2 + [shape_of(slab * zcap, width)] * parts,
+        [SMEM] * 2 + [VMEM] * 7,
+        scratch=[pltpu.VMEM((slab * zcap, width), F32)],
         flops=10**9,
         moved=6 * big,
         name="between",
-    )(z_extent, own, modes_now, modes_prev, force1, rows, zstack, ystack, xown, free)
+    )(z_extent, own, modes_now, modes_prev, force1, rows, zstack, ystack, xparts)
+    given = [free[0]] + [
+        lax.ppermute(free[k], "split", [(i, (i + k) % parts) for i in range(parts)])
+        for k in range(1, parts)
+    ]
     near2 = call(
         near_kernel,
         [shape_of(ROWS * full, width)],
@@ -651,20 +625,17 @@
     modes, pressure = call(
         functools.partial(last_kernel, full=full, parts=parts),
         [shape_of(slab, zcap, width), shape_of(slab * zcap, width)],
-        [SMEM] * 2 + [VMEM] * (9 + 2 * parts - 1),
+        [SMEM] + [VMEM] * (8 + 2 * parts),
         scratch=[
             pltpu.VMEM((ROWS * full, width), F32),
             pltpu.VMEM((ROWS * full, width), F32),
-            pltpu.VMEM((full * zcap, width), F32),
-            pltpu.VMEM((slab * zcap, width), F32),
+            pltpu.VMEM((depth * full, width), F32),
+            pltpu.VMEM((depth * slab, width), F32),
         ],
         flops=10**9,
         moved=6 * big,
         name="last",
-    )(
-        z_extent, own, near2, tx, uy, onward, summed, rows, zstack, ystack, xown,
-        *deliver(chosen2), *given,
-    )
+    )(own, near2, tx, uy, onward, estack, hstack, ystack, xown, *deliver(chosen2), *given)
     return (modes, current, pressure.reshape(slab, zcap, width))
 
 

time: 112 us -> 66.1 us (0.59)
  Pallas kernels: 49.1 us -> 15.7 us
  local copies, waits for them, and re-layouts: 11.2 us -> 3.38 us
  starting transfers between devices: 23.3 us -> 20.5 us
  waiting for transfers between devices: 24.8 us -> 22.8 us
    pallas_call x1, Pallas kernels: 16 us -> 3.49 us  [on_device(): call(functools.partial(last_kernel, full=full, parts=parts), [shape_of(sl...]
    pallas_call x1, Pallas kernels: 15.7 us -> 5.22 us  [on_device(): call(functools.partial(between_kernel, full=full), [shape_of(slab, zcap,...]
    pallas_call x1, Pallas kernels: 11.6 us -> 2.26 us  [on_device(): call(functools.partial(ahead_kernel, full=full), [shape_of(size, width),...]
    unnamed x38 -> x26, local copies, waits for them, and re-layouts: 10.1 us -> 3.37 us
    ppermute x6, waiting for transfers between devices: 10.5 us -> 5.73 us  [deliver(): got.append(lax.ppermute(chosen[k], 'dom', to))]
    ppermute x6, waiting for transfers between devices: 7.75 us -> 11.2 us  [spread(): held.append(lax.ppermute(packet, 'dom', to))]
    ppermute x6, starting transfers between devices: 11.5 us -> 9.62 us  [deliver(): got.append(lax.ppermute(chosen[k], 'dom', to))]
    ppermute x1, starting transfers between devices: 2.97 us -> 1.2 us  [on_device(): lax.ppermute(free[k], 'split', [(i, (i + k) % parts) for i in range(parts)])]
  transfers between devices with their start and end apart: 17 -> 17, of which waited for: 11 -> 10; matrix products, arithmetic and copies ran while one was open for 0% -> 0% of each run, Pallas kernels for 19% -> 8%
where the time goes in v1:
time: 66.1 us; the launch traced here: 65.1 us
  waiting for transfers between devices  22.8 us (34%)
  starting transfers between devices  20.5 us (31%)
  Pallas kernels  15.7 us (24%)
  local copies, waits for them, and re-layouts  3.38 us (5%)
  between operations  2.73 us (4%)
    ppermute x6, waiting for transfers between devices, spread(): held.append(lax.ppermute(packet, 'dom', to))  11.2 us
    ppermute x6, starting transfers between devices, deliver(): got.append(lax.ppermute(chosen[k], 'dom', to))  9.62 us
    ppermute x4, waiting for transfers between devices, swap(): lax.ppermute(piece, 'split', [(i, (i + k) % parts) for i in range(parts)])  5.83 us
    ppermute x6, waiting for transfers between devices, deliver(): got.append(lax.ppermute(chosen[k], 'dom', to))  5.73 us
    pallas_call x1, Pallas kernels, on_device(): call(functools.partial(between_kernel, full=full), [shape_of(slab, zcap,...  5.22 us
    ppermute x6, starting transfers between devices, spread(): held.append(lax.ppermute(packet, 'dom', to))  4.93 us
    ppermute x4, starting transfers between devices, swap(): lax.ppermute(piece, 'split', [(i, (i + k) % parts) for i in range(parts)])  4.79 us
    pallas_call x1, Pallas kernels, on_device(): call(functools.partial(last_kernel, full=full, parts=parts), [shape_of(sl...  3.49 us
  transfers between devices with their start and end apart: 17, of which 10 were waited for; matrix products, arithmetic and copies ran while one was open for 0% of the time, Pallas kernels for 8%

profile of v1, /device:TPU:0, one launch (start us, length us, event | category | flops | bytes accessed | tf_op | source)
XLA Modules:
  0.0 65.1 jit_solution(388501461357076504)
XLA Ops:
  2.6 1.2 %copy-done = f32[32,64,128]{2,1,0:T(8,128)S(1)} copy-done((f32[32,64,128]{2,1,0:T(8,128)S(1)}, f32[32,64,128]{2,1,0:T(8,128)}, u32[]{:S(2)}) %copy-start) | copy-done | bytes 1048600
  5.5 2.4 %collective-permute-start.2 = (f32[200,128]{1,0:T(8,128)S(1)}, f32[200,128]{1,0:T(8,128)S(1)}, u32[]{:S(2)}, u32[]{:S(2)}) collective-permute-start(f32[200,128]{1,0:T(8,128)S(1)} %get-tuple-element.35.refs_0_), channel_id=1, source_target_pairs={{0,6},{2,0},{4,2},{6,4},{8,14},{10,8},{12,10},{14,12},{16,22},{18,... | collective-permute-start | bytes 307208 | tf_op jit(solution)/shard_map/ppermute | solution.py:522
  8.7 2.4 %collective-permute-done.2.refs_3_ = f32[200,128]{1,0:T(8,128)S(1)} collective-permute-done((f32[200,128]{1,0:T(8,128)S(1)}, f32[200,128]{1,0:T(8,128)S(1)}, u32[]{:S(2)}, u32[]{:S(2)}) %collective-permute-start.2) | collective-permute-done | bytes 102432 | tf_op jit(solution)/shard_map/ppermute | solution.py:522
  11.1 3.2 %collective-permute-done.1.refs_2_ = f32[200,128]{1,0:T(8,128)S(1)} collective-permute-done((f32[200,128]{1,0:T(8,128)S(1)}, f32[200,128]{1,0:T(8,128)S(1)}, u32[]{:S(2)}, u32[]{:S(2)}) %collective-permute-start.1) | collective-permute-done | bytes 102432 | tf_op jit(solution)/shard_map/ppermute | solution.py:522
  14.3 1.8 %collective-permute-start.4 = (f32[192,128]{1,0:T(8,128)S(1)}, f32[192,128]{1,0:T(8,128)S(1)}, u32[]{:S(2)}, u32[]{:S(2)}) collective-permute-start(f32[192,128]{1,0:T(8,128)S(1)} %get-tuple-element.41), channel_id=1, source_target_pairs={{0,8},{2,10},{4,12},{6,14},{8,16},{10,18},{12,20},{14,22},{16,24},... | collective-permute-start | bytes 294920 | tf_op jit(solution)/shard_map/ppermute | solution.py:535
  16.1 2.6 %collective-permute-start.5 = (f32[192,128]{1,0:T(8,128)S(1)}, f32[192,128]{1,0:T(8,128)S(1)}, u32[]{:S(2)}, u32[]{:S(2)}) collective-permute-start(f32[192,128]{1,0:T(8,128)S(1)} %get-tuple-element.42), channel_id=1, source_target_pairs={{0,16},{2,18},{4,20},{6,22},{8,24},{10,26},{12,28},{14,30},{16,0},... | collective-permute-start | bytes 294920 | tf_op jit(solution)/shard_map/ppermute | solution.py:535
  18.7 1.3 %collective-permute-start.6 = (f32[192,128]{1,0:T(8,128)S(1)}, f32[192,128]{1,0:T(8,128)S(1)}, u32[]{:S(2)}, u32[]{:S(2)}) collective-permute-start(f32[192,128]{1,0:T(8,128)S(1)} %get-tuple-element.43), channel_id=1, source_target_pairs={{0,24},{2,26},{4,28},{6,30},{8,0},{10,2},{12,4},{14,6},{16,8},{18,... | collective-permute-start | bytes 294920 | tf_op jit(solution)/shard_map/ppermute | solution.py:535
  20.1 1.6 %collective-permute-start.3 = (f32[192,128]{1,0:T(8,128)S(1)}, f32[192,128]{1,0:T(8,128)S(1)}, u32[]{:S(2)}, u32[]{:S(2)}) collective-permute-start(f32[192,128]{1,0:T(8,128)S(1)} %slice.3.rest_0_), channel_id=1, source_target_pairs={{0,1},{1,0},{2,3},{3,2},{4,5},{5,4},{6,7},{7,6},{8,9},{9,8},{10,11... | collective-permute-start | bytes 294920 | tf_op jit(solution)/shard_map/ppermute | solution.py:515
  21.7 1.2 %copy-done.2 = f32[32,64,128]{2,1,0:T(8,128)S(1)} copy-done((f32[32,64,128]{2,1,0:T(8,128)S(1)}, f32[32,64,128]{2,1,0:T(8,128)}, u32[]{:S(2)}) %copy-start.2) | copy-done | bytes 1048600
  22.9 2.3 %ahead.1 = (f32[192,128]{1,0:T(8,128)S(1)}, bf16[64,192]{1,0:T(8,128)(2,1)S(1)}, bf16[64,144]{1,0:T(8,128)(2,1)S(1)}, bf16[64,144]{1,0:T(8,128)(2,1)S(1)}, f32[16,128]{1,0:T(8,128)S(1)}) custom-call(s32[1]{0:T(128)S(6)} %copy.16.extent, s32[1]{0:T(128)} %bitcast.own, f32[32,64,128]{2,1,0:T(8,128)S(1)} %copy-done.1, f32[32,64,128]{2,1,0:T(8,128)S(1)} %copy-done.2, ...), custom_call_target="tpu_custom_call" | custom-call | flops 100000000 | bytes 2097152 | tf_op jit(solution)/shard_map/ahead/pallas_call | solution.py:555
  26.0 1.4 %collective-permute-start.7 = (f32[192,128]{1,0:T(8,128)S(1)}, f32[192,128]{1,0:T(8,128)S(1)}, u32[]{:S(2)}, u32[]{:S(2)}) collective-permute-start(f32[192,128]{1,0:T(8,128)S(1)} %pick.2.rest_0_), channel_id=1, source_target_pairs={{0,1},{1,0},{2,3},{3,2},{4,5},{5,4},{6,7},{7,6},{8,9},{9,8},{10,11... | collective-permute-start | bytes 294920 | tf_op jit(solution)/shard_map/ppermute | solution.py:515
  27.5 2.1 %relation.1 = (f32[2,64,64]{2,1,0:T(8,128)S(1)}, f32[2,128,128]{2,1,0:T(8,128)S(1)}, f32[2,64,64]{2,1,0:T(8,128)S(1)}, f32[2,128,128]{2,1,0:T(8,128)S(1)}, f32[3...) custom-call(s32[1]{0:T(128)S(6)} %copy.17.below, s32[1]{0:T(128)S(6)} %copy.18.above, ...), custom_call_target="tpu_custom_call" | custom-call | flops 100000000 | bytes 2097152 | tf_op jit(solution)/shard_map/relation/pallas_call | solution.py:571
  29.9 1.1 %collective-permute-done.7.rest_1_ = f32[192,128]{1,0:T(8,128)S(1)} collective-permute-done((f32[192,128]{1,0:T(8,128)S(1)}, f32[192,128]{1,0:T(8,128)S(1)}, u32[]{:S(2)}, u32[]{:S(2)}) %collective-permute-start.7) | collective-permute-done | bytes 98336 | tf_op jit(solution)/shard_map/ppermute | solution.py:515
  31.8 5.2 %between.1 = (f32[32,64,128]{2,1,0:T(8,128)}, f32[32,64,128]{2,1,0:T(8,128)S(1)}, f32[2048,128]{1,0:T(8,128)S(1)}, f32[2048,128]{1,0:T(8,128)S(1)}) custom-call(s32[1]{0:T(128)S(6)} %copy.16.extent, s32[1]{0:T(128)} %bitcast.own, f32[32,64,128]{2,1,0:T(8,128)S(1)} %copy-done.1, f32[32,64,128]{2,1,0:T(8,128)S(1)} %copy-done.3, ...), custom_call_target="tpu_custom_call" | custom-call | flops 1000000000 | bytes 6291456 | tf_op jit(solution)/shard_map/between/pallas_call | solution.py:603
  37.1 1.2 %collective-permute-start.16 = (f32[2048,128]{1,0:T(8,128)S(1)}, f32[2048,128]{1,0:T(8,128)S(1)}, u32[]{:S(2)}, u32[]{:S(2)}) collective-permute-start(f32[2048,128]{1,0:T(8,128)S(1)} %get-tuple-element.59), channel_id=1, source_target_pairs={{0,1},{1,0},{2,3},{3,2},{4,5},{5,4},{6,7},{7,6},{8,9},{9,8},{10,11... | collective-permute-start | bytes 3145736 | tf_op jit(solution)/shard_map/ppermute | solution.py:613
  38.3 1.5 %collective-permute-start.10 = (f32[200,128]{1,0:T(8,128)S(1)}, f32[200,128]{1,0:T(8,128)S(1)}, u32[]{:S(2)}, u32[]{:S(2)}) collective-permute-start(f32[200,128]{1,0:T(8,128)S(1)} %get-tuple-element.53.refs_0_), channel_id=1, source_target_pairs={{0,4},{2,6},{4,0},{6,2},{8,12},{10,14},{12,8},{14,10},{16,20},{18,... | collective-permute-start | bytes 307208 | tf_op jit(solution)/shard_map/ppermute | solution.py:522
  40.5 5.0 %collective-permute-done.10.refs_2_ = f32[200,128]{1,0:T(8,128)S(1)} collective-permute-done((f32[200,128]{1,0:T(8,128)S(1)}, f32[200,128]{1,0:T(8,128)S(1)}, u32[]{:S(2)}, u32[]{:S(2)}) %collective-permute-start.10) | collective-permute-done | bytes 102432 | tf_op jit(solution)/shard_map/ppermute | solution.py:522
  46.6 1.5 %collective-permute-start.13 = (f32[192,128]{1,0:T(8,128)S(1)}, f32[192,128]{1,0:T(8,128)S(1)}, u32[]{:S(2)}, u32[]{:S(2)}) collective-permute-start(f32[192,128]{1,0:T(8,128)S(1)} %get-tuple-element.56), channel_id=1, source_target_pairs={{0,16},{2,18},{4,20},{6,22},{8,24},{10,26},{12,28},{14,30},{16,0},... | collective-permute-start | bytes 294920 | tf_op jit(solution)/shard_map/ppermute | solution.py:535
  48.1 1.5 %collective-permute-start.14 = (f32[192,128]{1,0:T(8,128)S(1)}, f32[192,128]{1,0:T(8,128)S(1)}, u32[]{:S(2)}, u32[]{:S(2)}) collective-permute-start(f32[192,128]{1,0:T(8,128)S(1)} %get-tuple-element.57), channel_id=1, source_target_pairs={{0,24},{2,26},{4,28},{6,30},{8,0},{10,2},{12,4},{14,6},{16,8},{18,... | collective-permute-start | bytes 294920 | tf_op jit(solution)/shard_map/ppermute | solution.py:535
  49.6 3.2 %collective-permute-done.12.refs_1_ = f32[192,128]{1,0:T(8,128)S(1)} collective-permute-done((f32[192,128]{1,0:T(8,128)S(1)}, f32[192,128]{1,0:T(8,128)S(1)}, u32[]{:S(2)}, u32[]{:S(2)}) %collective-permute-start.12) | collective-permute-done | bytes 98336 | tf_op jit(solution)/shard_map/ppermute | solution.py:535
  52.9 2.5 %collective-permute-done.13.refs_2_ = f32[192,128]{1,0:T(8,128)S(1)} collective-permute-done((f32[192,128]{1,0:T(8,128)S(1)}, f32[192,128]{1,0:T(8,128)S(1)}, u32[]{:S(2)}, u32[]{:S(2)}) %collective-permute-start.13) | collective-permute-done | bytes 98336 | tf_op jit(solution)/shard_map/ppermute | solution.py:535
  55.4 1.1 %collective-permute-start.15 = (f32[192,128]{1,0:T(8,128)S(1)}, f32[192,128]{1,0:T(8,128)S(1)}, u32[]{:S(2)}, u32[]{:S(2)}) collective-permute-start(f32[192,128]{1,0:T(8,128)S(1)} %pick.3.rest_0_), channel_id=1, source_target_pairs={{0,1},{1,0},{2,3},{3,2},{4,5},{5,4},{6,7},{7,6},{8,9},{9,8},{10,11... | collective-permute-start | bytes 294920 | tf_op jit(solution)/shard_map/ppermute | solution.py:515
  57.1 4.5 %collective-permute-done.15.rest_1_ = f32[192,128]{1,0:T(8,128)S(1)} collective-permute-done((f32[192,128]{1,0:T(8,128)S(1)}, f32[192,128]{1,0:T(8,128)S(1)}, u32[]{:S(2)}, u32[]{:S(2)}) %collective-permute-start.15) | collective-permute-done | bytes 98336 | tf_op jit(solution)/shard_map/ppermute | solution.py:515
  61.6 3.5 %last.1 = (f32[32,64,128]{2,1,0:T(8,128)}, f32[2048,128]{1,0:T(8,128)}) custom-call(s32[1]{0:T(128)} %bitcast.own, f32[384,128]{1,0:T(8,128)S(1)} %near.1, f32[2,64,64]{2,1,0:T(8,128)S(1)} %get-tuple-element.38.tx, f32[2,128,128]{2,1,0:T(8,128)S(1)} %get-tuple-element.39.uy, f32[32,64,128]{2,1,0:T(8,128)S(1)} %get-tuple-element.50.onward, ...), custom_call_target="tpu_custom_call" | custom-call | flops 1000000000 | bytes 6291456 | tf_op jit(solution)/shard_map/last/pallas_call | solution.py:625
  (48 shorter events, 7.2 us)
Async XLA Ops:
  4.5 17.2 %copy-start.1 = (f32[32,64,128]{2,1,0:T(8,128)S(1)}, f32[32,64,128]{2,1,0:T(8,128)}, u32[]{:S(2)}) copy-start(f32[32,64,128]{2,1,0:T(8,128)} %now.5) | copy-start | bytes 3145732
  5.5 5.6 %collective-permute-start.2 = (f32[200,128]{1,0:T(8,128)S(1)}, f32[200,128]{1,0:T(8,128)S(1)}, u32[]{:S(2)}, u32[]{:S(2)}) collective-permute-start(f32[200,128]{1,0:T(8,128)S(1)} %get-tuple-element.35.refs_0_), channel_id=1, source_target_pairs={{0,6},{2,0},{4,2},{6,4},{8,14},{10,8},{12,10},{14,12},{16,22},{18,... | collective-permute-start | bytes 307208 | tf_op jit(solution)/shard_map/ppermute | solution.py:522
  7.9 6.3 %collective-permute-start.1 = (f32[200,128]{1,0:T(8,128)S(1)}, f32[200,128]{1,0:T(8,128)S(1)}, u32[]{:S(2)}, u32[]{:S(2)}) collective-permute-start(f32[200,128]{1,0:T(8,128)S(1)} %get-tuple-element.35.refs_0_), channel_id=1, source_target_pairs={{0,4},{2,6},{4,0},{6,2},{8,12},{10,14},{12,8},{14,10},{16,20},{18,... | collective-permute-start | bytes 307208 | tf_op jit(solution)/shard_map/ppermute | solution.py:522
  8.6 5.7 %collective-permute-start = (f32[200,128]{1,0:T(8,128)S(1)}, f32[200,128]{1,0:T(8,128)S(1)}, u32[]{:S(2)}, u32[]{:S(2)}) collective-permute-start(f32[200,128]{1,0:T(8,128)S(1)} %get-tuple-element.35.refs_0_), channel_id=1, source_target_pairs={{0,2},{2,4},{4,6},{6,0},{8,10},{10,12},{12,14},{14,8},{16,18},{18,... | collective-permute-start | bytes 307208 | tf_op jit(solution)/shard_map/ppermute | solution.py:522
  14.3 11.6 %collective-permute-start.4 = (f32[192,128]{1,0:T(8,128)S(1)}, f32[192,128]{1,0:T(8,128)S(1)}, u32[]{:S(2)}, u32[]{:S(2)}) collective-permute-start(f32[192,128]{1,0:T(8,128)S(1)} %get-tuple-element.41), channel_id=1, source_target_pairs={{0,8},{2,10},{4,12},{6,14},{8,16},{10,18},{12,20},{14,22},{16,24},... | collective-permute-start | bytes 294920 | tf_op jit(solution)/shard_map/ppermute | solution.py:535
  16.1 9.8 %collective-permute-start.5 = (f32[192,128]{1,0:T(8,128)S(1)}, f32[192,128]{1,0:T(8,128)S(1)}, u32[]{:S(2)}, u32[]{:S(2)}) collective-permute-start(f32[192,128]{1,0:T(8,128)S(1)} %get-tuple-element.42), channel_id=1, source_target_pairs={{0,16},{2,18},{4,20},{6,22},{8,24},{10,26},{12,28},{14,30},{16,0},... | collective-permute-start | bytes 294920 | tf_op jit(solution)/shard_map/ppermute | solution.py:535
  18.7 7.2 %collective-permute-start.6 = (f32[192,128]{1,0:T(8,128)S(1)}, f32[192,128]{1,0:T(8,128)S(1)}, u32[]{:S(2)}, u32[]{:S(2)}) collective-permute-start(f32[192,128]{1,0:T(8,128)S(1)} %get-tuple-element.43), channel_id=1, source_target_pairs={{0,24},{2,26},{4,28},{6,30},{8,0},{10,2},{12,4},{14,6},{16,8},{18,... | collective-permute-start | bytes 294920 | tf_op jit(solution)/shard_map/ppermute | solution.py:535
  20.1 1.6 %copy-start.8 = (f32[40,128]{1,0:T(8,128)S(1)}, f32[40,128]{1,0:T(8,128)}, u32[]{:S(2)}) copy-start(f32[40,128]{1,0:T(8,128)} %constant.20.clone.consts) | copy-start | bytes 61444
  20.1 7.4 %collective-permute-start.3 = (f32[192,128]{1,0:T(8,128)S(1)}, f32[192,128]{1,0:T(8,128)S(1)}, u32[]{:S(2)}, u32[]{:S(2)}) collective-permute-start(f32[192,128]{1,0:T(8,128)S(1)} %slice.3.rest_0_), channel_id=1, source_target_pairs={{0,1},{1,0},{2,3},{3,2},{4,5},{5,4},{6,7},{7,6},{8,9},{9,8},{10,11... | collective-permute-start | bytes 294920 | tf_op jit(solution)/shard_map/ppermute | solution.py:515
  25.2 2.3 %copy-start.4 = (f32[512,128]{1,0:T(8,128)S(1)}, f32[512,128]{1,0:T(8,128)}, u32[]{:S(2)}) copy-start(f32[512,128]{1,0:T(8,128)} %constant.25.clone.ytall) | copy-start | bytes 786436
  25.2 4.7 %collective-permute-start.8 = (f32[192,128]{1,0:T(8,128)S(1)}, f32[192,128]{1,0:T(8,128)S(1)}, u32[]{:S(2)}, u32[]{:S(2)}) collective-permute-start(f32[192,128]{1,0:T(8,128)S(1)} %get-tuple-element.44.rest_2_), channel_id=1, source_target_pairs={{0,1},{1,0},{2,3},{3,2},{4,5},{5,4},{6,7},{7,6},{8,9},{9,8},{10,11... | collective-permute-start | bytes 294920 | tf_op jit(solution)/shard_map/ppermute | solution.py:515
  25.9 1.5 %copy-start.6 = (f32[256,64]{1,0:T(8,128)S(1)}, f32[256,64]{1,0:T(8,128)}, u32[]{:S(2)}) copy-start(f32[256,64]{1,0:T(8,128)} %constant.24.clone.xtall) | copy-start | bytes 196612
  26.0 1.5 %copy-start.10 = (s32[1,2]{1,0:T(1,128)S(1)}, s32[1,2]{1,0:T(1,128)}, u32[]{:S(2)}) copy-start(s32[1,2]{1,0:T(1,128)} %x_shift.1) | copy-start | bytes 28
  26.0 4.9 %collective-permute-start.7 = (f32[192,128]{1,0:T(8,128)S(1)}, f32[192,128]{1,0:T(8,128)S(1)}, u32[]{:S(2)}, u32[]{:S(2)}) collective-permute-start(f32[192,128]{1,0:T(8,128)S(1)} %pick.2.rest_0_), channel_id=1, source_target_pairs={{0,1},{1,0},{2,3},{3,2},{4,5},{5,4},{6,7},{7,6},{8,9},{9,8},{10,11... | collective-permute-start | bytes 294920 | tf_op jit(solution)/shard_map/ppermute | solution.py:515
  27.5 4.2 %copy-start.3 = (f32[32,64,128]{2,1,0:T(8,128)S(1)}, f32[32,64,128]{2,1,0:T(8,128)}, u32[]{:S(2)}) copy-start(f32[32,64,128]{2,1,0:T(8,128)} %prev.3) | copy-start | bytes 3145732
  37.1 24.5 %collective-permute-start.16 = (f32[2048,128]{1,0:T(8,128)S(1)}, f32[2048,128]{1,0:T(8,128)S(1)}, u32[]{:S(2)}, u32[]{:S(2)}) collective-permute-start(f32[2048,128]{1,0:T(8,128)S(1)} %get-tuple-element.59), channel_id=1, source_target_pairs={{0,1},{1,0},{2,3},{3,2},{4,5},{5,4},{6,7},{7,6},{8,9},{9,8},{10,11... | collective-permute-start | bytes 3145736 | tf_op jit(solution)/shard_map/ppermute | solution.py:613
  38.3 2.3 %collective-permute-start.11 = (f32[200,128]{1,0:T(8,128)S(1)}, f32[200,128]{1,0:T(8,128)S(1)}, u32[]{:S(2)}, u32[]{:S(2)}) collective-permute-start(f32[200,128]{1,0:T(8,128)S(1)} %get-tuple-element.53.refs_0_), channel_id=1, source_target_pairs={{0,6},{2,0},{4,2},{6,4},{8,14},{10,8},{12,10},{14,12},{16,22},{18,... | collective-permute-start | bytes 307208 | tf_op jit(solution)/shard_map/ppermute | solution.py:522
  38.3 7.3 %collective-permute-start.10 = (f32[200,128]{1,0:T(8,128)S(1)}, f32[200,128]{1,0:T(8,128)S(1)}, u32[]{:S(2)}, u32[]{:S(2)}) collective-permute-start(f32[200,128]{1,0:T(8,128)S(1)} %get-tuple-element.53.refs_0_), channel_id=1, source_target_pairs={{0,4},{2,6},{4,0},{6,2},{8,12},{10,14},{12,8},{14,10},{16,20},{18,... | collective-permute-start | bytes 307208 | tf_op jit(solution)/shard_map/ppermute | solution.py:522
  39.7 5.9 %collective-permute-start.9 = (f32[200,128]{1,0:T(8,128)S(1)}, f32[200,128]{1,0:T(8,128)S(1)}, u32[]{:S(2)}, u32[]{:S(2)}) collective-permute-start(f32[200,128]{1,0:T(8,128)S(1)} %get-tuple-element.53.refs_0_), channel_id=1, source_target_pairs={{0,2},{2,4},{4,6},{6,0},{8,10},{10,12},{12,14},{14,8},{16,18},{18,... | collective-permute-start | bytes 307208 | tf_op jit(solution)/shard_map/ppermute | solution.py:522
  45.8 7.1 %collective-permute-start.12 = (f32[192,128]{1,0:T(8,128)S(1)}, f32[192,128]{1,0:T(8,128)S(1)}, u32[]{:S(2)}, u32[]{:S(2)}) collective-permute-start(f32[192,128]{1,0:T(8,128)S(1)} %get-tuple-element.55), channel_id=1, source_target_pairs={{0,8},{2,10},{4,12},{6,14},{8,16},{10,18},{12,20},{14,22},{16,24},... | collective-permute-start | bytes 294920 | tf_op jit(solution)/shard_map/ppermute | solution.py:535
  46.6 8.7 %collective-permute-start.13 = (f32[192,128]{1,0:T(8,128)S(1)}, f32[192,128]{1,0:T(8,128)S(1)}, u32[]{:S(2)}, u32[]{:S(2)}) collective-permute-start(f32[192,128]{1,0:T(8,128)S(1)} %get-tuple-element.56), channel_id=1, source_target_pairs={{0,16},{2,18},{4,20},{6,22},{8,24},{10,26},{12,28},{14,30},{16,0},... | collective-permute-start | bytes 294920 | tf_op jit(solution)/shard_map/ppermute | solution.py:535
  48.1 7.3 %collective-permute-start.14 = (f32[192,128]{1,0:T(8,128)S(1)}, f32[192,128]{1,0:T(8,128)S(1)}, u32[]{:S(2)}, u32[]{:S(2)}) collective-permute-start(f32[192,128]{1,0:T(8,128)S(1)} %get-tuple-element.57), channel_id=1, source_target_pairs={{0,24},{2,26},{4,28},{6,30},{8,0},{10,2},{12,4},{14,6},{16,8},{18,... | collective-permute-start | bytes 294920 | tf_op jit(solution)/shard_map/ppermute | solution.py:535
  55.4 6.2 %collective-permute-start.15 = (f32[192,128]{1,0:T(8,128)S(1)}, f32[192,128]{1,0:T(8,128)S(1)}, u32[]{:S(2)}, u32[]{:S(2)}) collective-permute-start(f32[192,128]{1,0:T(8,128)S(1)} %pick.3.rest_0_), channel_id=1, source_target_pairs={{0,1},{1,0},{2,3},{3,2},{4,5},{5,4},{6,7},{7,6},{8,9},{9,8},{10,11... | collective-permute-start | bytes 294920 | tf_op jit(solution)/shard_map/ppermute | solution.py:515
  56.5 5.1 %copy-start.9 = (bf16[2,32,192]{2,1,0:T(8,128)(2,1)S(1)}, bf16[2,32,192]{2,1,0:T(8,128)(2,1)}, u32[]{:S(2)}) copy-start(bf16[2,32,192]{2,1,0:T(8,128)(2,1)} %constant.22.clone.xown) | copy-start | bytes 73732
  (6 other events, 6.5 us)

commit v2 on v1

--- a/solution.py
+++ b/solution.py
@@ -24,6 +24,9 @@
 VMEM = pl.BlockSpec(memory_space=pltpu.VMEM)
 SMEM = pl.BlockSpec(memory_space=pltpu.SMEM)
 ANY = pl.BlockSpec(memory_space=pl.ANY)
+HBM = pl.BlockSpec(memory_space=pltpu.HBM)
+CHUNK = 8
+COVER = 10**10
 LIMIT = 12 * 1024 * 1024
 
 
@@ -46,6 +49,16 @@
         if count % n == 0 and n * n <= count:
             best = n
     return best
+
+
+def partner(place, step, count):
+    if count & (count - 1) == 0:
+        return place ^ step
+    return (place + step) % count
+
+
+def giver(place, step, count):
+    return partner(place, step if count & (count - 1) == 0 else count - step, count)
 
 
 def tall_split(data):
@@ -152,16 +165,14 @@
     return ref[r * full : (r + 1) * full, :]
 
 
-def call(kernel, out_shape, in_specs, scratch=(), flops=0, moved=0, name=None, out_specs=None):
-    if out_specs is None:
-        out_specs = [VMEM] * len(out_shape)
+def call(kernel, out_shape, in_specs, scratch=(), flops=0, moved=0, name=None, limit=LIMIT):
     return pl.pallas_call(
         kernel,
         out_shape=out_shape,
         in_specs=in_specs,
-        out_specs=out_specs,
+        out_specs=[VMEM] * len(out_shape),
         scratch_shapes=list(scratch),
-        compiler_params=pltpu.CompilerParams(vmem_limit_bytes=LIMIT),
+        compiler_params=pltpu.CompilerParams(vmem_limit_bytes=limit),
         cost_estimate=pl.CostEstimate(flops=flops, bytes_accessed=moved, transcendentals=0),
         name=name,
     )
@@ -171,16 +182,34 @@
     return jax.ShapeDtypeStruct(dims, dtype)
 
 
-def strip_kernel(extent, below, above, now, consts, packet, rows):
+def load_chunks(source, held, sems):
+    copies = []
+    for i in range(held.shape[0] // CHUNK):
+        span = pl.ds(i * CHUNK, CHUNK)
+        copies.append(pltpu.make_async_copy(source.at[span], held.at[span], sems.at[i]))
+        copies[-1].start()
+    return copies
+
+
+def strip_kernel(extent, below, above, now, packet, rows, held, sems):
     slab, zcap, width = now.shape
-    table = face_rows(consts[0:1, :], consts[1:2, :], (zcap, width), extent[0])
+    copies = load_chunks(now, held, sems)
+    at = lax.broadcasted_iota(jnp.int32, (1, width), 1)
+    far_face = at >= FACE
+    near = jnp.where(far_face, ROWS - 1 - at, at)
+    near = jnp.where(at < ROWS, near, 0).astype(F32)
+    table = face_rows(near, far_face.astype(F32), (zcap, width), extent[0])
     rows[...] = table
-    for r in range(ROWS):
-        weight = jnp.broadcast_to(table[:, r : r + 1], (zcap, width))
-        packet[r * slab : (r + 1) * slab, :] = jnp.sum(now[...] * weight[None], axis=1)
     at = lax.broadcasted_iota(jnp.int32, (HEAD, width), 0)
     names = jnp.where(at < HEAD // 2, above[0], below[0])
     packet[ROWS * slab :, :] = names.astype(F32)
+    weights = [jnp.broadcast_to(table[:, r : r + 1], (zcap, width)) for r in range(ROWS)]
+    for i, copy in enumerate(copies):
+        copy.wait()
+        part = held[i * CHUNK : (i + 1) * CHUNK]
+        for r in range(ROWS):
+            span = slice(r * slab + i * CHUNK, r * slab + (i + 1) * CHUNK)
+            packet[span, :] = jnp.sum(part * weights[r][None], axis=1)
 
 
 def lane_series(consts, first, shape, extent):
@@ -200,10 +229,12 @@
 
 
 def ahead_kernel(
-    extent, own, now, prev, rows, consts, strip, zstack, estack, hstack, coefs, *, full
+    extent, own, now_far, prev_far, rows, consts, strip, zstack, estack, hstack, coefs,
+    now, prev, sems, *, full,
 ):
     slab, zcap, width = now.shape
     ext = extent[0]
+    copies = zip(load_chunks(now_far, now, sems.at[0]), load_chunks(prev_far, prev, sems.at[1]))
     kk = lax.broadcasted_iota(jnp.int32, (zcap, zcap), 1)
     zz = lax.broadcasted_iota(jnp.int32, (zcap, zcap), 0)
     lenf = jnp.full((zcap, zcap), ext.astype(F32))
@@ -224,22 +255,17 @@
     keep = lax.broadcasted_iota(jnp.int32, shape, 0) < ext
     square = plane_square(shape, ext)
     weights = [jnp.broadcast_to(rows[:, r : r + 1], shape) for r in range(ROWS)]
-    group = min(4, slab)
-
-    def body(i, _):
-        for half in range(group):
-            kx = group * i + half
+    for i, pair in enumerate(copies):
+        for copy in pair:
+            copy.wait()
+        for kx in range(i * CHUNK, (i + 1) * CHUNK):
             local = square + x_square(own[0] * slab + kx, full)
             twice = 2.0 - local * gain_of(local)
-            ahead = twice * now[kx] - prev[kx]
-            ahead = jnp.where(keep, ahead, 0.0)
+            ahead = jnp.where(keep, twice * now[kx] - prev[kx], 0.0)
             for r in range(ROWS):
-                strip[pl.ds(r * slab + kx, 1), :] = jnp.sum(
+                strip[r * slab + kx : r * slab + kx + 1, :] = jnp.sum(
                     ahead * weights[r], axis=0, keepdims=True
                 )
-        return 0
-
-    lax.fori_loop(0, slab // group, body, 0)
 
 
 def relation_kernel(
@@ -292,13 +318,13 @@
         force[r * full : (r + 1) * full, :] = value - plane(near, r)
 
 
-def choose_kernel(group, *refs, width):
+def choose_kernel(group, after, *refs, width):
     held, out = refs[:width], refs[width:]
     rows = out[0].shape[0]
     half = rows // 2
     h, l = group[0] // width, lax.rem(group[0], width)
     for k in range(len(out)):
-        dest = (lax.rem(h + k, len(out)) * width + l).astype(F32)
+        dest = (partner(h, k, len(out)) * width + l).astype(F32)
         for f in range(2):
             lo, hi = f * half, (f + 1) * half
             row = rows + (0 if f == 1 else HEAD // 2)
@@ -316,7 +342,7 @@
         lo = half if f == 0 else 0
         value = got[0][lo : lo + half, :]
         for k in range(1, tall):
-            here = jnp.maximum(nbr[0], 0) // width == lax.rem(h + tall - k, tall)
+            here = jnp.maximum(nbr[0], 0) // width == giver(h, k, tall)
             value = jnp.where(here, got[k][lo : lo + half, :], value)
         out[f * half : (f + 1) * half, :] = value
 
@@ -518,20 +544,24 @@
     def spread(packet):
         held = [packet]
         for k in range(1, inner):
-            to = [(i, i // inner * inner + (i + k) % inner) for i in range(count)]
+            to = [(i, i // inner * inner + partner(i % inner, k, inner)) for i in range(count)]
             held.append(lax.ppermute(packet, "dom", to))
+        return held
+
+    def choose(held, after):
         return call(
             functools.partial(choose_kernel, width=inner),
             [shape_of(size, width)] * tall,
-            [SMEM] + [VMEM] * inner,
+            [SMEM, ANY] + [VMEM] * inner,
+            flops=COVER,
             moved=8 * size * width * 4,
             name="choose",
-        )(group, *held)
+        )(group, after, *held)
 
     def deliver(chosen):
         got = [chosen[0]]
         for k in range(1, tall):
-            to = [(i, (i + k * inner) % count) for i in range(count)]
+            to = [(i, partner(i // inner, k, tall) * inner + i % inner) for i in range(count)]
             got.append(lax.ppermute(chosen[k], "dom", to))
         picked = call(
             functools.partial(pick_kernel, tall=tall, width=inner),
@@ -545,12 +575,16 @@
     packet, rows = call(
         strip_kernel,
         [shape_of(size + HEAD, width), shape_of(zcap, width)],
-        [SMEM] * 3 + [VMEM] * 2,
+        [SMEM] * 3 + [HBM],
+        scratch=[
+            pltpu.VMEM((slab, zcap, width), F32),
+            pltpu.SemaphoreType.DMA((slab // CHUNK,)),
+        ],
         moved=big,
         name="strip",
-    )(z_extent, lower_nbr, upper_nbr, modes_now, consts)
-    chosen = spread(packet)
-    mine = swap(packet[:size])
+        limit=63 * 1024 * 1024,
+    )(z_extent, lower_nbr, upper_nbr, modes_now)
+    held = spread(packet)
 
     ahead, zstack, estack, hstack, coefs = call(
         functools.partial(ahead_kernel, full=full),
@@ -561,11 +595,18 @@
             shape_of(zcap, 3 * depth, dtype=BF16),
             shape_of(16, width),
         ],
-        [SMEM] * 2 + [VMEM] * 4,
+        [SMEM] * 2 + [HBM] * 2 + [VMEM] * 2,
+        scratch=[
+            pltpu.VMEM((slab, zcap, width), F32),
+            pltpu.VMEM((slab, zcap, width), F32),
+            pltpu.SemaphoreType.DMA((2, slab // CHUNK)),
+        ],
         flops=10**8,
         moved=2 * big,
         name="ahead",
     )(z_extent, own, modes_now, modes_prev, rows, consts)
+    chosen = choose(held, ahead)
+    mine = swap(packet[:size])
     aheads = swap(ahead)
 
     tx, uy, vx, wy, near1, mixing, _ = call(
@@ -599,7 +640,7 @@
         name="middle",
     )(own, lower_nbr, upper_nbr, near1, tx, uy, mixing, *deliver(chosen), *aheads)
 
-    chosen2 = spread(packet2)
+    chosen2 = choose(spread(packet2), packet2)
     current, onward, *free = call(
         functools.partial(between_kernel, full=full),
         [shape_of(slab, zcap, width)] * 2 + [shape_of(slab * zcap, width)] * parts,

time: 66.1 us -> 70.4 us (1.065)
  waiting for transfers between devices: 22.8 us -> 27 us
  Pallas kernels: 15.7 us -> 17.2 us
    ppermute x6, waiting for transfers between devices: 11.2 us -> 0.02 us  [spread(): held.append(lax.ppermute(packet, 'dom', to))]
    ppermute x6, waiting for transfers between devices: 5.73 us -> 13.8 us  [deliver(): got.append(lax.ppermute(chosen[k], 'dom', to))]
    ppermute x4, waiting for transfers between devices: 5.83 us -> 13.2 us  [swap(): lax.ppermute(piece, 'split', [(i, (i + k) % parts) for i in range(parts)])]
    pallas_call x1, Pallas kernels: 0.97 us -> 2.33 us  [on_device(): call(strip_kernel, [shape_of(size + HEAD, width), shape_of(zcap, width)],...]
    unnamed x26 -> x30, local copies, waits for them, and re-layouts: 3.37 us -> 3.27 us
  transfers between devices with their start and end apart: 17 -> 17, of which waited for: 10 -> 5; matrix products, arithmetic and copies ran while one was open for 0% -> 0% of each run, Pallas kernels for 8% -> 15%
where the time goes in v2:
time: 70.4 us; the launch traced here: 70.1 us
  waiting for transfers between devices  27 us (38%)
  starting transfers between devices  19.9 us (28%)
  Pallas kernels  17.2 us (24%)
  local copies, waits for them, and re-layouts  3.28 us (5%)
  between operations  2.78 us (4%)
    ppermute x6, waiting for transfers between devices, deliver(): got.append(lax.ppermute(chosen[k], 'dom', to))  13.8 us
    ppermute x4, waiting for transfers between devices, swap(): lax.ppermute(piece, 'split', [(i, (i + k) % parts) for i in range(parts)])  13.2 us
    ppermute x6, starting transfers between devices, deliver(): got.append(lax.ppermute(chosen[k], 'dom', to))  8.98 us
    pallas_call x1, Pallas kernels, on_device(): call(functools.partial(between_kernel, full=full), [shape_of(slab, zcap,...  5.23 us
    ppermute x6, starting transfers between devices, spread(): held.append(lax.ppermute(packet, 'dom', to))  5.04 us
    ppermute x4, starting transfers between devices, swap(): lax.ppermute(piece, 'split', [(i, (i + k) % parts) for i in range(parts)])  4.25 us
    pallas_call x1, Pallas kernels, on_device(): call(functools.partial(last_kernel, full=full, parts=parts), [shape_of(sl...  3.49 us
    unnamed x30, local copies, waits for them, and re-layouts  3.27 us
  transfers between devices with their start and end apart: 17, of which 5 were waited for; matrix products, arithmetic and copies ran while one was open for 0% of the time, Pallas kernels for 15%

profile of v2, /device:TPU:0, one launch (start us, length us, event | category | flops | bytes accessed | tf_op | source)
XLA Modules:
  0.0 70.1 jit_solution(9815356837557458300)
XLA Ops:
  2.6 2.3 %strip.1 = (f32[200,128]{1,0:T(8,128)}, f32[64,128]{1,0:T(8,128)}) custom-call(s32[1]{0:T(128)S(6)} %copy.16.extent, s32[1]{0:T(128)S(6)} %copy.17.below, s32[1]{0:T(128)S(6)} %copy.18.above, f32[32,64,128]{2,1,0:T(8,128)} %now.3), custom_call_target="tpu_custom_call" | custom-call | bytes 1048576 | tf_op jit(solution)/shard_map/strip/pallas_call | solution.py:575
  4.9 2.4 %collective-permute-start.2 = (f32[200,128]{1,0:T(8,128)}, f32[200,128]{1,0:T(8,128)S(1)}, u32[]{:S(2)}, u32[]{:S(2)}) collective-permute-start(f32[200,128]{1,0:T(8,128)} %get-tuple-element.36.refs_0_), channel_id=1, source_target_pairs={{0,6},{2,4},{4,2},{6,0},{8,14},{10,12},{12,10},{14,8},{16,22},{18,... | collective-permute-start | bytes 307208 | tf_op jit(solution)/shard_map/ppermute | solution.py:548
  8.0 1.2 %copy-done = f32[32,64,128]{2,1,0:T(8,128)S(1)} copy-done((f32[32,64,128]{2,1,0:T(8,128)S(1)}, f32[32,64,128]{2,1,0:T(8,128)}, u32[]{:S(2)}) %copy-start) | copy-done | bytes 1048600
  9.3 1.2 %copy-done.2 = f32[32,64,128]{2,1,0:T(8,128)S(1)} copy-done((f32[32,64,128]{2,1,0:T(8,128)S(1)}, f32[32,64,128]{2,1,0:T(8,128)}, u32[]{:S(2)}) %copy-start.2) | copy-done | bytes 1048600
  10.5 0.8 %copy-done.9 = f32[64,128]{1,0:T(8,128)S(1)} copy-done((f32[64,128]{1,0:T(8,128)S(1)}, f32[64,128]{1,0:T(8,128)}, u32[]{:S(2)}) %copy-start.9) | copy-done | bytes 32792
  11.3 2.4 %ahead.1 = (f32[192,128]{1,0:T(8,128)S(1)}, bf16[64,192]{1,0:T(8,128)(2,1)S(1)}, bf16[64,144]{1,0:T(8,128)(2,1)S(1)}, bf16[64,144]{1,0:T(8,128)(2,1)S(1)}, f32[16,128]{1,0:T(8,128)S(1)}) custom-call(s32[1]{0:T(128)S(6)} %copy.16.extent, s32[1]{0:T(128)} %bitcast.own, f32[32,64,128]{2,1,0:T(8,128)S(1)} %copy-done, f32[32,64,128]{2,1,0:T(8,128)S(1)} %copy-done.2, ...), custom_call_target="tpu_custom_call" | custom-call | flops 100000000 | bytes 2097152 | tf_op jit(solution)/shard_map/ahead/pallas_call | solution.py:589
  13.8 1.9 %collective-permute-start.4 = (f32[192,128]{1,0:T(8,128)S(1)}, f32[192,128]{1,0:T(8,128)S(1)}, u32[]{:S(2)}, u32[]{:S(2)}) collective-permute-start(f32[192,128]{1,0:T(8,128)S(1)} %get-tuple-element.42), channel_id=1, source_target_pairs={{0,8},{2,10},{4,12},{6,14},{8,0},{10,2},{12,4},{14,6},{16,24},{18,... | collective-permute-start | bytes 294920 | tf_op jit(solution)/shard_map/ppermute | solution.py:565
  15.8 2.6 %collective-permute-start.5 = (f32[192,128]{1,0:T(8,128)S(1)}, f32[192,128]{1,0:T(8,128)S(1)}, u32[]{:S(2)}, u32[]{:S(2)}) collective-permute-start(f32[192,128]{1,0:T(8,128)S(1)} %get-tuple-element.43), channel_id=1, source_target_pairs={{0,16},{2,18},{4,20},{6,22},{8,24},{10,26},{12,28},{14,30},{16,0},... | collective-permute-start | bytes 294920 | tf_op jit(solution)/shard_map/ppermute | solution.py:565
  18.4 1.8 %collective-permute-start.3 = (f32[192,128]{1,0:T(8,128)S(1)}, f32[192,128]{1,0:T(8,128)S(1)}, u32[]{:S(2)}, u32[]{:S(2)}) collective-permute-start(f32[192,128]{1,0:T(8,128)S(1)} %slice.3.rest_0_), channel_id=1, source_target_pairs={{0,1},{1,0},{2,3},{3,2},{4,5},{5,4},{6,7},{7,6},{8,9},{9,8},{10,11... | collective-permute-start | bytes 294920 | tf_op jit(solution)/shard_map/ppermute | solution.py:541
  20.5 5.9 %collective-permute-done.5.refs_2_ = f32[192,128]{1,0:T(8,128)S(1)} collective-permute-done((f32[192,128]{1,0:T(8,128)S(1)}, f32[192,128]{1,0:T(8,128)S(1)}, u32[]{:S(2)}, u32[]{:S(2)}) %collective-permute-start.5) | collective-permute-done | bytes 98336 | tf_op jit(solution)/shard_map/ppermute | solution.py:565
  26.4 1.6 %collective-permute-start.7 = (f32[192,128]{1,0:T(8,128)S(1)}, f32[192,128]{1,0:T(8,128)S(1)}, u32[]{:S(2)}, u32[]{:S(2)}) collective-permute-start(f32[192,128]{1,0:T(8,128)S(1)} %pick.2.rest_0_), channel_id=1, source_target_pairs={{0,1},{1,0},{2,3},{3,2},{4,5},{5,4},{6,7},{7,6},{8,9},{9,8},{10,11... | collective-permute-start | bytes 294920 | tf_op jit(solution)/shard_map/ppermute | solution.py:541
  28.1 2.1 %relation.1 = (f32[2,64,64]{2,1,0:T(8,128)S(1)}, f32[2,128,128]{2,1,0:T(8,128)S(1)}, f32[2,64,64]{2,1,0:T(8,128)S(1)}, f32[2,128,128]{2,1,0:T(8,128)S(1)}, f32[3...) custom-call(s32[1]{0:T(128)S(6)} %copy.17.below, s32[1]{0:T(128)S(6)} %copy.18.above, ...), custom_call_target="tpu_custom_call" | custom-call | flops 100000000 | bytes 2097152 | tf_op jit(solution)/shard_map/relation/pallas_call | solution.py:612
  30.2 1.0 %collective-permute-done.7.rest_1_ = f32[192,128]{1,0:T(8,128)S(1)} collective-permute-done((f32[192,128]{1,0:T(8,128)S(1)}, f32[192,128]{1,0:T(8,128)S(1)}, u32[]{:S(2)}, u32[]{:S(2)}) %collective-permute-start.7) | collective-permute-done | bytes 98336 | tf_op jit(solution)/shard_map/ppermute | solution.py:541
  31.1 0.7 %middle.1 = (f32[200,128]{1,0:T(8,128)S(1)}, f32[384,128]{1,0:T(8,128)S(1)}, f32[384,128]{1,0:T(8,128)S(1)}) custom-call(s32[1]{0:T(128)} %bitcast.own, s32[1]{0:T(128)S(6)} %copy.17.below, s32[1]{0:T(128)S(6)} %copy.18.above, f32[384,128]{1,0:T(8,128)S(1)} %get-tuple-element.38.near, f32[2,64,64]{2,1,0:T(8,128)S(1)} %get-tuple-element.39.tx, ...), custom_call_target="tpu_custom_call" | custom-call | flops 100000000 | bytes 2097152 | tf_op jit(solution)/shard_map/middle/pallas_call | solution.py:629
  31.9 1.6 %collective-permute-start.10 = (f32[200,128]{1,0:T(8,128)S(1)}, f32[200,128]{1,0:T(8,128)S(1)}, u32[]{:S(2)}, u32[]{:S(2)}) collective-permute-start(f32[200,128]{1,0:T(8,128)S(1)} %get-tuple-element.53.after.refs_0_), channel_id=1, source_target_pairs={{0,4},{2,6},{4,0},{6,2},{8,12},{10,14},{12,8},{14,10},{16,20},{18,... | collective-permute-start | bytes 307208 | tf_op jit(solution)/shard_map/ppermute | solution.py:548
  33.8 5.2 %between.1 = (f32[32,64,128]{2,1,0:T(8,128)}, f32[32,64,128]{2,1,0:T(8,128)S(1)}, f32[2048,128]{1,0:T(8,128)S(1)}, f32[2048,128]{1,0:T(8,128)S(1)}) custom-call(s32[1]{0:T(128)S(6)} %copy.16.extent, s32[1]{0:T(128)} %bitcast.own, f32[32,64,128]{2,1,0:T(8,128)S(1)} %copy-done.1, f32[32,64,128]{2,1,0:T(8,128)S(1)} %copy-done.3, ...), custom_call_target="tpu_custom_call" | custom-call | flops 1000000000 | bytes 6291456 | tf_op jit(solution)/shard_map/between/pallas_call | solution.py:644
  39.1 1.6 %collective-permute-start.16 = (f32[2048,128]{1,0:T(8,128)S(1)}, f32[2048,128]{1,0:T(8,128)S(1)}, u32[]{:S(2)}, u32[]{:S(2)}) collective-permute-start(f32[2048,128]{1,0:T(8,128)S(1)} %get-tuple-element.59), channel_id=1, source_target_pairs={{0,1},{1,0},{2,3},{3,2},{4,5},{5,4},{6,7},{7,6},{8,9},{9,8},{10,11... | collective-permute-start | bytes 3145736 | tf_op jit(solution)/shard_map/ppermute | solution.py:654
  40.8 1.8 %collective-permute-start.12 = (f32[192,128]{1,0:T(8,128)S(1)}, f32[192,128]{1,0:T(8,128)S(1)}, u32[]{:S(2)}, u32[]{:S(2)}) collective-permute-start(f32[192,128]{1,0:T(8,128)S(1)} %get-tuple-element.55), channel_id=1, source_target_pairs={{0,8},{2,10},{4,12},{6,14},{8,0},{10,2},{12,4},{14,6},{16,24},{18,... | collective-permute-start | bytes 294920 | tf_op jit(solution)/shard_map/ppermute | solution.py:565
  42.6 1.4 %collective-permute-start.13 = (f32[192,128]{1,0:T(8,128)S(1)}, f32[192,128]{1,0:T(8,128)S(1)}, u32[]{:S(2)}, u32[]{:S(2)}) collective-permute-start(f32[192,128]{1,0:T(8,128)S(1)} %get-tuple-element.56), channel_id=1, source_target_pairs={{0,16},{2,18},{4,20},{6,22},{8,24},{10,26},{12,28},{14,30},{16,0},... | collective-permute-start | bytes 294920 | tf_op jit(solution)/shard_map/ppermute | solution.py:565
  44.0 1.2 %collective-permute-start.14 = (f32[192,128]{1,0:T(8,128)S(1)}, f32[192,128]{1,0:T(8,128)S(1)}, u32[]{:S(2)}, u32[]{:S(2)}) collective-permute-start(f32[192,128]{1,0:T(8,128)S(1)} %get-tuple-element.57), channel_id=1, source_target_pairs={{0,24},{2,26},{4,28},{6,30},{8,16},{10,18},{12,20},{14,22},{16,8},... | collective-permute-start | bytes 294920 | tf_op jit(solution)/shard_map/ppermute | solution.py:565
  45.7 7.4 %collective-permute-done.13.refs_2_ = f32[192,128]{1,0:T(8,128)S(1)} collective-permute-done((f32[192,128]{1,0:T(8,128)S(1)}, f32[192,128]{1,0:T(8,128)S(1)}, u32[]{:S(2)}, u32[]{:S(2)}) %collective-permute-start.13) | collective-permute-done | bytes 98336 | tf_op jit(solution)/shard_map/ppermute | solution.py:565
  53.7 0.7 near.1
  54.4 12.2 %collective-permute-done.15.rest_1_ = f32[192,128]{1,0:T(8,128)S(1)} collective-permute-done((f32[192,128]{1,0:T(8,128)S(1)}, f32[192,128]{1,0:T(8,128)S(1)}, u32[]{:S(2)}, u32[]{:S(2)}) %collective-permute-start.15) | collective-permute-done | bytes 98336 | tf_op jit(solution)/shard_map/ppermute | solution.py:541
  66.6 3.5 %last.1 = (f32[32,64,128]{2,1,0:T(8,128)}, f32[2048,128]{1,0:T(8,128)}) custom-call(s32[1]{0:T(128)} %bitcast.own, f32[384,128]{1,0:T(8,128)S(1)} %near.1, f32[2,64,64]{2,1,0:T(8,128)S(1)} %get-tuple-element.39.tx, f32[2,128,128]{2,1,0:T(8,128)S(1)} %get-tuple-element.40.uy, f32[32,64,128]{2,1,0:T(8,128)S(1)} %get-tuple-element.50.onward, ...), custom_call_target="tpu_custom_call" | custom-call | flops 1000000000 | bytes 6291456 | tf_op jit(solution)/shard_map/last/pallas_call | solution.py:666
  (52 shorter events, 2.7 us)
Async XLA Ops:
  2.6 5.5 %copy-start.11 = (f32[40,128]{1,0:T(8,128)S(1)}, f32[40,128]{1,0:T(8,128)}, u32[]{:S(2)}) copy-start(f32[40,128]{1,0:T(8,128)} %constant.20.clone.consts) | copy-start | bytes 61444
  4.9 8.8 %collective-permute-start.2 = (f32[200,128]{1,0:T(8,128)}, f32[200,128]{1,0:T(8,128)S(1)}, u32[]{:S(2)}, u32[]{:S(2)}) collective-permute-start(f32[200,128]{1,0:T(8,128)} %get-tuple-element.36.refs_0_), channel_id=1, source_target_pairs={{0,6},{2,4},{4,2},{6,0},{8,14},{10,12},{12,10},{14,8},{16,22},{18,... | collective-permute-start | bytes 307208 | tf_op jit(solution)/shard_map/ppermute | solution.py:548
  7.4 6.3 %collective-permute-start.1 = (f32[200,128]{1,0:T(8,128)}, f32[200,128]{1,0:T(8,128)S(1)}, u32[]{:S(2)}, u32[]{:S(2)}) collective-permute-start(f32[200,128]{1,0:T(8,128)} %get-tuple-element.36.refs_0_), channel_id=1, source_target_pairs={{0,4},{2,6},{4,0},{6,2},{8,12},{10,14},{12,8},{14,10},{16,20},{18,... | collective-permute-start | bytes 307208 | tf_op jit(solution)/shard_map/ppermute | solution.py:548
  8.0 5.7 %collective-permute-start = (f32[200,128]{1,0:T(8,128)}, f32[200,128]{1,0:T(8,128)S(1)}, u32[]{:S(2)}, u32[]{:S(2)}) collective-permute-start(f32[200,128]{1,0:T(8,128)} %get-tuple-element.36.refs_0_), channel_id=1, source_target_pairs={{0,2},{2,0},{4,6},{6,4},{8,10},{10,8},{12,14},{14,12},{16,18},{18,... | collective-permute-start | bytes 307208 | tf_op jit(solution)/shard_map/ppermute | solution.py:548
  13.7 14.3 %copy-start.6 = (f32[256,64]{1,0:T(8,128)S(1)}, f32[256,64]{1,0:T(8,128)}, u32[]{:S(2)}) copy-start(f32[256,64]{1,0:T(8,128)} %constant.24.clone.xtall) | copy-start | bytes 196612
  13.8 6.6 %collective-permute-start.4 = (f32[192,128]{1,0:T(8,128)S(1)}, f32[192,128]{1,0:T(8,128)S(1)}, u32[]{:S(2)}, u32[]{:S(2)}) collective-permute-start(f32[192,128]{1,0:T(8,128)S(1)} %get-tuple-element.42), channel_id=1, source_target_pairs={{0,8},{2,10},{4,12},{6,14},{8,0},{10,2},{12,4},{14,6},{16,24},{18,... | collective-permute-start | bytes 294920 | tf_op jit(solution)/shard_map/ppermute | solution.py:565
  15.8 10.6 %collective-permute-start.5 = (f32[192,128]{1,0:T(8,128)S(1)}, f32[192,128]{1,0:T(8,128)S(1)}, u32[]{:S(2)}, u32[]{:S(2)}) collective-permute-start(f32[192,128]{1,0:T(8,128)S(1)} %get-tuple-element.43), channel_id=1, source_target_pairs={{0,16},{2,18},{4,20},{6,22},{8,24},{10,26},{12,28},{14,30},{16,0},... | collective-permute-start | bytes 294920 | tf_op jit(solution)/shard_map/ppermute | solution.py:565
  18.4 8.0 %collective-permute-start.6 = (f32[192,128]{1,0:T(8,128)S(1)}, f32[192,128]{1,0:T(8,128)S(1)}, u32[]{:S(2)}, u32[]{:S(2)}) collective-permute-start(f32[192,128]{1,0:T(8,128)S(1)} %get-tuple-element.44), channel_id=1, source_target_pairs={{0,24},{2,26},{4,28},{6,30},{8,16},{10,18},{12,20},{14,22},{16,8},... | collective-permute-start | bytes 294920 | tf_op jit(solution)/shard_map/ppermute | solution.py:565
  18.4 9.7 %copy-start.4 = (f32[512,128]{1,0:T(8,128)S(1)}, f32[512,128]{1,0:T(8,128)}, u32[]{:S(2)}) copy-start(f32[512,128]{1,0:T(8,128)} %constant.25.clone.ytall) | copy-start | bytes 786436
  18.4 9.7 %collective-permute-start.3 = (f32[192,128]{1,0:T(8,128)S(1)}, f32[192,128]{1,0:T(8,128)S(1)}, u32[]{:S(2)}, u32[]{:S(2)}) collective-permute-start(f32[192,128]{1,0:T(8,128)S(1)} %slice.3.rest_0_), channel_id=1, source_target_pairs={{0,1},{1,0},{2,3},{3,2},{4,5},{5,4},{6,7},{7,6},{8,9},{9,8},{10,11... | collective-permute-start | bytes 294920 | tf_op jit(solution)/shard_map/ppermute | solution.py:541
  20.2 10.0 %collective-permute-start.8 = (f32[192,128]{1,0:T(8,128)S(1)}, f32[192,128]{1,0:T(8,128)S(1)}, u32[]{:S(2)}, u32[]{:S(2)}) collective-permute-start(f32[192,128]{1,0:T(8,128)S(1)} %get-tuple-element.35.after.rest_2_), channel_id=1, source_target_pairs={{0,1},{1,0},{2,3},{3,2},{4,5},{5,4},{6,7},{7,6},{8,9},{9,8},{10,11... | collective-permute-start | bytes 294920 | tf_op jit(solution)/shard_map/ppermute | solution.py:541
  26.4 7.4 %copy-start.5 = (bf16[256,256]{1,0:T(8,128)(2,1)S(1)}, bf16[256,256]{1,0:T(8,128)(2,1)}, u32[]{:S(2)}) copy-start(bf16[256,256]{1,0:T(8,128)(2,1)} %constant.21.clone.ystack) | copy-start | bytes 393220
  26.4 4.7 %collective-permute-start.7 = (f32[192,128]{1,0:T(8,128)S(1)}, f32[192,128]{1,0:T(8,128)S(1)}, u32[]{:S(2)}, u32[]{:S(2)}) collective-permute-start(f32[192,128]{1,0:T(8,128)S(1)} %pick.2.rest_0_), channel_id=1, source_target_pairs={{0,1},{1,0},{2,3},{3,2},{4,5},{5,4},{6,7},{7,6},{8,9},{9,8},{10,11... | collective-permute-start | bytes 294920 | tf_op jit(solution)/shard_map/ppermute | solution.py:541
  28.1 5.7 %copy-start.1 = (f32[32,64,128]{2,1,0:T(8,128)S(1)}, f32[32,64,128]{2,1,0:T(8,128)}, u32[]{:S(2)}) copy-start(f32[32,64,128]{2,1,0:T(8,128)} %now.3) | copy-start | bytes 3145732
  28.1 5.7 %copy-start.3 = (f32[32,64,128]{2,1,0:T(8,128)S(1)}, f32[32,64,128]{2,1,0:T(8,128)}, u32[]{:S(2)}) copy-start(f32[32,64,128]{2,1,0:T(8,128)} %prev.1) | copy-start | bytes 3145732
  31.9 8.8 %collective-permute-start.11 = (f32[200,128]{1,0:T(8,128)S(1)}, f32[200,128]{1,0:T(8,128)S(1)}, u32[]{:S(2)}, u32[]{:S(2)}) collective-permute-start(f32[200,128]{1,0:T(8,128)S(1)} %get-tuple-element.53.after.refs_0_), channel_id=1, source_target_pairs={{0,6},{2,4},{4,2},{6,0},{8,14},{10,12},{12,10},{14,8},{16,22},{18,... | collective-permute-start | bytes 307208 | tf_op jit(solution)/shard_map/ppermute | solution.py:548
  31.9 8.7 %collective-permute-start.10 = (f32[200,128]{1,0:T(8,128)S(1)}, f32[200,128]{1,0:T(8,128)S(1)}, u32[]{:S(2)}, u32[]{:S(2)}) collective-permute-start(f32[200,128]{1,0:T(8,128)S(1)} %get-tuple-element.53.after.refs_0_), channel_id=1, source_target_pairs={{0,4},{2,6},{4,0},{6,2},{8,12},{10,14},{12,8},{14,10},{16,20},{18,... | collective-permute-start | bytes 307208 | tf_op jit(solution)/shard_map/ppermute | solution.py:548
  33.6 7.1 %collective-permute-start.9 = (f32[200,128]{1,0:T(8,128)S(1)}, f32[200,128]{1,0:T(8,128)S(1)}, u32[]{:S(2)}, u32[]{:S(2)}) collective-permute-start(f32[200,128]{1,0:T(8,128)S(1)} %get-tuple-element.53.after.refs_0_), channel_id=1, source_target_pairs={{0,2},{2,0},{4,6},{6,4},{8,10},{10,8},{12,14},{14,12},{16,18},{18,... | collective-permute-start | bytes 307208 | tf_op jit(solution)/shard_map/ppermute | solution.py:548
  39.1 27.5 %collective-permute-start.16 = (f32[2048,128]{1,0:T(8,128)S(1)}, f32[2048,128]{1,0:T(8,128)S(1)}, u32[]{:S(2)}, u32[]{:S(2)}) collective-permute-start(f32[2048,128]{1,0:T(8,128)S(1)} %get-tuple-element.59), channel_id=1, source_target_pairs={{0,1},{1,0},{2,3},{3,2},{4,5},{5,4},{6,7},{7,6},{8,9},{9,8},{10,11... | collective-permute-start | bytes 3145736 | tf_op jit(solution)/shard_map/ppermute | solution.py:654
  40.8 5.0 %collective-permute-start.12 = (f32[192,128]{1,0:T(8,128)S(1)}, f32[192,128]{1,0:T(8,128)S(1)}, u32[]{:S(2)}, u32[]{:S(2)}) collective-permute-start(f32[192,128]{1,0:T(8,128)S(1)} %get-tuple-element.55), channel_id=1, source_target_pairs={{0,8},{2,10},{4,12},{6,14},{8,0},{10,2},{12,4},{14,6},{16,24},{18,... | collective-permute-start | bytes 294920 | tf_op jit(solution)/shard_map/ppermute | solution.py:565
  42.6 10.5 %collective-permute-start.13 = (f32[192,128]{1,0:T(8,128)S(1)}, f32[192,128]{1,0:T(8,128)S(1)}, u32[]{:S(2)}, u32[]{:S(2)}) collective-permute-start(f32[192,128]{1,0:T(8,128)S(1)} %get-tuple-element.56), channel_id=1, source_target_pairs={{0,16},{2,18},{4,20},{6,22},{8,24},{10,26},{12,28},{14,30},{16,0},... | collective-permute-start | bytes 294920 | tf_op jit(solution)/shard_map/ppermute | solution.py:565
  44.0 9.1 %collective-permute-start.14 = (f32[192,128]{1,0:T(8,128)S(1)}, f32[192,128]{1,0:T(8,128)S(1)}, u32[]{:S(2)}, u32[]{:S(2)}) collective-permute-start(f32[192,128]{1,0:T(8,128)S(1)} %get-tuple-element.57), channel_id=1, source_target_pairs={{0,24},{2,26},{4,28},{6,30},{8,16},{10,18},{12,20},{14,22},{16,8},... | collective-permute-start | bytes 294920 | tf_op jit(solution)/shard_map/ppermute | solution.py:565
  53.1 13.4 %collective-permute-start.15 = (f32[192,128]{1,0:T(8,128)S(1)}, f32[192,128]{1,0:T(8,128)S(1)}, u32[]{:S(2)}, u32[]{:S(2)}) collective-permute-start(f32[192,128]{1,0:T(8,128)S(1)} %pick.3.rest_0_), channel_id=1, source_target_pairs={{0,1},{1,0},{2,3},{3,2},{4,5},{5,4},{6,7},{7,6},{8,9},{9,8},{10,11... | collective-permute-start | bytes 294920 | tf_op jit(solution)/shard_map/ppermute | solution.py:541
  53.7 12.9 %copy-start.8 = (bf16[2,32,192]{2,1,0:T(8,128)(2,1)S(1)}, bf16[2,32,192]{2,1,0:T(8,128)(2,1)}, u32[]{:S(2)}) copy-start(bf16[2,32,192]{2,1,0:T(8,128)(2,1)} %constant.22.clone.xown) | copy-start | bytes 73732
  (8 other events, 14.3 us)

commit v3 on v2

--- a/solution.py
+++ b/solution.py
@@ -18,7 +18,10 @@
 ROWS = 2 * FACE
 HEAD = 8
 SERIES = [(-1) ** n * 2.0 / math.factorial(2 * n + 2) for n in range(10)]
-TERMS = 7
+TERMS = 6
+DOUBLE = [(-1) ** (n + 1) * (4 - 2.0 * 4.0 ** (n + 1)) / math.factorial(2 * n + 2) for n in range(14)]
+DOUBLE_TERMS = 9
+WIDE = 63 * 1024 * 1024
 BASE = (COURANT * math.pi) ** 2
 PAIRS = [(r, q) for r in range(ROWS) for q in range(r, ROWS)]
 VMEM = pl.BlockSpec(memory_space=pltpu.VMEM)
@@ -212,12 +215,12 @@
             packet[span, :] = jnp.sum(part * weights[r][None], axis=1)
 
 
-def lane_series(consts, first, shape, extent):
+def lane_series(consts, first, count, shape, extent):
     kz = lax.broadcasted_iota(jnp.int32, shape, 0)
     frac = kz.astype(F32) / jnp.full(shape, extent.astype(F32))
     middle = jnp.where(kz < extent, BASE * frac * frac, 0.0) + BASE
     total = jnp.zeros(shape, F32)
-    for j in reversed(range(len(SERIES))):
+    for j in reversed(range(count)):
         total = total * middle + consts[first + j : first + j + 1, :]
     return total
 
@@ -229,28 +232,17 @@
 
 
 def ahead_kernel(
-    extent, own, now_far, prev_far, rows, consts, strip, zstack, estack, hstack, coefs,
-    now, prev, sems, *, full,
+    extent, own, now_far, prev_far, rows, consts, strip, coefs, now, prev, sems, *, full
 ):
     slab, zcap, width = now.shape
     ext = extent[0]
     copies = zip(load_chunks(now_far, now, sems.at[0]), load_chunks(prev_far, prev, sems.at[1]))
-    kk = lax.broadcasted_iota(jnp.int32, (zcap, zcap), 1)
-    zz = lax.broadcasted_iota(jnp.int32, (zcap, zcap), 0)
-    lenf = jnp.full((zcap, zcap), ext.astype(F32))
-    ztable = scale_of(kk, lenf) * cosine_of(kk.astype(F32), 2.0 * zz.astype(F32) + 1.0, lenf)
-    ztable = jnp.where((kk < ext) & (zz < ext), ztable, 0.0)
-    zstack[...] = stack_lanes(ztable, zcap)
 
     shape = (zcap, width)
     pairs = face_rows(consts[2:3, :], consts[3:4, :], shape, ext)
     pairs = pairs * face_rows(consts[4:5, :], consts[5:6, :], shape, ext)
-    coefs[...] = exact_dot(lane_series(consts, 8, shape, ext).T[: coefs.shape[0]], pairs)
-    terms = face_rows(consts[6:7, :], consts[7:8, :], shape, ext)
-    terms = terms * lane_series(consts, 24, shape, ext)
-    depth = estack.shape[1] // 3
-    estack[...] = stack_lanes(terms, depth)
-    hstack[...] = stack_lanes(exact_dot(ztable, terms), depth)
+    series = lane_series(consts, 8, len(SERIES), shape, ext)
+    coefs[...] = exact_dot(series.T[: coefs.shape[0]], pairs)
 
     keep = lax.broadcasted_iota(jnp.int32, shape, 0) < ext
     square = plane_square(shape, ext)
@@ -334,7 +326,7 @@
             out[k][lo:hi, :] = chosen
 
 
-def pick_kernel(group, below, above, *refs, tall, width):
+def pick_kernel(group, below, above, after, *refs, tall, width):
     got, out = refs[:-1], refs[-1]
     half = out.shape[0] // 2
     h = group[0] // width
@@ -347,7 +339,7 @@
         out[f * half : (f + 1) * half, :] = value
 
 
-def middle_kernel(own, below, above, near, tx, uy, mixing, *rest, parts):
+def middle_kernel(own, below, above, after, near, tx, uy, mixing, *rest, parts):
     far, ahead = rest[:parts], rest[parts : 2 * parts]
     packet, force, strip, spare = rest[2 * parts :]
     gather_kx(spare, far, own[0])
@@ -372,37 +364,42 @@
     near_planes(strip, vx, wy, near)
 
 
-def between_kernel(
-    extent, own, now, prev, force, rows, zstack, ystack, xparts, current, onward, *rest, full,
+def unforced_kernel(
+    extent, own, after, now, prev, consts, ystack, xparts, estack, hstack, gstack, *rest, full
 ):
     free, field = rest[:-1], rest[-1]
     slab, zcap, width = now.shape
     shape = (zcap, width)
-    keep = lax.broadcasted_iota(jnp.int32, shape, 0) < extent[0]
-    square = plane_square(shape, extent[0])
-    weights = [jnp.broadcast_to(rows[:, r : r + 1], shape) for r in range(ROWS)]
+    ext = extent[0]
+    kk = lax.broadcasted_iota(jnp.int32, (zcap, zcap), 1)
+    zz = lax.broadcasted_iota(jnp.int32, (zcap, zcap), 0)
+    lenf = jnp.full((zcap, zcap), ext.astype(F32))
+    ztable = scale_of(kk, lenf) * cosine_of(kk.astype(F32), 2.0 * zz.astype(F32) + 1.0, lenf)
+    ztable = jnp.where((kk < ext) & (zz < ext), ztable, 0.0)
+    zstack = stack_lanes(ztable, zcap)
+    face = face_rows(consts[6:7, :], consts[7:8, :], shape, ext)
+    terms = face * lane_series(consts, 24, len(SERIES), shape, ext)
+    depth = estack.shape[1] // 3
+    estack[...] = stack_lanes(terms, depth)
+    hstack[...] = stack_lanes(exact_dot(ztable, terms), depth)
+    terms = face * lane_series(consts, 40, len(DOUBLE), shape, ext)
+    gstack[...] = stack_lanes(exact_dot(ztable, terms), gstack.shape[1] // 3)
+
+    keep = lax.broadcasted_iota(jnp.int32, shape, 0) < ext
+    square = plane_square(shape, ext)
     group = min(4, slab)
 
     def body(i, _):
         planes = []
         for half in range(group):
             at = group * i + half
-            kx = own[0] * slab + at
-            local = square + x_square(kx, full)
-            gain = gain_of(local)
-            total = None
-            for r in range(ROWS):
-                term = weights[r] * force[pl.ds(r * full + kx, 1), :]
-                total = term if total is None else total + term
-            twice = 2.0 - local * gain
-            first = jnp.where(keep, now[at], 0.0)
-            value = twice * first - jnp.where(keep, prev[at], 0.0) + gain * total
-            current[at] = value
-            later = twice * value - first
-            onward[at] = later
-            planes.append(later)
+            local = square + x_square(own[0] * slab + at, full)
+            twice = 2.0 - local * gain_of(local)
+            first = now[at]
+            later = twice * (twice * first - prev[at]) - first
+            planes.append(jnp.where(keep, later, 0.0))
         for j in range(0, group, 2):
-            wide = dot(zstack[...], tall_split(jnp.concatenate(planes[j : j + 2], axis=1)))
+            wide = dot(zstack, tall_split(jnp.concatenate(planes[j : j + 2], axis=1)))
             for half in range(2):
                 at = pl.multiple_of((group * i + j + half) * zcap, zcap)
                 field[pl.ds(at, zcap), :] = wide[:, half * width : (half + 1) * width]
@@ -425,52 +422,93 @@
                 ]
 
 
-def last_kernel(own, near, tx, uy, onward, estack, hstack, ystack, xown, *rest, full, parts):
-    far, given = rest[:parts], rest[parts : 2 * parts]
-    modes, pressure, spare, force, terms, turned = rest[2 * parts :]
-    slab, zcap, width = onward.shape
-    depth = estack.shape[1] // 3
-    used = TERMS * ROWS
-    gather_kx(spare, far, own[0])
-    force_planes(spare, near, tx, uy, force)
+def between_kernel(extent, own, now, prev, force, rows, current, onward, *, full):
+    slab, zcap, width = now.shape
+    shape = (zcap, width)
+    keep = lax.broadcasted_iota(jnp.int32, shape, 0) < extent[0]
+    square = plane_square(shape, extent[0])
+    weights = [jnp.broadcast_to(rows[:, r : r + 1], shape) for r in range(ROWS)]
+    group = min(4, slab)
+
+    def body(i, _):
+        for half in range(group):
+            at = group * i + half
+            kx = own[0] * slab + at
+            local = square + x_square(kx, full)
+            gain = gain_of(local)
+            total = None
+            for r in range(ROWS):
+                term = weights[r] * force[pl.ds(r * full + kx, 1), :]
+                total = term if total is None else total + term
+            twice = 2.0 - local * gain
+            first = jnp.where(keep, now[at], 0.0)
+            value = twice * first - jnp.where(keep, prev[at], 0.0) + gain * total
+            current[at] = value
+            onward[at] = twice * value - first
+        return 0
+
+    lax.fori_loop(0, slab // group, body, 0)
+
+
+def lift(force, across, table, ystack, given, terms, turned, pressure, count):
+    zcap = table.shape[0]
+    depth = table.shape[1] // 3
+    used = count * ROWS
+    full, width = force.shape[0] // ROWS, force.shape[1]
+    slab = across.shape[0]
     ax = lax.broadcasted_iota(jnp.int32, (full, width), 0).astype(F32) / full
     ay = lax.broadcasted_iota(jnp.int32, (full, width), 1).astype(F32) / width
     square = BASE * (ax * ax + ay * ay) - BASE
-    terms[used * full :, :] = jnp.zeros(((depth - used) * full, width), F32)
+    if terms is not None:
+        terms[used * full :, :] = jnp.zeros(((depth - used) * full, width), F32)
     turned[used * slab :, :] = jnp.zeros(((depth - used) * slab, width), F32)
-    across = xown[own[0]]
     planes = [plane(force, r) for r in range(ROWS)]
-    for n in range(TERMS):
+    for n in range(count):
         if n:
             planes = [value * square for value in planes]
         for r in range(0, ROWS, 2):
             at = n * ROWS + r
-            for half in range(2):
-                terms[(at + half) * full : (at + half + 1) * full, :] = planes[r + half]
+            if terms is not None:
+                for half in range(2):
+                    terms[(at + half) * full : (at + half + 1) * full, :] = planes[r + half]
             wide = dot(across, tall_split(jnp.concatenate(planes[r : r + 2], axis=1)))
             for half in range(2):
                 turned[(at + half) * slab : (at + half + 1) * slab, :] = wide[
                     :, half * width : (half + 1) * width
                 ]
     block = ROWS * slab
-    for n in range(TERMS):
+    for n in range(count):
         span = slice(n * block, (n + 1) * block)
         turned[span, :] = along_y(turned[span, :], ystack[...])
+    for i in range(0, slab, 2):
+        pair = [turned[pl.ds(i + half, depth, stride=slab), :] for half in range(2)]
+        wide = dot(table[...], tall_split(jnp.concatenate(pair, axis=1)))
+        for half in range(2):
+            span = slice((i + half) * zcap, (i + half + 1) * zcap)
+            value = wide[:, half * width : (half + 1) * width]
+            for piece in given:
+                value = value + piece[span, :]
+            pressure[span, :] = value
+
+
+def first_kernel(own, force, gstack, ystack, xown, free, summed, turned):
+    lift(force, xown[own[0]], gstack, ystack, [free], None, turned, summed, DOUBLE_TERMS)
+
+
+def last_kernel(own, near, tx, uy, onward, estack, hstack, ystack, xown, *rest, full, parts):
+    far, given = rest[:parts], rest[parts : 2 * parts]
+    modes, pressure, spare, force, terms, turned = rest[2 * parts :]
+    slab, zcap, width = onward.shape
+    depth = estack.shape[1] // 3
+    gather_kx(spare, far, own[0])
+    force_planes(spare, near, tx, uy, force)
+    lift(force, xown[own[0]], hstack, ystack, given, terms, turned, pressure, TERMS)
     own_at = own[0] * slab
     for i in range(0, slab, 2):
         pair = [terms[pl.ds(own_at + i + half, depth, stride=full), :] for half in range(2)]
         wide = dot(estack[...], tall_split(jnp.concatenate(pair, axis=1)))
         for half in range(2):
             modes[i + half] = onward[i + half] + wide[:, half * width : (half + 1) * width]
-    for i in range(0, slab, 2):
-        pair = [turned[pl.ds(i + half, depth, stride=slab), :] for half in range(2)]
-        wide = dot(hstack[...], tall_split(jnp.concatenate(pair, axis=1)))
-        for half in range(2):
-            span = slice((i + half) * zcap, (i + half + 1) * zcap)
-            value = wide[:, half * width : (half + 1) * width]
-            for piece in given:
-                value = value + piece[span, :]
-            pressure[span, :] = value
 
 
 def on_device(modes_now, modes_prev, z_extent, lower_nbr, upper_nbr, x_shift, y_shift):
@@ -486,18 +524,20 @@
     big = 4 * slab * zcap * width
 
     xtable, ytable = static_table(full), static_table(width)
-    consts = np.zeros((40, width), np.float32)
+    consts = np.zeros((56, width), np.float32)
     for r in range(ROWS):
         consts[0, r], consts[1, r] = (r, 0) if r < FACE else (ROWS - 1 - r, 1)
     for p, (r, q) in enumerate(PAIRS):
         consts[2:4, p], consts[4:6, p] = consts[0:2, r], consts[0:2, q]
-    for n in range(TERMS):
-        for j in range(len(SERIES) - n):
-            value = SERIES[n + j] * math.comb(n + j, n)
-            consts[8 + j, n] = value
-            consts[24 + j, n * ROWS : (n + 1) * ROWS] = value
-        consts[6:8, n * ROWS : (n + 1) * ROWS] = consts[0:2, :ROWS]
+    for n in range(DOUBLE_TERMS):
+        lanes = slice(n * ROWS, (n + 1) * ROWS)
+        consts[6:8, lanes] = consts[0:2, :ROWS]
+        for j in range(len(SERIES) - n if n < TERMS else 0):
+            consts[8 + j, n] = consts[24 + j, lanes] = SERIES[n + j] * math.comb(n + j, n)
+        for j in range(len(DOUBLE) - n):
+            consts[40 + j, lanes] = DOUBLE[n + j] * math.comb(n + j, n)
     depth = -(-TERMS * ROWS // 16) * 16
+    double_depth = -(-DOUBLE_TERMS * ROWS // 16) * 16
     yhigh, ylow = halves(ytable)
     ystack = np.block([[yhigh, ylow], [yhigh, np.zeros_like(yhigh)]])
     xhigh, xlow = halves(xtable.T)
@@ -558,7 +598,7 @@
             name="choose",
         )(group, after, *held)
 
-    def deliver(chosen):
+    def deliver(chosen, after):
         got = [chosen[0]]
         for k in range(1, tall):
             to = [(i, partner(i // inner, k, tall) * inner + i % inner) for i in range(count)]
@@ -566,10 +606,10 @@
         picked = call(
             functools.partial(pick_kernel, tall=tall, width=inner),
             [shape_of(size, width)],
-            [SMEM] * 3 + [VMEM] * tall,
+            [SMEM] * 3 + [ANY] + [VMEM] * tall,
             moved=5 * size * width * 4,
             name="pick",
-        )(group, lower_nbr, upper_nbr, *got)[0]
+        )(group, lower_nbr, upper_nbr, after, *got)[0]
         return swap(picked)
 
     packet, rows = call(
@@ -582,19 +622,13 @@
         ],
         moved=big,
         name="strip",
-        limit=63 * 1024 * 1024,
+        limit=WIDE,
     )(z_extent, lower_nbr, upper_nbr, modes_now)
     held = spread(packet)
 
-    ahead, zstack, estack, hstack, coefs = call(
+    ahead, coefs = call(
         functools.partial(ahead_kernel, full=full),
-        [
-            shape_of(size, width),
-            shape_of(zcap, 3 * zcap, dtype=BF16),
-            shape_of(zcap, 3 * depth, dtype=BF16),
-            shape_of(zcap, 3 * depth, dtype=BF16),
-            shape_of(16, width),
-        ],
+        [shape_of(size, width), shape_of(16, width)],
         [SMEM] * 2 + [HBM] * 2 + [VMEM] * 2,
         scratch=[
             pltpu.VMEM((slab, zcap, width), F32),
@@ -604,6 +638,7 @@
         flops=10**8,
         moved=2 * big,
         name="ahead",
+        limit=WIDE,
     )(z_extent, own, modes_now, modes_prev, rows, consts)
     chosen = choose(held, ahead)
     mine = swap(packet[:size])
@@ -625,6 +660,26 @@
         moved=2 * big,
         name="relation",
     )(lower_nbr, upper_nbr, x_shift, y_shift, own, coefs, chosen[0], xtall, ytall, *mine)
+    far1 = deliver(chosen, near1)
+
+    estack, hstack, gstack, *free = call(
+        functools.partial(unforced_kernel, full=full),
+        [
+            shape_of(zcap, 3 * depth, dtype=BF16),
+            shape_of(zcap, 3 * depth, dtype=BF16),
+            shape_of(zcap, 3 * double_depth, dtype=BF16),
+        ]
+        + [shape_of(slab * zcap, width)] * parts,
+        [SMEM] * 2 + [ANY] + [VMEM] * 5,
+        scratch=[pltpu.VMEM((slab * zcap, width), F32)],
+        flops=10**9,
+        moved=4 * big,
+        name="unforced",
+    )(z_extent, own, far1[0], modes_now, modes_prev, consts, ystack, xparts)
+    given = [
+        lax.ppermute(free[k], "split", [(i, (i + k) % parts) for i in range(parts)])
+        for k in range(1, parts)
+    ]
 
     packet2, force1, strip2 = call(
         functools.partial(middle_kernel, parts=parts),
@@ -633,27 +688,31 @@
             shape_of(ROWS * full, width),
             shape_of(ROWS * full, width),
         ],
-        [SMEM] * 3 + [VMEM] * (4 + 2 * parts),
+        [SMEM] * 3 + [ANY] + [VMEM] * (4 + 2 * parts),
         scratch=[pltpu.VMEM((ROWS * full, width), F32)],
         flops=10**8,
         moved=2 * big,
         name="middle",
-    )(own, lower_nbr, upper_nbr, near1, tx, uy, mixing, *deliver(chosen), *aheads)
-
-    chosen2 = choose(spread(packet2), packet2)
-    current, onward, *free = call(
+    )(own, lower_nbr, upper_nbr, estack, near1, tx, uy, mixing, *far1, *aheads)
+
+    current, onward = call(
         functools.partial(between_kernel, full=full),
-        [shape_of(slab, zcap, width)] * 2 + [shape_of(slab * zcap, width)] * parts,
-        [SMEM] * 2 + [VMEM] * 7,
-        scratch=[pltpu.VMEM((slab * zcap, width), F32)],
+        [shape_of(slab, zcap, width)] * 2,
+        [SMEM] * 2 + [VMEM] * 4,
         flops=10**9,
-        moved=6 * big,
+        moved=4 * big,
         name="between",
-    )(z_extent, own, modes_now, modes_prev, force1, rows, zstack, ystack, xparts)
-    given = [free[0]] + [
-        lax.ppermute(free[k], "split", [(i, (i + k) % parts) for i in range(parts)])
-        for k in range(1, parts)
-    ]
+    )(z_extent, own, modes_now, modes_prev, force1, rows)
+    chosen2 = choose(spread(packet2), onward)
+    summed = call(
+        first_kernel,
+        [shape_of(slab * zcap, width)],
+        [SMEM] + [VMEM] * 5,
+        scratch=[pltpu.VMEM((double_depth * slab, width), F32)],
+        flops=10**9,
+        moved=2 * big,
+        name="first",
+    )(own, force1, gstack, ystack, xown, free[0])[0]
     near2 = call(
         near_kernel,
         [shape_of(ROWS * full, width)],
@@ -676,7 +735,10 @@
         flops=10**9,
         moved=6 * big,
         name="last",
-    )(own, near2, tx, uy, onward, estack, hstack, ystack, xown, *deliver(chosen2), *given)
+    )(
+        own, near2, tx, uy, onward, estack, hstack, ystack, xown,
+        *deliver(chosen2, summed), summed, *given,
+    )
     return (modes, current, pressure.reshape(slab, zcap, width))
 
 

time: 70.4 us -> 68.7 us (0.976)
  Pallas kernels: 17.2 us -> 24.6 us
  waiting for transfers between devices: 27 us -> 20.5 us
  local copies, waits for them, and re-layouts: 3.28 us -> 1.16 us
    pallas_call x0 -> x2, Pallas kernels: none -> 7 us  [the longest x1 5.33 us: on_device(): call(functools.partial(unforced_kernel, full=full), [shape_of(zcap, 3 * d...]
    ppermute x4, waiting for transfers between devices: 13.2 us -> 7.58 us  [swap(): lax.ppermute(piece, 'split', [(i, (i + k) % parts) for i in range(parts)])]
    unnamed x30 -> x26, local copies, waits for them, and re-layouts: 3.27 us -> 0.23 us
    pallas_call x1, Pallas kernels: 5.23 us -> 2.66 us  [on_device(): call(functools.partial(between_kernel, full=full), [shape_of(slab, zcap,...]
    ppermute x6, waiting for transfers between devices: 13.8 us -> 11.5 us  [deliver(): got.append(lax.ppermute(chosen[k], 'dom', to))]
    pallas_call x1, Pallas kernels: 2.42 us -> 4.24 us  [on_device(): call(functools.partial(ahead_kernel, full=full), [shape_of(size, width),...]
    ppermute x6, waiting for transfers between devices: 0.02 us -> 1.42 us  [spread(): held.append(lax.ppermute(packet, 'dom', to))]
    slice x1, local copies, waits for them, and re-layouts: 0.01 us -> 0.93 us  [on_device(): mine = swap(packet[:size])]
  transfers between devices with their start and end apart: 17 -> 17, of which waited for: 5 -> 4; matrix products, arithmetic and copies ran while one was open for 0% -> 1% of each run, Pallas kernels for 15% -> 25%
where the time goes in v3:
time: 68.7 us; the launch traced here: 68.4 us
  Pallas kernels  24.6 us (36%)
  waiting for transfers between devices  20.5 us (30%)
  starting transfers between devices  19.2 us (28%)
  between operations  2.8 us (4%)
  local copies, waits for them, and re-layouts  1.16 us (2%)
    ppermute x6, waiting for transfers between devices, deliver(): got.append(lax.ppermute(chosen[k], 'dom', to))  11.5 us
    ppermute x6, starting transfers between devices, deliver(): got.append(lax.ppermute(chosen[k], 'dom', to))  8.9 us
    ppermute x4, waiting for transfers between devices, swap(): lax.ppermute(piece, 'split', [(i, (i + k) % parts) for i in range(parts)])  7.58 us
    pallas_call x1, Pallas kernels, on_device(): call(functools.partial(unforced_kernel, full=full), [shape_of(zcap, 3 * d...  5.33 us
    ppermute x6, starting transfers between devices, spread(): held.append(lax.ppermute(packet, 'dom', to))  5.04 us
    pallas_call x1, Pallas kernels, on_device(): call(functools.partial(ahead_kernel, full=full), [shape_of(size, width),...  4.24 us
    ppermute x4, starting transfers between devices, swap(): lax.ppermute(piece, 'split', [(i, (i + k) % parts) for i in range(parts)])  4.02 us
    pallas_call x1, Pallas kernels, on_device(): call(functools.partial(last_kernel, full=full, parts=parts), [shape_of(sl...  3.9 us
  transfers between devices with their start and end apart: 17, of which 4 were waited for; matrix products, arithmetic and copies ran while one was open for 1% of the time, Pallas kernels for 25%

profile of v3, /device:TPU:0, one launch (start us, length us, event | category | flops | bytes accessed | tf_op | source)
XLA Modules:
  0.0 68.4 jit_solution(5274967877705732870)
XLA Ops:
  2.6 2.3 %strip.1 = (f32[200,128]{1,0:T(8,128)}, f32[64,128]{1,0:T(8,128)}) custom-call(s32[1]{0:T(128)S(6)} %copy.16.extent, s32[1]{0:T(128)S(6)} %copy.17.below, s32[1]{0:T(128)S(6)} %copy.18.above, f32[32,64,128]{2,1,0:T(8,128)} %now.5), custom_call_target="tpu_custom_call" | custom-call | bytes 1048576 | tf_op jit(solution)/shard_map/strip/pallas_call | solution.py:615
  4.9 2.4 %collective-permute-start.2 = (f32[200,128]{1,0:T(8,128)}, f32[200,128]{1,0:T(8,128)S(1)}, u32[]{:S(2)}, u32[]{:S(2)}) collective-permute-start(f32[200,128]{1,0:T(8,128)} %get-tuple-element.36.refs_0_), channel_id=1, source_target_pairs={{0,6},{2,4},{4,2},{6,0},{8,14},{10,12},{12,10},{14,8},{16,22},{18,... | collective-permute-start | bytes 307208 | tf_op jit(solution)/shard_map/ppermute | solution.py:588
  8.0 0.9 %slice.3.rest_0_ = f32[192,128]{1,0:T(8,128)S(1)} slice(f32[200,128]{1,0:T(8,128)} %get-tuple-element.36.refs_0_), slice={[0:192], [0:128]} | slice | bytes 196608 | tf_op jit(solution)/shard_map/slice | solution.py:644
  9.0 1.7 %collective-permute-start.3 = (f32[192,128]{1,0:T(8,128)S(1)}, f32[192,128]{1,0:T(8,128)S(1)}, u32[]{:S(2)}, u32[]{:S(2)}) collective-permute-start(f32[192,128]{1,0:T(8,128)S(1)} %slice.3.rest_0_), channel_id=1, source_target_pairs={{0,1},{1,0},{2,3},{3,2},{4,5},{5,4},{6,7},{7,6},{8,9},{9,8},{10,11... | collective-permute-start | bytes 294920 | tf_op jit(solution)/shard_map/ppermute | solution.py:581
  10.7 4.2 %ahead.1 = (f32[192,128]{1,0:T(8,128)}, f32[16,128]{1,0:T(8,128)}) custom-call(s32[1]{0:T(128)S(6)} %copy.16.extent, s32[1]{0:T(128)} %bitcast.own, f32[32,64,128]{2,1,0:T(8,128)} %now.5, f32[32,64,128]{2,1,0:T(8,128)} %prev.3, f32[64,128]{1,0:T(8,128)} %get-tuple-element.33.rows, f32[56,128]{1,0:T(8,128)} %constant.20.clone.consts), custom_call_target="tpu_custom_call" | custom-call | flops 100000000 | bytes 2097152 | tf_op jit(solution)/shard_map/ahead/pallas_call | solution.py:629
  15.2 1.6 %collective-permute-start.4 = (f32[192,128]{1,0:T(8,128)S(1)}, f32[192,128]{1,0:T(8,128)S(1)}, u32[]{:S(2)}, u32[]{:S(2)}) collective-permute-start(f32[192,128]{1,0:T(8,128)S(1)} %get-tuple-element.39), channel_id=1, source_target_pairs={{0,8},{2,10},{4,12},{6,14},{8,0},{10,2},{12,4},{14,6},{16,24},{18,... | collective-permute-start | bytes 294920 | tf_op jit(solution)/shard_map/ppermute | solution.py:605
  16.8 2.6 %collective-permute-start.5 = (f32[192,128]{1,0:T(8,128)S(1)}, f32[192,128]{1,0:T(8,128)S(1)}, u32[]{:S(2)}, u32[]{:S(2)}) collective-permute-start(f32[192,128]{1,0:T(8,128)S(1)} %get-tuple-element.40), channel_id=1, source_target_pairs={{0,16},{2,18},{4,20},{6,22},{8,24},{10,26},{12,28},{14,30},{16,0},... | collective-permute-start | bytes 294920 | tf_op jit(solution)/shard_map/ppermute | solution.py:605
  20.2 2.0 %relation.1 = (f32[2,64,64]{2,1,0:T(8,128)S(1)}, f32[2,128,128]{2,1,0:T(8,128)S(1)}, f32[2,64,64]{2,1,0:T(8,128)S(1)}, f32[2,128,128]{2,1,0:T(8,128)S(1)}, f32[3...) custom-call(s32[1]{0:T(128)S(6)} %copy.17.below, s32[1]{0:T(128)S(6)} %copy.18.above, ...), custom_call_target="tpu_custom_call" | custom-call | flops 100000000 | bytes 2097152 | tf_op jit(solution)/shard_map/relation/pallas_call | solution.py:647
  22.2 5.2 %collective-permute-done.5.refs_2_ = f32[192,128]{1,0:T(8,128)S(1)} collective-permute-done((f32[192,128]{1,0:T(8,128)S(1)}, f32[192,128]{1,0:T(8,128)S(1)}, u32[]{:S(2)}, u32[]{:S(2)}) %collective-permute-start.5) | collective-permute-done | bytes 98336 | tf_op jit(solution)/shard_map/ppermute | solution.py:605
  27.4 0.7 %collective-permute-start.7 = (f32[192,128]{1,0:T(8,128)S(1)}, f32[192,128]{1,0:T(8,128)S(1)}, u32[]{:S(2)}, u32[]{:S(2)}) collective-permute-start(f32[192,128]{1,0:T(8,128)S(1)} %pick.2.after.rest_0_), channel_id=1, source_target_pairs={{0,1},{1,0},{2,3},{3,2},{4,5},{5,4},{6,7},{7,6},{8,9},{9,8},{10,11... | collective-permute-start | bytes 294920 | tf_op jit(solution)/shard_map/ppermute | solution.py:581
  28.3 5.3 %unforced.1 = (bf16[64,144]{1,0:T(8,128)(2,1)S(1)}, bf16[64,144]{1,0:T(8,128)(2,1)S(1)}, bf16[64,192]{1,0:T(8,128)(2,1)S(1)}, f32[2048,128]{1,0:T(8,128)S(1)}, f32[2048,128]{1,0:T(8,128)S(1)}) custom-call(s32[1]{0:T(128)S(6)} %copy.16.extent, s32[1]{0:T(128)} %bitcast.own, f32[192,128]{1,0:T(8,128)S(1)} %pick.2.after.rest_0_, f32[32,64,128]{2,1,0:T(8,128)S(1)} %copy-done, ...), custom_call_target="tpu_custom_call" | custom-call | flops 1000000000 | bytes 4194304 | tf_op jit(solution)/shard_map/unforced/pallas_call | solution.py:665
  33.7 1.6 %middle.1 = (f32[200,128]{1,0:T(8,128)S(1)}, f32[384,128]{1,0:T(8,128)S(1)}, f32[384,128]{1,0:T(8,128)S(1)}) custom-call(s32[1]{0:T(128)} %bitcast.own, s32[1]{0:T(128)S(6)} %copy.17.below, s32[1]{0:T(128)S(6)} %copy.18.above, bf16[64,144]{1,0:T(8,128)(2,1)S(1)} %get-tuple-element.42.after.estack, f32[384,128]{1,0:T(8,128)S(1)} %get-tuple-element.38.after.near, ...), custom_call_target="tpu_custom_call" | custom-call | flops 100000000 | bytes 2097152 | tf_op jit(solution)/shard_map/middle/pallas_call | solution.py:684
  35.4 1.4 %collective-permute-start.10 = (f32[200,128]{1,0:T(8,128)S(1)}, f32[200,128]{1,0:T(8,128)S(1)}, u32[]{:S(2)}, u32[]{:S(2)}) collective-permute-start(f32[200,128]{1,0:T(8,128)S(1)} %get-tuple-element.54.refs_0_), channel_id=1, source_target_pairs={{0,4},{2,6},{4,0},{6,2},{8,12},{10,14},{12,8},{14,10},{16,20},{18,... | collective-permute-start | bytes 307208 | tf_op jit(solution)/shard_map/ppermute | solution.py:588
  37.2 1.3 %collective-permute-start.16 = (f32[2048,128]{1,0:T(8,128)S(1)}, f32[2048,128]{1,0:T(8,128)S(1)}, u32[]{:S(2)}, u32[]{:S(2)}) collective-permute-start(f32[2048,128]{1,0:T(8,128)S(1)} %get-tuple-element.59), channel_id=1, source_target_pairs={{0,1},{1,0},{2,3},{3,2},{4,5},{5,4},{6,7},{7,6},{8,9},{9,8},{10,11... | collective-permute-start | bytes 3145736 | tf_op jit(solution)/shard_map/ppermute | solution.py:680
  38.5 2.7 %between.1 = (f32[32,64,128]{2,1,0:T(8,128)}, f32[32,64,128]{2,1,0:T(8,128)S(1)}) custom-call(s32[1]{0:T(128)S(6)} %copy.16.extent, s32[1]{0:T(128)} %bitcast.own, f32[32,64,128]{2,1,0:T(8,128)S(1)} %copy-done, f32[32,64,128]{2,1,0:T(8,128)S(1)} %copy-done.1, f32[384,128]{1,0:T(8,128)S(1)} %get-tuple-element.49.force, f32[64,128]{1,0:T(8,128)S(1)} %copy-done.7), custom_call_target="tpu_custom_call" | custom-call | flops 1000000000 | bytes 4194304 | tf_op jit(solution)/shard_map/between/pallas_call | solution.py:698
  41.1 1.4 %collective-permute-done.10.refs_2_ = f32[200,128]{1,0:T(8,128)S(1)} collective-permute-done((f32[200,128]{1,0:T(8,128)S(1)}, f32[200,128]{1,0:T(8,128)S(1)}, u32[]{:S(2)}, u32[]{:S(2)}) %collective-permute-start.10) | collective-permute-done | bytes 102432 | tf_op jit(solution)/shard_map/ppermute | solution.py:588
  42.7 1.8 %collective-permute-start.12 = (f32[192,128]{1,0:T(8,128)S(1)}, f32[192,128]{1,0:T(8,128)S(1)}, u32[]{:S(2)}, u32[]{:S(2)}) collective-permute-start(f32[192,128]{1,0:T(8,128)S(1)} %get-tuple-element.56), channel_id=1, source_target_pairs={{0,8},{2,10},{4,12},{6,14},{8,0},{10,2},{12,4},{14,6},{16,24},{18,... | collective-permute-start | bytes 294920 | tf_op jit(solution)/shard_map/ppermute | solution.py:605
  44.5 1.4 %collective-permute-start.13 = (f32[192,128]{1,0:T(8,128)S(1)}, f32[192,128]{1,0:T(8,128)S(1)}, u32[]{:S(2)}, u32[]{:S(2)}) collective-permute-start(f32[192,128]{1,0:T(8,128)S(1)} %get-tuple-element.57), channel_id=1, source_target_pairs={{0,16},{2,18},{4,20},{6,22},{8,24},{10,26},{12,28},{14,30},{16,0},... | collective-permute-start | bytes 294920 | tf_op jit(solution)/shard_map/ppermute | solution.py:605
  45.9 1.2 %collective-permute-start.14 = (f32[192,128]{1,0:T(8,128)S(1)}, f32[192,128]{1,0:T(8,128)S(1)}, u32[]{:S(2)}, u32[]{:S(2)}) collective-permute-start(f32[192,128]{1,0:T(8,128)S(1)} %get-tuple-element.58), channel_id=1, source_target_pairs={{0,24},{2,26},{4,28},{6,30},{8,16},{10,18},{12,20},{14,22},{16,8},... | collective-permute-start | bytes 294920 | tf_op jit(solution)/shard_map/ppermute | solution.py:605
  47.1 1.7 %first.1.after.rest_2_ = f32[2048,128]{1,0:T(8,128)S(1)} custom-call(s32[1]{0:T(128)} %bitcast.own, f32[384,128]{1,0:T(8,128)S(1)} %get-tuple-element.49.force, bf16[64,192]{1,0:T(8,128)(2,1)S(1)} %get-tuple-element.52.gstack, bf16[256,256]{1,0:T(8,128)(2,1)S(1)} %copy-done.3, bf16[2,32,192]{2,1,0:T(8,128)(2,1)S(1)} %copy-done.6, ...), custom_call_target="tpu_custom_call" | custom-call | flops 1000000000 | bytes 2097152 | tf_op jit(solution)/shard_map/first/pallas_call | solution.py:707
  48.8 6.4 %collective-permute-done.13.refs_2_ = f32[192,128]{1,0:T(8,128)S(1)} collective-permute-done((f32[192,128]{1,0:T(8,128)S(1)}, f32[192,128]{1,0:T(8,128)S(1)}, u32[]{:S(2)}, u32[]{:S(2)}) %collective-permute-start.13) | collective-permute-done | bytes 98336 | tf_op jit(solution)/shard_map/ppermute | solution.py:605
  55.2 1.1 %collective-permute-start.15 = (f32[192,128]{1,0:T(8,128)S(1)}, f32[192,128]{1,0:T(8,128)S(1)}, u32[]{:S(2)}, u32[]{:S(2)}) collective-permute-start(f32[192,128]{1,0:T(8,128)S(1)} %pick.3.rest_0_), channel_id=1, source_target_pairs={{0,1},{1,0},{2,3},{3,2},{4,5},{5,4},{6,7},{7,6},{8,9},{9,8},{10,11... | collective-permute-start | bytes 294920 | tf_op jit(solution)/shard_map/ppermute | solution.py:581
  56.9 7.6 %collective-permute-done.15.rest_1_ = f32[192,128]{1,0:T(8,128)S(1)} collective-permute-done((f32[192,128]{1,0:T(8,128)S(1)}, f32[192,128]{1,0:T(8,128)S(1)}, u32[]{:S(2)}, u32[]{:S(2)}) %collective-permute-start.15) | collective-permute-done | bytes 98336 | tf_op jit(solution)/shard_map/ppermute | solution.py:581
  64.5 3.9 %last.1 = (f32[32,64,128]{2,1,0:T(8,128)}, f32[2048,128]{1,0:T(8,128)}) custom-call(s32[1]{0:T(128)} %bitcast.own, f32[384,128]{1,0:T(8,128)S(1)} %near.1, f32[2,64,64]{2,1,0:T(8,128)S(1)} %get-tuple-element.43.tx, f32[2,128,128]{2,1,0:T(8,128)S(1)} %get-tuple-element.44.uy, f32[32,64,128]{2,1,0:T(8,128)S(1)} %get-tuple-element.50.after.onward, ...), custom_call_target="tpu_custom_call" | custom-call | flops 1000000000 | bytes 6291456 | tf_op jit(solution)/shard_map/last/pallas_call | solution.py:725
  (50 shorter events, 3.1 us)
Async XLA Ops:
  4.9 10.0 %collective-permute-start.2 = (f32[200,128]{1,0:T(8,128)}, f32[200,128]{1,0:T(8,128)S(1)}, u32[]{:S(2)}, u32[]{:S(2)}) collective-permute-start(f32[200,128]{1,0:T(8,128)} %get-tuple-element.36.refs_0_), channel_id=1, source_target_pairs={{0,6},{2,4},{4,2},{6,0},{8,14},{10,12},{12,10},{14,8},{16,22},{18,... | collective-permute-start | bytes 307208 | tf_op jit(solution)/shard_map/ppermute | solution.py:588
  7.3 7.6 %collective-permute-start.1 = (f32[200,128]{1,0:T(8,128)}, f32[200,128]{1,0:T(8,128)S(1)}, u32[]{:S(2)}, u32[]{:S(2)}) collective-permute-start(f32[200,128]{1,0:T(8,128)} %get-tuple-element.36.refs_0_), channel_id=1, source_target_pairs={{0,4},{2,6},{4,0},{6,2},{8,12},{10,14},{12,8},{14,10},{16,20},{18,... | collective-permute-start | bytes 307208 | tf_op jit(solution)/shard_map/ppermute | solution.py:588
  8.0 7.0 %collective-permute-start = (f32[200,128]{1,0:T(8,128)}, f32[200,128]{1,0:T(8,128)S(1)}, u32[]{:S(2)}, u32[]{:S(2)}) collective-permute-start(f32[200,128]{1,0:T(8,128)} %get-tuple-element.36.refs_0_), channel_id=1, source_target_pairs={{0,2},{2,0},{4,6},{6,4},{8,10},{10,8},{12,14},{14,12},{16,18},{18,... | collective-permute-start | bytes 307208 | tf_op jit(solution)/shard_map/ppermute | solution.py:588
  9.0 11.2 %collective-permute-start.3 = (f32[192,128]{1,0:T(8,128)S(1)}, f32[192,128]{1,0:T(8,128)S(1)}, u32[]{:S(2)}, u32[]{:S(2)}) collective-permute-start(f32[192,128]{1,0:T(8,128)S(1)} %slice.3.rest_0_), channel_id=1, source_target_pairs={{0,1},{1,0},{2,3},{3,2},{4,5},{5,4},{6,7},{7,6},{8,9},{9,8},{10,11... | collective-permute-start | bytes 294920 | tf_op jit(solution)/shard_map/ppermute | solution.py:581
  15.0 5.2 %copy-start.2 = (f32[512,128]{1,0:T(8,128)S(1)}, f32[512,128]{1,0:T(8,128)}, u32[]{:S(2)}) copy-start(f32[512,128]{1,0:T(8,128)} %constant.25.clone.ytall) | copy-start | bytes 786436
  15.0 5.2 %copy-start.4 = (f32[256,64]{1,0:T(8,128)S(1)}, f32[256,64]{1,0:T(8,128)}, u32[]{:S(2)}) copy-start(f32[256,64]{1,0:T(8,128)} %constant.24.clone.xtall) | copy-start | bytes 196612
  15.0 5.2 %copy-start.9 = (f32[16,128]{1,0:T(8,128)S(1)}, f32[16,128]{1,0:T(8,128)}, u32[]{:S(2)}) copy-start(f32[16,128]{1,0:T(8,128)} %get-tuple-element.34.coefs) | copy-start | bytes 24580
  15.0 5.2 %copy-start.10 = (s32[1,2]{1,0:T(1,128)S(1)}, s32[1,2]{1,0:T(1,128)}, u32[]{:S(2)}) copy-start(s32[1,2]{1,0:T(1,128)} %x_shift.1) | copy-start | bytes 28
  15.0 5.2 %copy-start.11 = (s32[1,2]{1,0:T(1,128)S(1)}, s32[1,2]{1,0:T(1,128)}, u32[]{:S(2)}) copy-start(s32[1,2]{1,0:T(1,128)} %y_shift.1) | copy-start | bytes 28
  15.0 13.1 %copy-start.1 = (f32[32,64,128]{2,1,0:T(8,128)S(1)}, f32[32,64,128]{2,1,0:T(8,128)}, u32[]{:S(2)}) copy-start(f32[32,64,128]{2,1,0:T(8,128)} %prev.3) | copy-start | bytes 3145732
  15.2 13.0 %copy-start = (f32[32,64,128]{2,1,0:T(8,128)S(1)}, f32[32,64,128]{2,1,0:T(8,128)}, u32[]{:S(2)}) copy-start(f32[32,64,128]{2,1,0:T(8,128)} %now.5) | copy-start | bytes 3145732
  15.2 7.0 %collective-permute-start.4 = (f32[192,128]{1,0:T(8,128)S(1)}, f32[192,128]{1,0:T(8,128)S(1)}, u32[]{:S(2)}, u32[]{:S(2)}) collective-permute-start(f32[192,128]{1,0:T(8,128)S(1)} %get-tuple-element.39), channel_id=1, source_target_pairs={{0,8},{2,10},{4,12},{6,14},{8,0},{10,2},{12,4},{14,6},{16,24},{18,... | collective-permute-start | bytes 294920 | tf_op jit(solution)/shard_map/ppermute | solution.py:605
  16.8 10.6 %collective-permute-start.5 = (f32[192,128]{1,0:T(8,128)S(1)}, f32[192,128]{1,0:T(8,128)S(1)}, u32[]{:S(2)}, u32[]{:S(2)}) collective-permute-start(f32[192,128]{1,0:T(8,128)S(1)} %get-tuple-element.40), channel_id=1, source_target_pairs={{0,16},{2,18},{4,20},{6,22},{8,24},{10,26},{12,28},{14,30},{16,0},... | collective-permute-start | bytes 294920 | tf_op jit(solution)/shard_map/ppermute | solution.py:605
  19.4 8.0 %collective-permute-start.6 = (f32[192,128]{1,0:T(8,128)S(1)}, f32[192,128]{1,0:T(8,128)S(1)}, u32[]{:S(2)}, u32[]{:S(2)}) collective-permute-start(f32[192,128]{1,0:T(8,128)S(1)} %get-tuple-element.41), channel_id=1, source_target_pairs={{0,24},{2,26},{4,28},{6,30},{8,16},{10,18},{12,20},{14,22},{16,8},... | collective-permute-start | bytes 294920 | tf_op jit(solution)/shard_map/ppermute | solution.py:605
  19.6 14.0 %collective-permute-start.8 = (f32[192,128]{1,0:T(8,128)}, f32[192,128]{1,0:T(8,128)S(1)}, u32[]{:S(2)}, u32[]{:S(2)}) collective-permute-start(f32[192,128]{1,0:T(8,128)} %get-tuple-element.35.after.rest_2_), channel_id=1, source_target_pairs={{0,1},{1,0},{2,3},{3,2},{4,5},{5,4},{6,7},{7,6},{8,9},{9,8},{10,11... | collective-permute-start | bytes 294920 | tf_op jit(solution)/shard_map/ppermute | solution.py:581
  27.4 6.2 %collective-permute-start.7 = (f32[192,128]{1,0:T(8,128)S(1)}, f32[192,128]{1,0:T(8,128)S(1)}, u32[]{:S(2)}, u32[]{:S(2)}) collective-permute-start(f32[192,128]{1,0:T(8,128)S(1)} %pick.2.after.rest_0_), channel_id=1, source_target_pairs={{0,1},{1,0},{2,3},{3,2},{4,5},{5,4},{6,7},{7,6},{8,9},{9,8},{10,11... | collective-permute-start | bytes 294920 | tf_op jit(solution)/shard_map/ppermute | solution.py:581
  35.3 5.9 %collective-permute-start.11 = (f32[200,128]{1,0:T(8,128)S(1)}, f32[200,128]{1,0:T(8,128)S(1)}, u32[]{:S(2)}, u32[]{:S(2)}) collective-permute-start(f32[200,128]{1,0:T(8,128)S(1)} %get-tuple-element.54.refs_0_), channel_id=1, source_target_pairs={{0,6},{2,4},{4,2},{6,0},{8,14},{10,12},{12,10},{14,8},{16,22},{18,... | collective-permute-start | bytes 307208 | tf_op jit(solution)/shard_map/ppermute | solution.py:588
  35.4 7.2 %collective-permute-start.10 = (f32[200,128]{1,0:T(8,128)S(1)}, f32[200,128]{1,0:T(8,128)S(1)}, u32[]{:S(2)}, u32[]{:S(2)}) collective-permute-start(f32[200,128]{1,0:T(8,128)S(1)} %get-tuple-element.54.refs_0_), channel_id=1, source_target_pairs={{0,4},{2,6},{4,0},{6,2},{8,12},{10,14},{12,8},{14,10},{16,20},{18,... | collective-permute-start | bytes 307208 | tf_op jit(solution)/shard_map/ppermute | solution.py:588
  36.8 5.8 %collective-permute-start.9 = (f32[200,128]{1,0:T(8,128)S(1)}, f32[200,128]{1,0:T(8,128)S(1)}, u32[]{:S(2)}, u32[]{:S(2)}) collective-permute-start(f32[200,128]{1,0:T(8,128)S(1)} %get-tuple-element.54.refs_0_), channel_id=1, source_target_pairs={{0,2},{2,0},{4,6},{6,4},{8,10},{10,8},{12,14},{14,12},{16,18},{18,... | collective-permute-start | bytes 307208 | tf_op jit(solution)/shard_map/ppermute | solution.py:588
  37.2 27.3 %collective-permute-start.16 = (f32[2048,128]{1,0:T(8,128)S(1)}, f32[2048,128]{1,0:T(8,128)S(1)}, u32[]{:S(2)}, u32[]{:S(2)}) collective-permute-start(f32[2048,128]{1,0:T(8,128)S(1)} %get-tuple-element.59), channel_id=1, source_target_pairs={{0,1},{1,0},{2,3},{3,2},{4,5},{5,4},{6,7},{7,6},{8,9},{9,8},{10,11... | collective-permute-start | bytes 3145736 | tf_op jit(solution)/shard_map/ppermute | solution.py:680
  42.7 6.1 %collective-permute-start.12 = (f32[192,128]{1,0:T(8,128)S(1)}, f32[192,128]{1,0:T(8,128)S(1)}, u32[]{:S(2)}, u32[]{:S(2)}) collective-permute-start(f32[192,128]{1,0:T(8,128)S(1)} %get-tuple-element.56), channel_id=1, source_target_pairs={{0,8},{2,10},{4,12},{6,14},{8,0},{10,2},{12,4},{14,6},{16,24},{18,... | collective-permute-start | bytes 294920 | tf_op jit(solution)/shard_map/ppermute | solution.py:605
  44.5 10.7 %collective-permute-start.13 = (f32[192,128]{1,0:T(8,128)S(1)}, f32[192,128]{1,0:T(8,128)S(1)}, u32[]{:S(2)}, u32[]{:S(2)}) collective-permute-start(f32[192,128]{1,0:T(8,128)S(1)} %get-tuple-element.57), channel_id=1, source_target_pairs={{0,16},{2,18},{4,20},{6,22},{8,24},{10,26},{12,28},{14,30},{16,0},... | collective-permute-start | bytes 294920 | tf_op jit(solution)/shard_map/ppermute | solution.py:605
  45.9 9.3 %collective-permute-start.14 = (f32[192,128]{1,0:T(8,128)S(1)}, f32[192,128]{1,0:T(8,128)S(1)}, u32[]{:S(2)}, u32[]{:S(2)}) collective-permute-start(f32[192,128]{1,0:T(8,128)S(1)} %get-tuple-element.58), channel_id=1, source_target_pairs={{0,24},{2,26},{4,28},{6,30},{8,16},{10,18},{12,20},{14,22},{16,8},... | collective-permute-start | bytes 294920 | tf_op jit(solution)/shard_map/ppermute | solution.py:605
  55.2 9.3 %collective-permute-start.15 = (f32[192,128]{1,0:T(8,128)S(1)}, f32[192,128]{1,0:T(8,128)S(1)}, u32[]{:S(2)}, u32[]{:S(2)}) collective-permute-start(f32[192,128]{1,0:T(8,128)S(1)} %pick.3.rest_0_), channel_id=1, source_target_pairs={{0,1},{1,0},{2,3},{3,2},{4,5},{5,4},{6,7},{7,6},{8,9},{9,8},{10,11... | collective-permute-start | bytes 294920 | tf_op jit(solution)/shard_map/ppermute | solution.py:581
  (6 other events, 16.4 us)

commit v4 on v3

--- a/solution.py
+++ b/solution.py
@@ -21,7 +21,6 @@
 TERMS = 6
 DOUBLE = [(-1) ** (n + 1) * (4 - 2.0 * 4.0 ** (n + 1)) / math.factorial(2 * n + 2) for n in range(14)]
 DOUBLE_TERMS = 9
-WIDE = 63 * 1024 * 1024
 BASE = (COURANT * math.pi) ** 2
 PAIRS = [(r, q) for r in range(ROWS) for q in range(r, ROWS)]
 VMEM = pl.BlockSpec(memory_space=pltpu.VMEM)
@@ -168,14 +167,16 @@
     return ref[r * full : (r + 1) * full, :]
 
 
-def call(kernel, out_shape, in_specs, scratch=(), flops=0, moved=0, name=None, limit=LIMIT):
+def call(
+    kernel, out_shape, in_specs, scratch=(), flops=0, moved=0, name=None, out=VMEM
+):
     return pl.pallas_call(
         kernel,
         out_shape=out_shape,
         in_specs=in_specs,
-        out_specs=[VMEM] * len(out_shape),
+        out_specs=[out] * len(out_shape),
         scratch_shapes=list(scratch),
-        compiler_params=pltpu.CompilerParams(vmem_limit_bytes=limit),
+        compiler_params=pltpu.CompilerParams(vmem_limit_bytes=LIMIT),
         cost_estimate=pl.CostEstimate(flops=flops, bytes_accessed=moved, transcendentals=0),
         name=name,
     )
@@ -185,34 +186,28 @@
     return jax.ShapeDtypeStruct(dims, dtype)
 
 
-def load_chunks(source, held, sems):
-    copies = []
-    for i in range(held.shape[0] // CHUNK):
-        span = pl.ds(i * CHUNK, CHUNK)
-        copies.append(pltpu.make_async_copy(source.at[span], held.at[span], sems.at[i]))
-        copies[-1].start()
-    return copies
-
-
-def strip_kernel(extent, below, above, now, packet, rows, held, sems):
+def label(packet, nbr):
+    packet[packet.shape[0] - HEAD :, :] = jnp.full((HEAD, packet.shape[1]), nbr.astype(F32))
+
+
+def strip_kernel(extent, below, above, now, strip, upper, lower, rows):
     slab, zcap, width = now.shape
-    copies = load_chunks(now, held, sems)
     at = lax.broadcasted_iota(jnp.int32, (1, width), 1)
     far_face = at >= FACE
     near = jnp.where(far_face, ROWS - 1 - at, at)
     near = jnp.where(at < ROWS, near, 0).astype(F32)
     table = face_rows(near, far_face.astype(F32), (zcap, width), extent[0])
     rows[...] = table
-    at = lax.broadcasted_iota(jnp.int32, (HEAD, width), 0)
-    names = jnp.where(at < HEAD // 2, above[0], below[0])
-    packet[ROWS * slab :, :] = names.astype(F32)
+    label(upper, above[0])
+    label(lower, below[0])
     weights = [jnp.broadcast_to(table[:, r : r + 1], (zcap, width)) for r in range(ROWS)]
-    for i, copy in enumerate(copies):
-        copy.wait()
-        part = held[i * CHUNK : (i + 1) * CHUNK]
+    for i in range(slab // CHUNK):
+        part = now[i * CHUNK : (i + 1) * CHUNK]
         for r in range(ROWS):
-            span = slice(r * slab + i * CHUNK, r * slab + (i + 1) * CHUNK)
-            packet[span, :] = jnp.sum(part * weights[r][None], axis=1)
+            value = jnp.sum(part * weights[r][None], axis=1)
+            strip[r * slab + i * CHUNK : r * slab + (i + 1) * CHUNK, :] = value
+            at = r % FACE * slab + i * CHUNK
+            (lower if r < FACE else upper)[at : at + CHUNK, :] = value
 
 
 def lane_series(consts, first, count, shape, extent):
@@ -225,6 +220,14 @@
     return total
 
 
+def z_table(ext, zcap):
+    kk = lax.broadcasted_iota(jnp.int32, (zcap, zcap), 1)
+    zz = lax.broadcasted_iota(jnp.int32, (zcap, zcap), 0)
+    lenf = jnp.full((zcap, zcap), ext.astype(F32))
+    table = scale_of(kk, lenf) * cosine_of(kk.astype(F32), 2.0 * zz.astype(F32) + 1.0, lenf)
+    return jnp.where((kk < ext) & (zz < ext), table, 0.0)
+
+
 def stack_lanes(table, depth):
     table = table[:, :depth]
     high = table.astype(BF16).astype(F32)
@@ -232,11 +235,10 @@
 
 
 def ahead_kernel(
-    extent, own, now_far, prev_far, rows, consts, strip, coefs, now, prev, sems, *, full
+    extent, own, now, prev, rows, consts, strip, coefs, *, full
 ):
     slab, zcap, width = now.shape
     ext = extent[0]
-    copies = zip(load_chunks(now_far, now, sems.at[0]), load_chunks(prev_far, prev, sems.at[1]))
 
     shape = (zcap, width)
     pairs = face_rows(consts[2:3, :], consts[3:4, :], shape, ext)
@@ -247,17 +249,14 @@
     keep = lax.broadcasted_iota(jnp.int32, shape, 0) < ext
     square = plane_square(shape, ext)
     weights = [jnp.broadcast_to(rows[:, r : r + 1], shape) for r in range(ROWS)]
-    for i, pair in enumerate(copies):
-        for copy in pair:
-            copy.wait()
-        for kx in range(i * CHUNK, (i + 1) * CHUNK):
-            local = square + x_square(own[0] * slab + kx, full)
-            twice = 2.0 - local * gain_of(local)
-            ahead = jnp.where(keep, twice * now[kx] - prev[kx], 0.0)
-            for r in range(ROWS):
-                strip[r * slab + kx : r * slab + kx + 1, :] = jnp.sum(
-                    ahead * weights[r], axis=0, keepdims=True
-                )
+    for kx in range(slab):
+        local = square + x_square(own[0] * slab + kx, full)
+        twice = 2.0 - local * gain_of(local)
+        ahead = jnp.where(keep, twice * now[kx] - prev[kx], 0.0)
+        for r in range(ROWS):
+            strip[r * slab + kx : r * slab + kx + 1, :] = jnp.sum(
+                ahead * weights[r], axis=0, keepdims=True
+            )
 
 
 def relation_kernel(
@@ -310,38 +309,42 @@
         force[r * full : (r + 1) * full, :] = value - plane(near, r)
 
 
-def choose_kernel(group, after, *refs, width):
-    held, out = refs[:width], refs[width:]
-    rows = out[0].shape[0]
-    half = rows // 2
+def choose_kernel(group, after, *refs, tall, width):
+    uppers, lowers = refs[:tall], refs[tall : tall + width]
+    out = refs[tall + width :]
     h, l = group[0] // width, lax.rem(group[0], width)
-    for k in range(len(out)):
-        dest = (partner(h, k, len(out)) * width + l).astype(F32)
-        for f in range(2):
-            lo, hi = f * half, (f + 1) * half
-            row = rows + (0 if f == 1 else HEAD // 2)
-            chosen = held[0][lo:hi, :]
+    for held, packets, places in (
+        (uppers, out[:width], [h * width + partner(l, k, width) for k in range(width)]),
+        (lowers, out[width:], [partner(h, k, tall) * width + l for k in range(tall)]),
+    ):
+        rows = packets[0].shape[0]
+        for packet, place in zip(packets, places):
+            dest = place.astype(F32)
+            chosen = held[0][:rows, :]
             for other in held[1:]:
-                chosen = jnp.where(other[row : row + 1, :] == dest, other[lo:hi, :], chosen)
-            out[k][lo:hi, :] = chosen
+                chosen = jnp.where(other[rows : rows + 1, :] == dest, other[:rows, :], chosen)
+            packet[...] = chosen
 
 
 def pick_kernel(group, below, above, after, *refs, tall, width):
-    got, out = refs[:-1], refs[-1]
+    uppers, lowers, out = refs[:width], refs[width:-1], refs[-1]
     half = out.shape[0] // 2
-    h = group[0] // width
-    for f, nbr in enumerate((below, above)):
-        lo = half if f == 0 else 0
-        value = got[0][lo : lo + half, :]
-        for k in range(1, tall):
-            here = jnp.maximum(nbr[0], 0) // width == giver(h, k, tall)
-            value = jnp.where(here, got[k][lo : lo + half, :], value)
-        out[f * half : (f + 1) * half, :] = value
+    h, l = group[0] // width, lax.rem(group[0], width)
+    value = uppers[0][...]
+    for k in range(1, width):
+        here = lax.rem(jnp.maximum(below[0], 0), width) == giver(l, k, width)
+        value = jnp.where(here, uppers[k][...], value)
+    out[:half, :] = value
+    value = lowers[0][...]
+    for k in range(1, tall):
+        here = jnp.maximum(above[0], 0) // width == giver(h, k, tall)
+        value = jnp.where(here, lowers[k][...], value)
+    out[half:, :] = value
 
 
 def middle_kernel(own, below, above, after, near, tx, uy, mixing, *rest, parts):
     far, ahead = rest[:parts], rest[parts : 2 * parts]
-    packet, force, strip, spare = rest[2 * parts :]
+    upper, lower, force, strip, spare = rest[2 * parts :]
     gather_kx(spare, far, own[0])
     force_planes(spare, near, tx, uy, force)
     gather_kx(strip, ahead, own[0])
@@ -354,10 +357,10 @@
         strip[r * full : (r + 1) * full, :] = total
     at = pl.multiple_of(own[0] * slab, slab)
     for r in range(ROWS):
-        packet[r * slab : (r + 1) * slab, :] = strip[pl.ds(r * full + at, slab), :]
-    at = lax.broadcasted_iota(jnp.int32, (HEAD, packet.shape[1]), 0)
-    names = jnp.where(at < HEAD // 2, above[0], below[0])
-    packet[ROWS * slab :, :] = names.astype(F32)
+        packet = lower if r < FACE else upper
+        packet[r % FACE * slab : (r % FACE + 1) * slab, :] = strip[pl.ds(r * full + at, slab), :]
+    label(upper, above[0])
+    label(lower, below[0])
 
 
 def near_kernel(strip, vx, wy, near):
@@ -365,26 +368,13 @@
 
 
 def unforced_kernel(
-    extent, own, after, now, prev, consts, ystack, xparts, estack, hstack, gstack, *rest, full
+    extent, own, after, now, prev, ystack, xparts, *rest, full
 ):
     free, field = rest[:-1], rest[-1]
     slab, zcap, width = now.shape
     shape = (zcap, width)
     ext = extent[0]
-    kk = lax.broadcasted_iota(jnp.int32, (zcap, zcap), 1)
-    zz = lax.broadcasted_iota(jnp.int32, (zcap, zcap), 0)
-    lenf = jnp.full((zcap, zcap), ext.astype(F32))
-    ztable = scale_of(kk, lenf) * cosine_of(kk.astype(F32), 2.0 * zz.astype(F32) + 1.0, lenf)
-    ztable = jnp.where((kk < ext) & (zz < ext), ztable, 0.0)
-    zstack = stack_lanes(ztable, zcap)
-    face = face_rows(consts[6:7, :], consts[7:8, :], shape, ext)
-    terms = face * lane_series(consts, 24, len(SERIES), shape, ext)
-    depth = estack.shape[1] // 3
-    estack[...] = stack_lanes(terms, depth)
-    hstack[...] = stack_lanes(exact_dot(ztable, terms), depth)
-    terms = face * lane_series(consts, 40, len(DOUBLE), shape, ext)
-    gstack[...] = stack_lanes(exact_dot(ztable, terms), gstack.shape[1] // 3)
-
+    zstack = stack_lanes(z_table(ext, zcap), zcap)
     keep = lax.broadcasted_iota(jnp.int32, shape, 0) < ext
     square = plane_square(shape, ext)
     group = min(4, slab)
@@ -422,9 +412,20 @@
                 ]
 
 
-def between_kernel(extent, own, now, prev, force, rows, current, onward, *, full):
+def between_kernel(
+    extent, own, now, prev, force, rows, consts, current, onward, estack, hstack, gstack, *, full
+):
     slab, zcap, width = now.shape
     shape = (zcap, width)
+    ext = extent[0]
+    ztable = z_table(ext, zcap)
+    face = face_rows(consts[6:7, :], consts[7:8, :], shape, ext)
+    terms = face * lane_series(consts, 24, len(SERIES), shape, ext)
+    depth = estack.shape[1] // 3
+    estack[...] = stack_lanes(terms, depth)
+    hstack[...] = stack_lanes(exact_dot(ztable, terms), depth)
+    terms = face * lane_series(consts, 40, len(DOUBLE), shape, ext)
+    gstack[...] = stack_lanes(exact_dot(ztable, terms), gstack.shape[1] // 3)
     keep = lax.broadcasted_iota(jnp.int32, shape, 0) < extent[0]
     square = plane_square(shape, extent[0])
     weights = [jnp.broadcast_to(rows[:, r : r + 1], shape) for r in range(ROWS)]
@@ -450,32 +451,37 @@
     lax.fori_loop(0, slab // group, body, 0)
 
 
-def lift(force, across, table, ystack, given, terms, turned, pressure, count):
-    zcap = table.shape[0]
-    depth = table.shape[1] // 3
-    used = count * ROWS
+def series_planes(force, terms, count):
     full, width = force.shape[0] // ROWS, force.shape[1]
-    slab = across.shape[0]
     ax = lax.broadcasted_iota(jnp.int32, (full, width), 0).astype(F32) / full
     ay = lax.broadcasted_iota(jnp.int32, (full, width), 1).astype(F32) / width
     square = BASE * (ax * ax + ay * ay) - BASE
-    if terms is not None:
-        terms[used * full :, :] = jnp.zeros(((depth - used) * full, width), F32)
-    turned[used * slab :, :] = jnp.zeros(((depth - used) * slab, width), F32)
     planes = [plane(force, r) for r in range(ROWS)]
     for n in range(count):
         if n:
             planes = [value * square for value in planes]
-        for r in range(0, ROWS, 2):
-            at = n * ROWS + r
-            if terms is not None:
-                for half in range(2):
-                    terms[(at + half) * full : (at + half + 1) * full, :] = planes[r + half]
-            wide = dot(across, tall_split(jnp.concatenate(planes[r : r + 2], axis=1)))
-            for half in range(2):
-                turned[(at + half) * slab : (at + half + 1) * slab, :] = wide[
-                    :, half * width : (half + 1) * width
-                ]
+        for r in range(ROWS):
+            at = (n * ROWS + r) * full
+            terms[at : at + full, :] = planes[r]
+    used = count * ROWS * full
+    if used < terms.shape[0]:
+        terms[used:, :] = jnp.zeros((terms.shape[0] - used, width), F32)
+
+
+def lift(terms, across, table, ystack, given, turned, pressure, count, done):
+    zcap = table.shape[0]
+    depth = table.shape[1] // 3
+    used = count * ROWS
+    full, width = across.shape[1] // 3, terms.shape[1]
+    slab = across.shape[0]
+    turned[used * slab :, :] = jnp.zeros(((depth - used) * slab, width), F32)
+    for at in range(0, used, 2):
+        pair = [terms[(at + half) * full : (at + half + 1) * full, :] for half in range(2)]
+        wide = dot(across, tall_split(jnp.concatenate(pair, axis=1)))
+        for half in range(2):
+            turned[(at + half) * slab : (at + half + 1) * slab, :] = wide[
+                :, half * width : (half + 1) * width
+            ]
     block = ROWS * slab
     for n in range(count):
         span = slice(n * block, (n + 1) * block)
@@ -489,26 +495,49 @@
             for piece in given:
                 value = value + piece[span, :]
             pressure[span, :] = value
-
-
-def first_kernel(own, force, gstack, ystack, xown, free, summed, turned):
-    lift(force, xown[own[0]], gstack, ystack, [free], None, turned, summed, DOUBLE_TERMS)
+        done(i + 2)
+
+
+def first_kernel(own, force, gstack, ystack, xown, free, summed, terms, turned):
+    series_planes(force, terms, DOUBLE_TERMS)
+    lift(
+        terms, xown[own[0]], gstack, ystack, [free], turned, summed, DOUBLE_TERMS, lambda i: None
+    )
 
 
 def last_kernel(own, near, tx, uy, onward, estack, hstack, ystack, xown, *rest, full, parts):
     far, given = rest[:parts], rest[parts : 2 * parts]
-    modes, pressure, spare, force, terms, turned = rest[2 * parts :]
+    modes_out, pressure_out, modes, pressure, spare, force, terms, turned, sems = rest[2 * parts :]
     slab, zcap, width = onward.shape
     depth = estack.shape[1] // 3
     gather_kx(spare, far, own[0])
     force_planes(spare, near, tx, uy, force)
-    lift(force, xown[own[0]], hstack, ystack, given, terms, turned, pressure, TERMS)
+    sends = []
+
+    def send(source, target, at, size):
+        span = pl.ds(at, size)
+        sends.append(
+            pltpu.make_async_copy(source.at[span], target.at[span], sems.at[len(sends)])
+        )
+        sends[-1].start()
+
+    series_planes(force, terms, TERMS)
     own_at = own[0] * slab
     for i in range(0, slab, 2):
         pair = [terms[pl.ds(own_at + i + half, depth, stride=full), :] for half in range(2)]
         wide = dot(estack[...], tall_split(jnp.concatenate(pair, axis=1)))
         for half in range(2):
             modes[i + half] = onward[i + half] + wide[:, half * width : (half + 1) * width]
+        if (i + 2) % CHUNK == 0:
+            send(modes, modes_out, i + 2 - CHUNK, CHUNK)
+
+    def done(i):
+        if i % CHUNK == 0:
+            send(pressure, pressure_out, (i - CHUNK) * zcap, CHUNK * zcap)
+
+    lift(terms, xown[own[0]], hstack, ystack, given, turned, pressure, TERMS, done)
+    for copy in sends:
+        copy.wait()
 
 
 def on_device(modes_now, modes_prev, z_extent, lower_nbr, upper_nbr, x_shift, y_shift):
@@ -581,67 +610,61 @@
             got.append(lax.ppermute(piece, "split", [(i, (i + k) % parts) for i in range(parts)]))
         return got
 
-    def spread(packet):
-        held = [packet]
-        for k in range(1, inner):
-            to = [(i, i // inner * inner + partner(i % inner, k, inner)) for i in range(count)]
-            held.append(lax.ppermute(packet, "dom", to))
-        return held
+    face = FACE * slab
+    fast = lambda k: [(i, i // inner * inner + partner(i % inner, k, inner)) for i in range(count)]
+    slow = lambda k: [(i, partner(i // inner, k, tall) * inner + i % inner) for i in range(count)]
+
+    def spread(upper, lower):
+        uppers = [upper] + [lax.ppermute(upper, "dom", slow(k)) for k in range(1, tall)]
+        lowers = [lower] + [lax.ppermute(lower, "dom", fast(k)) for k in range(1, inner)]
+        return uppers + lowers
 
     def choose(held, after):
         return call(
-            functools.partial(choose_kernel, width=inner),
-            [shape_of(size, width)] * tall,
-            [SMEM, ANY] + [VMEM] * inner,
+            functools.partial(choose_kernel, tall=tall, width=inner),
+            [shape_of(face, width)] * (inner + tall),
+            [SMEM, ANY] + [VMEM] * (inner + tall),
             flops=COVER,
             moved=8 * size * width * 4,
             name="choose",
         )(group, after, *held)
 
     def deliver(chosen, after):
-        got = [chosen[0]]
-        for k in range(1, tall):
-            to = [(i, partner(i // inner, k, tall) * inner + i % inner) for i in range(count)]
-            got.append(lax.ppermute(chosen[k], "dom", to))
+        uppers, lowers = chosen[:inner], chosen[inner:]
+        got = [uppers[0]] + [lax.ppermute(uppers[k], "dom", fast(k)) for k in range(1, inner)]
+        got += [lowers[0]] + [lax.ppermute(lowers[k], "dom", slow(k)) for k in range(1, tall)]
         picked = call(
             functools.partial(pick_kernel, tall=tall, width=inner),
             [shape_of(size, width)],
-            [SMEM] * 3 + [ANY] + [VMEM] * tall,
+            [SMEM] * 3 + [ANY] + [VMEM] * (inner + tall),
             moved=5 * size * width * 4,
             name="pick",
         )(group, lower_nbr, upper_nbr, after, *got)[0]
         return swap(picked)
 
-    packet, rows = call(
+    strip, upper, lower, rows = call(
         strip_kernel,
-        [shape_of(size + HEAD, width), shape_of(zcap, width)],
-        [SMEM] * 3 + [HBM],
-        scratch=[
-            pltpu.VMEM((slab, zcap, width), F32),
-            pltpu.SemaphoreType.DMA((slab // CHUNK,)),
+        [
+            shape_of(size, width),
+            shape_of(face + HEAD, width),
+            shape_of(face + HEAD, width),
+            shape_of(zcap, width),
         ],
+        [SMEM] * 3 + [VMEM],
         moved=big,
         name="strip",
-        limit=WIDE,
     )(z_extent, lower_nbr, upper_nbr, modes_now)
-    held = spread(packet)
-
+    held = spread(upper, lower)
     ahead, coefs = call(
         functools.partial(ahead_kernel, full=full),
         [shape_of(size, width), shape_of(16, width)],
-        [SMEM] * 2 + [HBM] * 2 + [VMEM] * 2,
-        scratch=[
-            pltpu.VMEM((slab, zcap, width), F32),
-            pltpu.VMEM((slab, zcap, width), F32),
-            pltpu.SemaphoreType.DMA((2, slab // CHUNK)),
-        ],
+        [SMEM] * 2 + [VMEM] * 4,
         flops=10**8,
         moved=2 * big,
         name="ahead",
-        limit=WIDE,
     )(z_extent, own, modes_now, modes_prev, rows, consts)
     chosen = choose(held, ahead)
-    mine = swap(packet[:size])
+    mine = swap(strip)
     aheads = swap(ahead)
 
     tx, uy, vx, wy, near1, mixing, _ = call(
@@ -662,29 +685,25 @@
     )(lower_nbr, upper_nbr, x_shift, y_shift, own, coefs, chosen[0], xtall, ytall, *mine)
     far1 = deliver(chosen, near1)
 
-    estack, hstack, gstack, *free = call(
+    free = call(
         functools.partial(unforced_kernel, full=full),
-        [
-            shape_of(zcap, 3 * depth, dtype=BF16),
-            shape_of(zcap, 3 * depth, dtype=BF16),
-            shape_of(zcap, 3 * double_depth, dtype=BF16),
-        ]
-        + [shape_of(slab * zcap, width)] * parts,
-        [SMEM] * 2 + [ANY] + [VMEM] * 5,
+        [shape_of(slab * zcap, width)] * parts,
+        [SMEM] * 2 + [ANY] + [VMEM] * 4,
         scratch=[pltpu.VMEM((slab * zcap, width), F32)],
         flops=10**9,
         moved=4 * big,
         name="unforced",
-    )(z_extent, own, far1[0], modes_now, modes_prev, consts, ystack, xparts)
+    )(z_extent, own, far1[0], modes_now, modes_prev, ystack, xparts)
     given = [
         lax.ppermute(free[k], "split", [(i, (i + k) % parts) for i in range(parts)])
         for k in range(1, parts)
     ]
 
-    packet2, force1, strip2 = call(
+    upper2, lower2, force1, strip2 = call(
         functools.partial(middle_kernel, parts=parts),
         [
-            shape_of(size + HEAD, width),
+            shape_of(face + HEAD, width),
+            shape_of(face + HEAD, width),
             shape_of(ROWS * full, width),
             shape_of(ROWS * full, width),
         ],
@@ -693,22 +712,31 @@
         flops=10**8,
         moved=2 * big,
         name="middle",
-    )(own, lower_nbr, upper_nbr, estack, near1, tx, uy, mixing, *far1, *aheads)
-
-    current, onward = call(
+    )(own, lower_nbr, upper_nbr, free[0], near1, tx, uy, mixing, *far1, *aheads)
+
+    current, onward, estack, hstack, gstack = call(
         functools.partial(between_kernel, full=full),
-        [shape_of(slab, zcap, width)] * 2,
-        [SMEM] * 2 + [VMEM] * 4,
+        [
+            shape_of(slab, zcap, width),
+            shape_of(slab, zcap, width),
+            shape_of(zcap, 3 * depth, dtype=BF16),
+            shape_of(zcap, 3 * depth, dtype=BF16),
+            shape_of(zcap, 3 * double_depth, dtype=BF16),
+        ],
+        [SMEM] * 2 + [VMEM] * 5,
         flops=10**9,
         moved=4 * big,
         name="between",
-    )(z_extent, own, modes_now, modes_prev, force1, rows)
-    chosen2 = choose(spread(packet2), onward)
+    )(z_extent, own, modes_now, modes_prev, force1, rows, consts)
+    chosen2 = choose(spread(upper2, lower2), onward)
     summed = call(
         first_kernel,
         [shape_of(slab * zcap, width)],
         [SMEM] + [VMEM] * 5,
-        scratch=[pltpu.VMEM((double_depth * slab, width), F32)],
+        scratch=[
+            pltpu.VMEM((DOUBLE_TERMS * ROWS * full, width), F32),
+            pltpu.VMEM((double_depth * slab, width), F32),
+        ],
         flops=10**9,
         moved=2 * big,
         name="first",
@@ -727,14 +755,18 @@
         [shape_of(slab, zcap, width), shape_of(slab * zcap, width)],
         [SMEM] + [VMEM] * (8 + 2 * parts),
         scratch=[
+            pltpu.VMEM((slab, zcap, width), F32),
+            pltpu.VMEM((slab * zcap, width), F32),
             pltpu.VMEM((ROWS * full, width), F32),
             pltpu.VMEM((ROWS * full, width), F32),
             pltpu.VMEM((depth * full, width), F32),
             pltpu.VMEM((depth * slab, width), F32),
+            pltpu.SemaphoreType.DMA((2 * (slab // CHUNK),)),
         ],
         flops=10**9,
         moved=6 * big,
         name="last",
+        out=HBM,
     )(
         own, near2, tx, uy, onward, estack, hstack, ystack, xown,
         *deliver(chosen2, summed), summed, *given,

time: 68.7 us -> 77.9 us (1.13)
  starting transfers between devices: 19.2 us -> 34 us
  Pallas kernels: 24.6 us -> 19.4 us
  waiting for transfers between devices: 20.5 us -> 18 us
  local copies, waits for them, and re-layouts: 1.16 us -> 3.25 us
    ppermute x12 -> x24, starting transfers between devices: 13.9 us -> 27.5 us  [the longest x6 10.2 us: spread(): lax.ppermute(upper, 'dom', slow(k))]
    ppermute x12 -> x24, waiting for transfers between devices: 13 us -> 3.74 us  [the longest x6 3.67 us: deliver(): lax.ppermute(lowers[k], 'dom', slow(k))]
    ppermute x4, waiting for transfers between devices: 7.58 us -> 14.3 us  [swap(): lax.ppermute(piece, 'split', [(i, (i + k) % parts) for i in range(parts)])]
    unnamed x26, local copies, waits for them, and re-layouts: 0.23 us -> 3.25 us
    pallas_call x5, Pallas kernels: 9.45 us -> 6.61 us  [the longest x1 4.88 us: on_device(): call(functools.partial(unforced_kernel, full=full), [shape_of(slab * zcap...]
    pallas_call x1, Pallas kernels: 4.24 us -> 1.72 us  [on_device(): call(functools.partial(ahead_kernel, full=full), [shape_of(size, width),...]
    ppermute x4, starting transfers between devices: 4.02 us -> 5.54 us  [swap(): lax.ppermute(piece, 'split', [(i, (i + k) % parts) for i in range(parts)])]
    slice x1 -> x0, local copies, waits for them, and re-layouts: 0.93 us -> none  [on_device(): mine = swap(packet[:size])]
  transfers between devices with their start and end apart: 17 -> 29, of which waited for: 4 -> 4; matrix products, arithmetic and copies ran while one was open for 1% -> 0% of each run, Pallas kernels for 25% -> 18%
where the time goes in v4:
time: 77.9 us; the launch traced here: 77.6 us
  starting transfers between devices  34 us (44%)
  Pallas kernels  19.4 us (25%)
  waiting for transfers between devices  18 us (23%)
  local copies, waits for them, and re-layouts  3.25 us (4%)
  between operations  2.95 us (4%)
    ppermute x4, waiting for transfers between devices, swap(): lax.ppermute(piece, 'split', [(i, (i + k) % parts) for i in range(parts)])  14.3 us
    ppermute x6, starting transfers between devices, spread(): lax.ppermute(upper, 'dom', slow(k))  10.2 us
    ppermute x6, starting transfers between devices, deliver(): lax.ppermute(lowers[k], 'dom', slow(k))  9.76 us
    ppermute x4, starting transfers between devices, swap(): lax.ppermute(piece, 'split', [(i, (i + k) % parts) for i in range(parts)])  5.54 us
    pallas_call x1, Pallas kernels, on_device(): call(functools.partial(unforced_kernel, full=full), [shape_of(slab * zcap...  4.88 us
    ppermute x6, starting transfers between devices, deliver(): lax.ppermute(uppers[k], 'dom', fast(k))  3.86 us
    ppermute x6, starting transfers between devices, spread(): lax.ppermute(lower, 'dom', fast(k))  3.7 us
    ppermute x6, waiting for transfers between devices, deliver(): lax.ppermute(lowers[k], 'dom', slow(k))  3.67 us
  transfers between devices with their start and end apart: 29, of which 4 were waited for; matrix products, arithmetic and copies ran while one was open for 0% of the time, Pallas kernels for 18%

profile of v4, /device:TPU:0, one launch (start us, length us, event | category | flops | bytes accessed | tf_op | source)
XLA Modules:
  0.0 77.6 jit_solution(15718720458151926272)
XLA Ops:
  2.6 1.2 %copy-done = f32[32,64,128]{2,1,0:T(8,128)S(1)} copy-done((f32[32,64,128]{2,1,0:T(8,128)S(1)}, f32[32,64,128]{2,1,0:T(8,128)}, u32[]{:S(2)}) %copy-start) | copy-done | bytes 1048600
  4.6 5.1 %collective-permute-start.2 = (f32[104,128]{1,0:T(8,128)S(1)}, f32[104,128]{1,0:T(8,128)S(1)}, u32[]{:S(2)}, u32[]{:S(2)}) collective-permute-start(f32[104,128]{1,0:T(8,128)S(1)} %get-tuple-element.47.refs_0_), channel_id=1, source_target_pairs={{0,24},{2,26},{4,28},{6,30},{8,16},{10,18},{12,20},{14,22},{16,8},... | collective-permute-start | bytes 159752 | tf_op jit(solution)/shard_map/ppermute | solution.py:618
  10.8 1.3 %collective-permute-start.4 = (f32[104,128]{1,0:T(8,128)S(1)}, f32[104,128]{1,0:T(8,128)S(1)}, u32[]{:S(2)}, u32[]{:S(2)}) collective-permute-start(f32[104,128]{1,0:T(8,128)S(1)} %get-tuple-element.48.refs_4_), channel_id=1, source_target_pairs={{0,4},{2,6},{4,0},{6,2},{8,12},{10,14},{12,8},{14,10},{16,20},{18,... | collective-permute-start | bytes 159752 | tf_op jit(solution)/shard_map/ppermute | solution.py:619
  12.3 1.2 %copy-done.2 = f32[32,64,128]{2,1,0:T(8,128)S(1)} copy-done((f32[32,64,128]{2,1,0:T(8,128)S(1)}, f32[32,64,128]{2,1,0:T(8,128)}, u32[]{:S(2)}) %copy-start.2) | copy-done | bytes 1048600
  14.2 1.7 %ahead.1 = (f32[192,128]{1,0:T(8,128)S(1)}, f32[16,128]{1,0:T(8,128)S(1)}) custom-call(s32[1]{0:T(128)S(6)} %copy.16.extent, s32[1]{0:T(128)} %bitcast.own, f32[32,64,128]{2,1,0:T(8,128)S(1)} %copy-done.1, f32[32,64,128]{2,1,0:T(8,128)S(1)} %copy-done.2, f32[64,128]{1,0:T(8,128)S(1)} %get-tuple-element.44.rows, f32[56,128]{1,0:T(8,128)S(1)} %copy-done.8), custom_call_target="tpu_custom_call" | custom-call | flops 100000000 | bytes 2097152 | tf_op jit(solution)/shard_map/ahead/pallas_call | solution.py:658
  16.0 1.8 %collective-permute-start.6 = (f32[192,128]{1,0:T(8,128)S(1)}, f32[192,128]{1,0:T(8,128)S(1)}, u32[]{:S(2)}, u32[]{:S(2)}) collective-permute-start(f32[192,128]{1,0:T(8,128)S(1)} %get-tuple-element.50.rest_0_), channel_id=1, source_target_pairs={{0,1},{1,0},{2,3},{3,2},{4,5},{5,4},{6,7},{7,6},{8,9},{9,8},{10,11... | collective-permute-start | bytes 294920 | tf_op jit(solution)/shard_map/ppermute | solution.py:610
  18.2 1.5 %collective-permute-start.8 = (f32[96,128]{1,0:T(8,128)S(1)}, f32[96,128]{1,0:T(8,128)S(1)}, u32[]{:S(2)}, u32[]{:S(2)}) collective-permute-start(f32[96,128]{1,0:T(8,128)S(1)} %get-tuple-element.53), channel_id=1, source_target_pairs={{0,4},{2,6},{4,0},{6,2},{8,12},{10,14},{12,8},{14,10},{16,20},{18,... | collective-permute-start | bytes 147464 | tf_op jit(solution)/shard_map/ppermute | solution.py:634
  19.8 1.2 %collective-permute-start.10 = (f32[96,128]{1,0:T(8,128)S(1)}, f32[96,128]{1,0:T(8,128)S(1)}, u32[]{:S(2)}, u32[]{:S(2)}) collective-permute-start(f32[96,128]{1,0:T(8,128)S(1)} %get-tuple-element.56), channel_id=1, source_target_pairs={{0,8},{2,10},{4,12},{6,14},{8,0},{10,2},{12,4},{14,6},{16,24},{18,... | collective-permute-start | bytes 147464 | tf_op jit(solution)/shard_map/ppermute | solution.py:635
  21.2 3.1 %collective-permute-start.11 = (f32[96,128]{1,0:T(8,128)S(1)}, f32[96,128]{1,0:T(8,128)S(1)}, u32[]{:S(2)}, u32[]{:S(2)}) collective-permute-start(f32[96,128]{1,0:T(8,128)S(1)} %get-tuple-element.57), channel_id=1, source_target_pairs={{0,16},{2,18},{4,20},{6,22},{8,24},{10,26},{12,28},{14,30},{16,0},... | collective-permute-start | bytes 147464 | tf_op jit(solution)/shard_map/ppermute | solution.py:635
  25.4 2.0 %relation.1 = (f32[2,64,64]{2,1,0:T(8,128)S(1)}, f32[2,128,128]{2,1,0:T(8,128)S(1)}, f32[2,64,64]{2,1,0:T(8,128)S(1)}, f32[2,128,128]{2,1,0:T(8,128)S(1)}, f32[3...) custom-call(s32[1]{0:T(128)S(6)} %copy.17.below, s32[1]{0:T(128)S(6)} %copy.18.above, ...), custom_call_target="tpu_custom_call" | custom-call | flops 100000000 | bytes 2097152 | tf_op jit(solution)/shard_map/relation/pallas_call | solution.py:670
  27.4 1.5 %collective-permute-start.14 = (f32[192,128]{1,0:T(8,128)S(1)}, f32[192,128]{1,0:T(8,128)S(1)}, u32[]{:S(2)}, u32[]{:S(2)}) collective-permute-start(f32[192,128]{1,0:T(8,128)S(1)} %get-tuple-element.46.after.rest_2_), channel_id=1, source_target_pairs={{0,1},{1,0},{2,3},{3,2},{4,5},{5,4},{6,7},{7,6},{8,9},{9,8},{10,11... | collective-permute-start | bytes 294920 | tf_op jit(solution)/shard_map/ppermute | solution.py:610
  29.0 1.3 %collective-permute-done.12.refs_7_ = f32[96,128]{1,0:T(8,128)S(1)} collective-permute-done((f32[96,128]{1,0:T(8,128)S(1)}, f32[96,128]{1,0:T(8,128)S(1)}, u32[]{:S(2)}, u32[]{:S(2)}) %collective-permute-start.12) | collective-permute-done | bytes 49184 | tf_op jit(solution)/shard_map/ppermute | solution.py:635
  31.5 4.9 %unforced.1 = (f32[2048,128]{1,0:T(8,128)S(1)}, f32[2048,128]{1,0:T(8,128)S(1)}) custom-call(s32[1]{0:T(128)S(6)} %copy.16.extent, s32[1]{0:T(128)} %bitcast.own, f32[192,128]{1,0:T(8,128)S(1)} %pick.2.after.rest_0_, f32[32,64,128]{2,1,0:T(8,128)S(1)} %copy-done.1, f32[32,64,128]{2,1,0:T(8,128)S(1)} %copy-done.3, bf16[256,256]{1,0:T(8,128)(2,1)S(1)} %copy-done.5, ...), custom_call_target="tpu_custom_call" | custom-call | flops 1000000000 | bytes 4194304 | tf_op jit(solution)/shard_map/unforced/pallas_call | solution.py:688
  37.1 2.0 %collective-permute-start.17 = (f32[104,128]{1,0:T(8,128)S(1)}, f32[104,128]{1,0:T(8,128)S(1)}, u32[]{:S(2)}, u32[]{:S(2)}) collective-permute-start(f32[104,128]{1,0:T(8,128)S(1)} %get-tuple-element.71.refs_0_), channel_id=1, source_target_pairs={{0,24},{2,26},{4,28},{6,30},{8,16},{10,18},{12,20},{14,22},{16,8},... | collective-permute-start | bytes 159752 | tf_op jit(solution)/shard_map/ppermute | solution.py:618
  39.4 2.2 %collective-permute-start.15 = (f32[104,128]{1,0:T(8,128)S(1)}, f32[104,128]{1,0:T(8,128)S(1)}, u32[]{:S(2)}, u32[]{:S(2)}) collective-permute-start(f32[104,128]{1,0:T(8,128)S(1)} %get-tuple-element.71.refs_0_), channel_id=1, source_target_pairs={{0,8},{2,10},{4,12},{6,14},{8,0},{10,2},{12,4},{14,6},{16,24},{18,... | collective-permute-start | bytes 159752 | tf_op jit(solution)/shard_map/ppermute | solution.py:618
  41.6 1.5 %collective-permute-start.19 = (f32[104,128]{1,0:T(8,128)S(1)}, f32[104,128]{1,0:T(8,128)S(1)}, u32[]{:S(2)}, u32[]{:S(2)}) collective-permute-start(f32[104,128]{1,0:T(8,128)S(1)} %get-tuple-element.72.refs_4_), channel_id=1, source_target_pairs={{0,4},{2,6},{4,0},{6,2},{8,12},{10,14},{12,8},{14,10},{16,20},{18,... | collective-permute-start | bytes 159752 | tf_op jit(solution)/shard_map/ppermute | solution.py:619
  43.5 3.2 %between.1 = (f32[32,64,128]{2,1,0:T(8,128)}, f32[32,64,128]{2,1,0:T(8,128)S(1)}, bf16[64,144]{1,0:T(8,128)(2,1)S(1)}, bf16[64,144]{1,0:T(8,128)(2,1)S(1)}, bf16[64,192]{1,0:T(8,128)(2,1)S(1)}) custom-call(s32[1]{0:T(128)S(6)} %copy.16.extent, s32[1]{0:T(128)} %bitcast.own, f32[32,64,128]{2,1,0:T(8,128)S(1)} %copy-done.1, f32[32,64,128]{2,1,0:T(8,128)S(1)} %copy-done.3, ...), custom_call_target="tpu_custom_call" | custom-call | flops 1000000000 | bytes 4194304 | tf_op jit(solution)/shard_map/between/pallas_call | solution.py:717
  47.7 1.6 %collective-permute-start.22 = (f32[96,128]{1,0:T(8,128)S(1)}, f32[96,128]{1,0:T(8,128)S(1)}, u32[]{:S(2)}, u32[]{:S(2)}) collective-permute-start(f32[96,128]{1,0:T(8,128)S(1)} %get-tuple-element.75), channel_id=1, source_target_pairs={{0,4},{2,6},{4,0},{6,2},{8,12},{10,14},{12,8},{14,10},{16,20},{18,... | collective-permute-start | bytes 147464 | tf_op jit(solution)/shard_map/ppermute | solution.py:634
  49.6 2.6 %collective-permute-start.25 = (f32[96,128]{1,0:T(8,128)S(1)}, f32[96,128]{1,0:T(8,128)S(1)}, u32[]{:S(2)}, u32[]{:S(2)}) collective-permute-start(f32[96,128]{1,0:T(8,128)S(1)} %get-tuple-element.79), channel_id=1, source_target_pairs={{0,16},{2,18},{4,20},{6,22},{8,24},{10,26},{12,28},{14,30},{16,0},... | collective-permute-start | bytes 147464 | tf_op jit(solution)/shard_map/ppermute | solution.py:635
  52.2 1.8 %collective-permute-start.26 = (f32[96,128]{1,0:T(8,128)S(1)}, f32[96,128]{1,0:T(8,128)S(1)}, u32[]{:S(2)}, u32[]{:S(2)}) collective-permute-start(f32[96,128]{1,0:T(8,128)S(1)} %get-tuple-element.80), channel_id=1, source_target_pairs={{0,24},{2,26},{4,28},{6,30},{8,16},{10,18},{12,20},{14,22},{16,8},... | collective-permute-start | bytes 147464 | tf_op jit(solution)/shard_map/ppermute | solution.py:635
  54.0 1.7 %first.1.after.rest_2_ = f32[2048,128]{1,0:T(8,128)S(1)} custom-call(s32[1]{0:T(128)} %bitcast.own, f32[384,128]{1,0:T(8,128)S(1)} %get-tuple-element.66.force, bf16[64,192]{1,0:T(8,128)(2,1)S(1)} %get-tuple-element.70.gstack, bf16[256,256]{1,0:T(8,128)(2,1)S(1)} %copy-done.5, bf16[2,32,192]{2,1,0:T(8,128)(2,1)S(1)} %copy-done.7, ...), custom_call_target="tpu_custom_call" | custom-call | flops 1000000000 | bytes 2097152 | tf_op jit(solution)/shard_map/first/pallas_call | solution.py:732
  55.7 2.3 %collective-permute-done.26.refs_7_ = f32[96,128]{1,0:T(8,128)S(1)} collective-permute-done((f32[96,128]{1,0:T(8,128)S(1)}, f32[96,128]{1,0:T(8,128)S(1)}, u32[]{:S(2)}, u32[]{:S(2)}) %collective-permute-start.26) | collective-permute-done | bytes 49184 | tf_op jit(solution)/shard_map/ppermute | solution.py:635
  59.8 14.1 %collective-permute-done.27.rest_1_ = f32[192,128]{1,0:T(8,128)S(1)} collective-permute-done((f32[192,128]{1,0:T(8,128)S(1)}, f32[192,128]{1,0:T(8,128)S(1)}, u32[]{:S(2)}, u32[]{:S(2)}) %collective-permute-start.27) | collective-permute-done | bytes 98336 | tf_op jit(solution)/shard_map/ppermute | solution.py:610
  74.0 3.5 %last.1 = (f32[32,64,128]{2,1,0:T(8,128)}, f32[2048,128]{1,0:T(8,128)}) custom-call(s32[1]{0:T(128)} %bitcast.own, f32[384,128]{1,0:T(8,128)S(1)} %near.1, f32[2,64,64]{2,1,0:T(8,128)S(1)} %get-tuple-element.60.tx, f32[2,128,128]{2,1,0:T(8,128)S(1)} %get-tuple-element.61.uy, f32[32,64,128]{2,1,0:T(8,128)S(1)} %get-tuple-element.67.after.onward, ...), custom_call_target="tpu_custom_call" | custom-call | flops 1000000000 | bytes 6291456 | tf_op jit(solution)/shard_map/last/pallas_call | solution.py:753
  (73 shorter events, 10.3 us)
Async XLA Ops:
  4.6 7.4 %collective-permute-start.2 = (f32[104,128]{1,0:T(8,128)S(1)}, f32[104,128]{1,0:T(8,128)S(1)}, u32[]{:S(2)}, u32[]{:S(2)}) collective-permute-start(f32[104,128]{1,0:T(8,128)S(1)} %get-tuple-element.47.refs_0_), channel_id=1, source_target_pairs={{0,24},{2,26},{4,28},{6,30},{8,16},{10,18},{12,20},{14,22},{16,8},... | collective-permute-start | bytes 159752 | tf_op jit(solution)/shard_map/ppermute | solution.py:618
  9.8 6.2 %collective-permute-start.1 = (f32[104,128]{1,0:T(8,128)S(1)}, f32[104,128]{1,0:T(8,128)S(1)}, u32[]{:S(2)}, u32[]{:S(2)}) collective-permute-start(f32[104,128]{1,0:T(8,128)S(1)} %get-tuple-element.47.refs_0_), channel_id=1, source_target_pairs={{0,16},{2,18},{4,20},{6,22},{8,24},{10,26},{12,28},{14,30},{16,0},... | collective-permute-start | bytes 159752 | tf_op jit(solution)/shard_map/ppermute | solution.py:618
  9.8 8.0 %collective-permute-start = (f32[104,128]{1,0:T(8,128)S(1)}, f32[104,128]{1,0:T(8,128)S(1)}, u32[]{:S(2)}, u32[]{:S(2)}) collective-permute-start(f32[104,128]{1,0:T(8,128)S(1)} %get-tuple-element.47.refs_0_), channel_id=1, source_target_pairs={{0,8},{2,10},{4,12},{6,14},{8,0},{10,2},{12,4},{14,6},{16,24},{18,... | collective-permute-start | bytes 159752 | tf_op jit(solution)/shard_map/ppermute | solution.py:618
  10.4 7.4 %collective-permute-start.5 = (f32[104,128]{1,0:T(8,128)S(1)}, f32[104,128]{1,0:T(8,128)S(1)}, u32[]{:S(2)}, u32[]{:S(2)}) collective-permute-start(f32[104,128]{1,0:T(8,128)S(1)} %get-tuple-element.48.refs_4_), channel_id=1, source_target_pairs={{0,6},{2,4},{4,2},{6,0},{8,14},{10,12},{12,10},{14,8},{16,22},{18,... | collective-permute-start | bytes 159752 | tf_op jit(solution)/shard_map/ppermute | solution.py:619
  10.8 7.0 %collective-permute-start.4 = (f32[104,128]{1,0:T(8,128)S(1)}, f32[104,128]{1,0:T(8,128)S(1)}, u32[]{:S(2)}, u32[]{:S(2)}) collective-permute-start(f32[104,128]{1,0:T(8,128)S(1)} %get-tuple-element.48.refs_4_), channel_id=1, source_target_pairs={{0,4},{2,6},{4,0},{6,2},{8,12},{10,14},{12,8},{14,10},{16,20},{18,... | collective-permute-start | bytes 159752 | tf_op jit(solution)/shard_map/ppermute | solution.py:619
  17.9 6.4 %collective-permute-start.7 = (f32[96,128]{1,0:T(8,128)S(1)}, f32[96,128]{1,0:T(8,128)S(1)}, u32[]{:S(2)}, u32[]{:S(2)}) collective-permute-start(f32[96,128]{1,0:T(8,128)S(1)} %get-tuple-element.52), channel_id=1, source_target_pairs={{0,2},{2,0},{4,6},{6,4},{8,10},{10,8},{12,14},{14,12},{16,18},{18,... | collective-permute-start | bytes 147464 | tf_op jit(solution)/shard_map/ppermute | solution.py:634
  18.2 9.2 %collective-permute-start.8 = (f32[96,128]{1,0:T(8,128)S(1)}, f32[96,128]{1,0:T(8,128)S(1)}, u32[]{:S(2)}, u32[]{:S(2)}) collective-permute-start(f32[96,128]{1,0:T(8,128)S(1)} %get-tuple-element.53), channel_id=1, source_target_pairs={{0,4},{2,6},{4,0},{6,2},{8,12},{10,14},{12,8},{14,10},{16,20},{18,... | collective-permute-start | bytes 147464 | tf_op jit(solution)/shard_map/ppermute | solution.py:634
  19.7 9.2 %collective-permute-start.9 = (f32[96,128]{1,0:T(8,128)S(1)}, f32[96,128]{1,0:T(8,128)S(1)}, u32[]{:S(2)}, u32[]{:S(2)}) collective-permute-start(f32[96,128]{1,0:T(8,128)S(1)} %get-tuple-element.54), channel_id=1, source_target_pairs={{0,6},{2,4},{4,2},{6,0},{8,14},{10,12},{12,10},{14,8},{16,22},{18,... | collective-permute-start | bytes 147464 | tf_op jit(solution)/shard_map/ppermute | solution.py:634
  19.8 9.1 %collective-permute-start.10 = (f32[96,128]{1,0:T(8,128)S(1)}, f32[96,128]{1,0:T(8,128)S(1)}, u32[]{:S(2)}, u32[]{:S(2)}) collective-permute-start(f32[96,128]{1,0:T(8,128)S(1)} %get-tuple-element.56), channel_id=1, source_target_pairs={{0,8},{2,10},{4,12},{6,14},{8,0},{10,2},{12,4},{14,6},{16,24},{18,... | collective-permute-start | bytes 147464 | tf_op jit(solution)/shard_map/ppermute | solution.py:635
  21.2 7.7 %collective-permute-start.11 = (f32[96,128]{1,0:T(8,128)S(1)}, f32[96,128]{1,0:T(8,128)S(1)}, u32[]{:S(2)}, u32[]{:S(2)}) collective-permute-start(f32[96,128]{1,0:T(8,128)S(1)} %get-tuple-element.57), channel_id=1, source_target_pairs={{0,16},{2,18},{4,20},{6,22},{8,24},{10,26},{12,28},{14,30},{16,0},... | collective-permute-start | bytes 147464 | tf_op jit(solution)/shard_map/ppermute | solution.py:635
  24.3 5.9 %collective-permute-start.12 = (f32[96,128]{1,0:T(8,128)S(1)}, f32[96,128]{1,0:T(8,128)S(1)}, u32[]{:S(2)}, u32[]{:S(2)}) collective-permute-start(f32[96,128]{1,0:T(8,128)S(1)} %get-tuple-element.58), channel_id=1, source_target_pairs={{0,24},{2,26},{4,28},{6,30},{8,16},{10,18},{12,20},{14,22},{16,8},... | collective-permute-start | bytes 147464 | tf_op jit(solution)/shard_map/ppermute | solution.py:635
  27.4 9.0 %collective-permute-start.14 = (f32[192,128]{1,0:T(8,128)S(1)}, f32[192,128]{1,0:T(8,128)S(1)}, u32[]{:S(2)}, u32[]{:S(2)}) collective-permute-start(f32[192,128]{1,0:T(8,128)S(1)} %get-tuple-element.46.after.rest_2_), channel_id=1, source_target_pairs={{0,1},{1,0},{2,3},{3,2},{4,5},{5,4},{6,7},{7,6},{8,9},{9,8},{10,11... | collective-permute-start | bytes 294920 | tf_op jit(solution)/shard_map/ppermute | solution.py:610
  30.3 6.1 %collective-permute-start.13 = (f32[192,128]{1,0:T(8,128)S(1)}, f32[192,128]{1,0:T(8,128)S(1)}, u32[]{:S(2)}, u32[]{:S(2)}) collective-permute-start(f32[192,128]{1,0:T(8,128)S(1)} %pick.2.after.rest_0_), channel_id=1, source_target_pairs={{0,1},{1,0},{2,3},{3,2},{4,5},{5,4},{6,7},{7,6},{8,9},{9,8},{10,11... | collective-permute-start | bytes 294920 | tf_op jit(solution)/shard_map/ppermute | solution.py:610
  37.1 6.0 %collective-permute-start.17 = (f32[104,128]{1,0:T(8,128)S(1)}, f32[104,128]{1,0:T(8,128)S(1)}, u32[]{:S(2)}, u32[]{:S(2)}) collective-permute-start(f32[104,128]{1,0:T(8,128)S(1)} %get-tuple-element.71.refs_0_), channel_id=1, source_target_pairs={{0,24},{2,26},{4,28},{6,30},{8,16},{10,18},{12,20},{14,22},{16,8},... | collective-permute-start | bytes 159752 | tf_op jit(solution)/shard_map/ppermute | solution.py:618
  39.1 7.5 %collective-permute-start.16 = (f32[104,128]{1,0:T(8,128)S(1)}, f32[104,128]{1,0:T(8,128)S(1)}, u32[]{:S(2)}, u32[]{:S(2)}) collective-permute-start(f32[104,128]{1,0:T(8,128)S(1)} %get-tuple-element.71.refs_0_), channel_id=1, source_target_pairs={{0,16},{2,18},{4,20},{6,22},{8,24},{10,26},{12,28},{14,30},{16,0},... | collective-permute-start | bytes 159752 | tf_op jit(solution)/shard_map/ppermute | solution.py:618
  39.4 8.2 %collective-permute-start.15 = (f32[104,128]{1,0:T(8,128)S(1)}, f32[104,128]{1,0:T(8,128)S(1)}, u32[]{:S(2)}, u32[]{:S(2)}) collective-permute-start(f32[104,128]{1,0:T(8,128)S(1)} %get-tuple-element.71.refs_0_), channel_id=1, source_target_pairs={{0,8},{2,10},{4,12},{6,14},{8,0},{10,2},{12,4},{14,6},{16,24},{18,... | collective-permute-start | bytes 159752 | tf_op jit(solution)/shard_map/ppermute | solution.py:618
  41.6 6.0 %collective-permute-start.20 = (f32[104,128]{1,0:T(8,128)S(1)}, f32[104,128]{1,0:T(8,128)S(1)}, u32[]{:S(2)}, u32[]{:S(2)}) collective-permute-start(f32[104,128]{1,0:T(8,128)S(1)} %get-tuple-element.72.refs_4_), channel_id=1, source_target_pairs={{0,6},{2,4},{4,2},{6,0},{8,14},{10,12},{12,10},{14,8},{16,22},{18,... | collective-permute-start | bytes 159752 | tf_op jit(solution)/shard_map/ppermute | solution.py:619
  41.6 6.0 %collective-permute-start.19 = (f32[104,128]{1,0:T(8,128)S(1)}, f32[104,128]{1,0:T(8,128)S(1)}, u32[]{:S(2)}, u32[]{:S(2)}) collective-permute-start(f32[104,128]{1,0:T(8,128)S(1)} %get-tuple-element.72.refs_4_), channel_id=1, source_target_pairs={{0,4},{2,6},{4,0},{6,2},{8,12},{10,14},{12,8},{14,10},{16,20},{18,... | collective-permute-start | bytes 159752 | tf_op jit(solution)/shard_map/ppermute | solution.py:619
  46.6 27.4 %collective-permute-start.28 = (f32[2048,128]{1,0:T(8,128)S(1)}, f32[2048,128]{1,0:T(8,128)S(1)}, u32[]{:S(2)}, u32[]{:S(2)}) collective-permute-start(f32[2048,128]{1,0:T(8,128)S(1)} %get-tuple-element.81), channel_id=1, source_target_pairs={{0,1},{1,0},{2,3},{3,2},{4,5},{5,4},{6,7},{7,6},{8,9},{9,8},{10,11... | collective-permute-start | bytes 3145736 | tf_op jit(solution)/shard_map/ppermute | solution.py:698
  49.3 6.4 %collective-permute-start.23 = (f32[96,128]{1,0:T(8,128)S(1)}, f32[96,128]{1,0:T(8,128)S(1)}, u32[]{:S(2)}, u32[]{:S(2)}) collective-permute-start(f32[96,128]{1,0:T(8,128)S(1)} %get-tuple-element.76), channel_id=1, source_target_pairs={{0,6},{2,4},{4,2},{6,0},{8,14},{10,12},{12,10},{14,8},{16,22},{18,... | collective-permute-start | bytes 147464 | tf_op jit(solution)/shard_map/ppermute | solution.py:634
  49.6 6.1 %collective-permute-start.24 = (f32[96,128]{1,0:T(8,128)S(1)}, f32[96,128]{1,0:T(8,128)S(1)}, u32[]{:S(2)}, u32[]{:S(2)}) collective-permute-start(f32[96,128]{1,0:T(8,128)S(1)} %get-tuple-element.78), channel_id=1, source_target_pairs={{0,8},{2,10},{4,12},{6,14},{8,0},{10,2},{12,4},{14,6},{16,24},{18,... | collective-permute-start | bytes 147464 | tf_op jit(solution)/shard_map/ppermute | solution.py:635
  49.6 6.1 %collective-permute-start.25 = (f32[96,128]{1,0:T(8,128)S(1)}, f32[96,128]{1,0:T(8,128)S(1)}, u32[]{:S(2)}, u32[]{:S(2)}) collective-permute-start(f32[96,128]{1,0:T(8,128)S(1)} %get-tuple-element.79), channel_id=1, source_target_pairs={{0,16},{2,18},{4,20},{6,22},{8,24},{10,26},{12,28},{14,30},{16,0},... | collective-permute-start | bytes 147464 | tf_op jit(solution)/shard_map/ppermute | solution.py:635
  52.2 5.9 %collective-permute-start.26 = (f32[96,128]{1,0:T(8,128)S(1)}, f32[96,128]{1,0:T(8,128)S(1)}, u32[]{:S(2)}, u32[]{:S(2)}) collective-permute-start(f32[96,128]{1,0:T(8,128)S(1)} %get-tuple-element.80), channel_id=1, source_target_pairs={{0,24},{2,26},{4,28},{6,30},{8,16},{10,18},{12,20},{14,22},{16,8},... | collective-permute-start | bytes 147464 | tf_op jit(solution)/shard_map/ppermute | solution.py:635
  58.1 15.9 %collective-permute-start.27 = (f32[192,128]{1,0:T(8,128)S(1)}, f32[192,128]{1,0:T(8,128)S(1)}, u32[]{:S(2)}, u32[]{:S(2)}) collective-permute-start(f32[192,128]{1,0:T(8,128)S(1)} %pick.3.rest_0_), channel_id=1, source_target_pairs={{0,1},{1,0},{2,3},{3,2},{4,5},{5,4},{6,7},{7,6},{8,9},{9,8},{10,11... | collective-permute-start | bytes 294920 | tf_op jit(solution)/shard_map/ppermute | solution.py:610
  (18 other events, 93.2 us)

commit v5 on v4

--- a/solution.py
+++ b/solution.py
@@ -59,10 +59,6 @@
     return (place + step) % count
 
 
-def giver(place, step, count):
-    return partner(place, step if count & (count - 1) == 0 else count - step, count)
-
-
 def tall_split(data):
     high = data.astype(BF16).astype(F32)
     return jnp.concatenate([high, high, data - high], axis=0).astype(BF16)
@@ -154,8 +150,8 @@
 
 def gather_kx(out, pieces, own):
     count = len(pieces)
-    slab = pieces[0].shape[0] // ROWS
-    full = slab * count
+    full = out.shape[0] // ROWS
+    slab = full // count
     for k, piece in enumerate(pieces):
         at = pl.multiple_of(lax.rem(own + count - k, count) * slab, slab)
         for r in range(ROWS):
@@ -186,11 +182,13 @@
     return jax.ShapeDtypeStruct(dims, dtype)
 
 
-def label(packet, nbr):
-    packet[packet.shape[0] - HEAD :, :] = jnp.full((HEAD, packet.shape[1]), nbr.astype(F32))
-
-
-def strip_kernel(extent, below, above, now, strip, upper, lower, rows):
+def label(packet, below, above):
+    at = lax.broadcasted_iota(jnp.int32, (HEAD, packet.shape[1]), 0)
+    names = jnp.where(at < HEAD // 2, above, below)
+    packet[packet.shape[0] - HEAD :, :] = names.astype(F32)
+
+
+def strip_kernel(extent, below, above, now, packet, rows):
     slab, zcap, width = now.shape
     at = lax.broadcasted_iota(jnp.int32, (1, width), 1)
     far_face = at >= FACE
@@ -198,16 +196,13 @@
     near = jnp.where(at < ROWS, near, 0).astype(F32)
     table = face_rows(near, far_face.astype(F32), (zcap, width), extent[0])
     rows[...] = table
-    label(upper, above[0])
-    label(lower, below[0])
+    label(packet, below[0], above[0])
     weights = [jnp.broadcast_to(table[:, r : r + 1], (zcap, width)) for r in range(ROWS)]
     for i in range(slab // CHUNK):
         part = now[i * CHUNK : (i + 1) * CHUNK]
         for r in range(ROWS):
-            value = jnp.sum(part * weights[r][None], axis=1)
-            strip[r * slab + i * CHUNK : r * slab + (i + 1) * CHUNK, :] = value
-            at = r % FACE * slab + i * CHUNK
-            (lower if r < FACE else upper)[at : at + CHUNK, :] = value
+            span = slice(r * slab + i * CHUNK, r * slab + (i + 1) * CHUNK)
+            packet[span, :] = jnp.sum(part * weights[r][None], axis=1)
 
 
 def lane_series(consts, first, count, shape, extent):
@@ -309,42 +304,38 @@
         force[r * full : (r + 1) * full, :] = value - plane(near, r)
 
 
-def choose_kernel(group, after, *refs, tall, width):
-    uppers, lowers = refs[:tall], refs[tall : tall + width]
-    out = refs[tall + width :]
+def choose_kernel(group, after, *refs, width):
+    held, out = refs[:width], refs[width:]
+    rows = out[0].shape[0]
+    half = rows // 2
     h, l = group[0] // width, lax.rem(group[0], width)
-    for held, packets, places in (
-        (uppers, out[:width], [h * width + partner(l, k, width) for k in range(width)]),
-        (lowers, out[width:], [partner(h, k, tall) * width + l for k in range(tall)]),
-    ):
-        rows = packets[0].shape[0]
-        for packet, place in zip(packets, places):
-            dest = place.astype(F32)
-            chosen = held[0][:rows, :]
+    for k in range(len(out)):
+        dest = (lax.rem(h + k, len(out)) * width + l).astype(F32)
+        for f in range(2):
+            lo, hi = f * half, (f + 1) * half
+            row = rows + (0 if f == 1 else HEAD // 2)
+            chosen = held[0][lo:hi, :]
             for other in held[1:]:
-                chosen = jnp.where(other[rows : rows + 1, :] == dest, other[:rows, :], chosen)
-            packet[...] = chosen
+                chosen = jnp.where(other[row : row + 1, :] == dest, other[lo:hi, :], chosen)
+            out[k][lo:hi, :] = chosen
 
 
 def pick_kernel(group, below, above, after, *refs, tall, width):
-    uppers, lowers, out = refs[:width], refs[width:-1], refs[-1]
+    got, out = refs[:-1], refs[-1]
     half = out.shape[0] // 2
-    h, l = group[0] // width, lax.rem(group[0], width)
-    value = uppers[0][...]
-    for k in range(1, width):
-        here = lax.rem(jnp.maximum(below[0], 0), width) == giver(l, k, width)
-        value = jnp.where(here, uppers[k][...], value)
-    out[:half, :] = value
-    value = lowers[0][...]
-    for k in range(1, tall):
-        here = jnp.maximum(above[0], 0) // width == giver(h, k, tall)
-        value = jnp.where(here, lowers[k][...], value)
-    out[half:, :] = value
+    h = group[0] // width
+    for f, nbr in enumerate((below, above)):
+        lo = half if f == 0 else 0
+        value = got[0][lo : lo + half, :]
+        for k in range(1, tall):
+            here = jnp.maximum(nbr[0], 0) // width == lax.rem(h + tall - k, tall)
+            value = jnp.where(here, got[k][lo : lo + half, :], value)
+        out[f * half : (f + 1) * half, :] = value
 
 
 def middle_kernel(own, below, above, after, near, tx, uy, mixing, *rest, parts):
     far, ahead = rest[:parts], rest[parts : 2 * parts]
-    upper, lower, force, strip, spare = rest[2 * parts :]
+    packet, force, strip, spare = rest[2 * parts :]
     gather_kx(spare, far, own[0])
     force_planes(spare, near, tx, uy, force)
     gather_kx(strip, ahead, own[0])
@@ -357,10 +348,8 @@
         strip[r * full : (r + 1) * full, :] = total
     at = pl.multiple_of(own[0] * slab, slab)
     for r in range(ROWS):
-        packet = lower if r < FACE else upper
-        packet[r % FACE * slab : (r % FACE + 1) * slab, :] = strip[pl.ds(r * full + at, slab), :]
-    label(upper, above[0])
-    label(lower, below[0])
+        packet[r * slab : (r + 1) * slab, :] = strip[pl.ds(r * full + at, slab), :]
+    label(packet, below[0], above[0])
 
 
 def near_kernel(strip, vx, wy, near):
@@ -610,51 +599,45 @@
             got.append(lax.ppermute(piece, "split", [(i, (i + k) % parts) for i in range(parts)]))
         return got
 
-    face = FACE * slab
-    fast = lambda k: [(i, i // inner * inner + partner(i % inner, k, inner)) for i in range(count)]
-    slow = lambda k: [(i, partner(i // inner, k, tall) * inner + i % inner) for i in range(count)]
-
-    def spread(upper, lower):
-        uppers = [upper] + [lax.ppermute(upper, "dom", slow(k)) for k in range(1, tall)]
-        lowers = [lower] + [lax.ppermute(lower, "dom", fast(k)) for k in range(1, inner)]
-        return uppers + lowers
+    def spread(packet):
+        held = [packet]
+        for k in range(1, inner):
+            to = [(i, i // inner * inner + partner(i % inner, k, inner)) for i in range(count)]
+            held.append(lax.ppermute(packet, "dom", to))
+        return held
 
     def choose(held, after):
         return call(
-            functools.partial(choose_kernel, tall=tall, width=inner),
-            [shape_of(face, width)] * (inner + tall),
-            [SMEM, ANY] + [VMEM] * (inner + tall),
+            functools.partial(choose_kernel, width=inner),
+            [shape_of(size, width)] * tall,
+            [SMEM, ANY] + [VMEM] * inner,
             flops=COVER,
             moved=8 * size * width * 4,
             name="choose",
         )(group, after, *held)
 
     def deliver(chosen, after):
-        uppers, lowers = chosen[:inner], chosen[inner:]
-        got = [uppers[0]] + [lax.ppermute(uppers[k], "dom", fast(k)) for k in range(1, inner)]
-        got += [lowers[0]] + [lax.ppermute(lowers[k], "dom", slow(k)) for k in range(1, tall)]
+        got = [chosen[0]]
+        for k in range(1, tall):
+            to = [(i, (i + k * inner) % count) for i in range(count)]
+            got.append(lax.ppermute(chosen[k], "dom", to))
         picked = call(
             functools.partial(pick_kernel, tall=tall, width=inner),
             [shape_of(size, width)],
-            [SMEM] * 3 + [ANY] + [VMEM] * (inner + tall),
+            [SMEM] * 3 + [ANY] + [VMEM] * tall,
             moved=5 * size * width * 4,
             name="pick",
         )(group, lower_nbr, upper_nbr, after, *got)[0]
         return swap(picked)
 
-    strip, upper, lower, rows = call(
+    packet, rows = call(
         strip_kernel,
-        [
-            shape_of(size, width),
-            shape_of(face + HEAD, width),
-            shape_of(face + HEAD, width),
-            shape_of(zcap, width),
-        ],
+        [shape_of(size + HEAD, width), shape_of(zcap, width)],
         [SMEM] * 3 + [VMEM],
         moved=big,
         name="strip",
     )(z_extent, lower_nbr, upper_nbr, modes_now)
-    held = spread(upper, lower)
+    held = spread(packet)
     ahead, coefs = call(
         functools.partial(ahead_kernel, full=full),
         [shape_of(size, width), shape_of(16, width)],
@@ -664,7 +647,7 @@
         name="ahead",
     )(z_extent, own, modes_now, modes_prev, rows, consts)
     chosen = choose(held, ahead)
-    mine = swap(strip)
+    mine = swap(packet)
     aheads = swap(ahead)
 
     tx, uy, vx, wy, near1, mixing, _ = call(
@@ -699,11 +682,10 @@
         for k in range(1, parts)
     ]
 
-    upper2, lower2, force1, strip2 = call(
+    packet2, force1, strip2 = call(
         functools.partial(middle_kernel, parts=parts),
         [
-            shape_of(face + HEAD, width),
-            shape_of(face + HEAD, width),
+            shape_of(size + HEAD, width),
             shape_of(ROWS * full, width),
             shape_of(ROWS * full, width),
         ],
@@ -728,7 +710,7 @@
         moved=4 * big,
         name="between",
     )(z_extent, own, modes_now, modes_prev, force1, rows, consts)
-    chosen2 = choose(spread(upper2, lower2), onward)
+    chosen2 = choose(spread(packet2), onward)
     summed = call(
         first_kernel,
         [shape_of(slab * zcap, width)],

time: 77.9 us -> 65.1 us (0.84)
  starting transfers between devices: 34 us -> 22.5 us
  waiting for transfers between devices: 18 us -> 16.9 us
    ppermute x24 -> x12, starting transfers between devices: 27.5 us -> 15.9 us  [the longest x6 10.9 us: deliver(): got.append(lax.ppermute(chosen[k], 'dom', to))]
    ppermute x4, waiting for transfers between devices: 14.3 us -> 9.18 us  [swap(): lax.ppermute(piece, 'split', [(i, (i + k) % parts) for i in range(parts)])]
    ppermute x24 -> x12, waiting for transfers between devices: 3.74 us -> 7.75 us  [the longest x6 6.2 us: deliver(): got.append(lax.ppermute(chosen[k], 'dom', to))]
  transfers between devices with their start and end apart: 29 -> 17, of which waited for: 4 -> 6; matrix products, arithmetic and copies ran while one was open for 0% -> 0% of each run, Pallas kernels for 18% -> 22%
where the time goes in v5:
time: 65.1 us; the launch traced here: 64.8 us
  starting transfers between devices  22.5 us (35%)
  Pallas kernels  19.3 us (30%)
  waiting for transfers between devices  16.9 us (26%)
  local copies, waits for them, and re-layouts  3.24 us (5%)
  between operations  2.91 us (4%)
    ppermute x6, starting transfers between devices, deliver(): got.append(lax.ppermute(chosen[k], 'dom', to))  10.9 us
    ppermute x4, waiting for transfers between devices, swap(): lax.ppermute(piece, 'split', [(i, (i + k) % parts) for i in range(parts)])  9.18 us
    ppermute x6, waiting for transfers between devices, deliver(): got.append(lax.ppermute(chosen[k], 'dom', to))  6.2 us
    ppermute x4, starting transfers between devices, swap(): lax.ppermute(piece, 'split', [(i, (i + k) % parts) for i in range(parts)])  5.77 us
    ppermute x6, starting transfers between devices, spread(): held.append(lax.ppermute(packet, 'dom', to))  5.05 us
    pallas_call x1, Pallas kernels, on_device(): call(functools.partial(unforced_kernel, full=full), [shape_of(slab * zcap...  4.76 us
    pallas_call x1, Pallas kernels, on_device(): call(functools.partial(last_kernel, full=full, parts=parts), [shape_of(sl...  3.45 us
    unnamed x26, local copies, waits for them, and re-layouts  3.24 us
  transfers between devices with their start and end apart: 17, of which 6 were waited for; matrix products, arithmetic and copies ran while one was open for 0% of the time, Pallas kernels for 22%

profile of v5, /device:TPU:0, one launch (start us, length us, event | category | flops | bytes accessed | tf_op | source)
XLA Modules:
  0.0 64.8 jit_solution(17836050729750255552)
XLA Ops:
  2.6 1.2 %copy-done = f32[32,64,128]{2,1,0:T(8,128)S(1)} copy-done((f32[32,64,128]{2,1,0:T(8,128)S(1)}, f32[32,64,128]{2,1,0:T(8,128)}, u32[]{:S(2)}) %copy-start) | copy-done | bytes 1048600
  4.6 2.4 %collective-permute-start.2 = (f32[200,128]{1,0:T(8,128)S(1)}, f32[200,128]{1,0:T(8,128)S(1)}, u32[]{:S(2)}, u32[]{:S(2)}) collective-permute-start(f32[200,128]{1,0:T(8,128)S(1)} %get-tuple-element.36.refs_0_.rest_0_), channel_id=1, source_target_pairs={{0,6},{2,4},{4,2},{6,0},{8,14},{10,12},{12,10},{14,8},{16,22},{18,... | collective-permute-start | bytes 307208 | tf_op jit(solution)/shard_map/ppermute | solution.py:606
  7.8 1.8 %collective-permute-start.3 = (f32[200,128]{1,0:T(8,128)S(1)}, f32[200,128]{1,0:T(8,128)S(1)}, u32[]{:S(2)}, u32[]{:S(2)}) collective-permute-start(f32[200,128]{1,0:T(8,128)S(1)} %get-tuple-element.36.refs_0_.rest_0_), channel_id=1, source_target_pairs={{0,1},{1,0},{2,3},{3,2},{4,5},{5,4},{6,7},{7,6},{8,9},{9,8},{10,11... | collective-permute-start | bytes 307208 | tf_op jit(solution)/shard_map/ppermute | solution.py:599
  9.5 1.2 %copy-done.2 = f32[32,64,128]{2,1,0:T(8,128)S(1)} copy-done((f32[32,64,128]{2,1,0:T(8,128)S(1)}, f32[32,64,128]{2,1,0:T(8,128)}, u32[]{:S(2)}) %copy-start.2) | copy-done | bytes 1048600
  11.5 1.7 %ahead.1 = (f32[192,128]{1,0:T(8,128)S(1)}, f32[16,128]{1,0:T(8,128)S(1)}) custom-call(s32[1]{0:T(128)S(6)} %copy.16.extent, s32[1]{0:T(128)} %bitcast.own, f32[32,64,128]{2,1,0:T(8,128)S(1)} %copy-done.1, f32[32,64,128]{2,1,0:T(8,128)S(1)} %copy-done.2, f32[64,128]{1,0:T(8,128)S(1)} %get-tuple-element.33.rows, f32[56,128]{1,0:T(8,128)S(1)} %copy-done.8), custom_call_target="tpu_custom_call" | custom-call | flops 100000000 | bytes 2097152 | tf_op jit(solution)/shard_map/ahead/pallas_call | solution.py:641
  13.4 1.9 %collective-permute-start.4 = (f32[192,128]{1,0:T(8,128)S(1)}, f32[192,128]{1,0:T(8,128)S(1)}, u32[]{:S(2)}, u32[]{:S(2)}) collective-permute-start(f32[192,128]{1,0:T(8,128)S(1)} %get-tuple-element.39), channel_id=1, source_target_pairs={{0,8},{2,10},{4,12},{6,14},{8,16},{10,18},{12,20},{14,22},{16,24},... | collective-permute-start | bytes 294920 | tf_op jit(solution)/shard_map/ppermute | solution.py:623
  15.3 2.6 %collective-permute-start.5 = (f32[192,128]{1,0:T(8,128)S(1)}, f32[192,128]{1,0:T(8,128)S(1)}, u32[]{:S(2)}, u32[]{:S(2)}) collective-permute-start(f32[192,128]{1,0:T(8,128)S(1)} %get-tuple-element.40), channel_id=1, source_target_pairs={{0,16},{2,18},{4,20},{6,22},{8,24},{10,26},{12,28},{14,30},{16,0},... | collective-permute-start | bytes 294920 | tf_op jit(solution)/shard_map/ppermute | solution.py:623
  17.9 1.3 %collective-permute-start.6 = (f32[192,128]{1,0:T(8,128)S(1)}, f32[192,128]{1,0:T(8,128)S(1)}, u32[]{:S(2)}, u32[]{:S(2)}) collective-permute-start(f32[192,128]{1,0:T(8,128)S(1)} %get-tuple-element.41), channel_id=1, source_target_pairs={{0,24},{2,26},{4,28},{6,30},{8,0},{10,2},{12,4},{14,6},{16,8},{18,... | collective-permute-start | bytes 294920 | tf_op jit(solution)/shard_map/ppermute | solution.py:623
  19.2 1.5 %collective-permute-start.8 = (f32[192,128]{1,0:T(8,128)S(1)}, f32[192,128]{1,0:T(8,128)S(1)}, u32[]{:S(2)}, u32[]{:S(2)}) collective-permute-start(f32[192,128]{1,0:T(8,128)S(1)} %get-tuple-element.35.after.rest_2_), channel_id=1, source_target_pairs={{0,1},{1,0},{2,3},{3,2},{4,5},{5,4},{6,7},{7,6},{8,9},{9,8},{10,11... | collective-permute-start | bytes 294920 | tf_op jit(solution)/shard_map/ppermute | solution.py:599
  20.8 2.0 %relation.1 = (f32[2,64,64]{2,1,0:T(8,128)S(1)}, f32[2,128,128]{2,1,0:T(8,128)S(1)}, f32[2,64,64]{2,1,0:T(8,128)S(1)}, f32[2,128,128]{2,1,0:T(8,128)S(1)}, f32[3...) custom-call(s32[1]{0:T(128)S(6)} %copy.17.below, s32[1]{0:T(128)S(6)} %copy.18.above, ...), custom_call_target="tpu_custom_call" | custom-call | flops 100000000 | bytes 2097152 | tf_op jit(solution)/shard_map/relation/pallas_call | solution.py:653
  22.8 1.8 %collective-permute-done.5.refs_2_ = f32[192,128]{1,0:T(8,128)S(1)} collective-permute-done((f32[192,128]{1,0:T(8,128)S(1)}, f32[192,128]{1,0:T(8,128)S(1)}, u32[]{:S(2)}, u32[]{:S(2)}) %collective-permute-start.5) | collective-permute-done | bytes 98336 | tf_op jit(solution)/shard_map/ppermute | solution.py:623
  24.7 1.6 %collective-permute-start.7 = (f32[192,128]{1,0:T(8,128)S(1)}, f32[192,128]{1,0:T(8,128)S(1)}, u32[]{:S(2)}, u32[]{:S(2)}) collective-permute-start(f32[192,128]{1,0:T(8,128)S(1)} %pick.2.after.rest_0_), channel_id=1, source_target_pairs={{0,1},{1,0},{2,3},{3,2},{4,5},{5,4},{6,7},{7,6},{8,9},{9,8},{10,11... | collective-permute-start | bytes 294920 | tf_op jit(solution)/shard_map/ppermute | solution.py:599
  26.3 4.8 %unforced.1 = (f32[2048,128]{1,0:T(8,128)S(1)}, f32[2048,128]{1,0:T(8,128)S(1)}) custom-call(s32[1]{0:T(128)S(6)} %copy.16.extent, s32[1]{0:T(128)} %bitcast.own, f32[192,128]{1,0:T(8,128)S(1)} %pick.2.after.rest_0_, f32[32,64,128]{2,1,0:T(8,128)S(1)} %copy-done.1, f32[32,64,128]{2,1,0:T(8,128)S(1)} %copy-done.3, bf16[256,256]{1,0:T(8,128)(2,1)S(1)} %copy-done.5, ...), custom_call_target="tpu_custom_call" | custom-call | flops 1000000000 | bytes 4194304 | tf_op jit(solution)/shard_map/unforced/pallas_call | solution.py:671
  34.6 3.2 %between.1 = (f32[32,64,128]{2,1,0:T(8,128)}, f32[32,64,128]{2,1,0:T(8,128)S(1)}, bf16[64,144]{1,0:T(8,128)(2,1)S(1)}, bf16[64,144]{1,0:T(8,128)(2,1)S(1)}, bf16[64,192]{1,0:T(8,128)(2,1)S(1)}) custom-call(s32[1]{0:T(128)S(6)} %copy.16.extent, s32[1]{0:T(128)} %bitcast.own, f32[32,64,128]{2,1,0:T(8,128)S(1)} %copy-done.1, f32[32,64,128]{2,1,0:T(8,128)S(1)} %copy-done.3, ...), custom_call_target="tpu_custom_call" | custom-call | flops 1000000000 | bytes 4194304 | tf_op jit(solution)/shard_map/between/pallas_call | solution.py:699
  37.8 1.5 %collective-permute-done.10.refs_2_ = f32[200,128]{1,0:T(8,128)S(1)} collective-permute-done((f32[200,128]{1,0:T(8,128)S(1)}, f32[200,128]{1,0:T(8,128)S(1)}, u32[]{:S(2)}, u32[]{:S(2)}) %collective-permute-start.10) | collective-permute-done | bytes 102432 | tf_op jit(solution)/shard_map/ppermute | solution.py:606
  39.4 2.6 %collective-permute-start.12 = (f32[192,128]{1,0:T(8,128)S(1)}, f32[192,128]{1,0:T(8,128)S(1)}, u32[]{:S(2)}, u32[]{:S(2)}) collective-permute-start(f32[192,128]{1,0:T(8,128)S(1)} %get-tuple-element.56), channel_id=1, source_target_pairs={{0,8},{2,10},{4,12},{6,14},{8,16},{10,18},{12,20},{14,22},{16,24},... | collective-permute-start | bytes 294920 | tf_op jit(solution)/shard_map/ppermute | solution.py:623
  42.0 1.6 %collective-permute-start.13 = (f32[192,128]{1,0:T(8,128)S(1)}, f32[192,128]{1,0:T(8,128)S(1)}, u32[]{:S(2)}, u32[]{:S(2)}) collective-permute-start(f32[192,128]{1,0:T(8,128)S(1)} %get-tuple-element.57), channel_id=1, source_target_pairs={{0,16},{2,18},{4,20},{6,22},{8,24},{10,26},{12,28},{14,30},{16,0},... | collective-permute-start | bytes 294920 | tf_op jit(solution)/shard_map/ppermute | solution.py:623
  43.6 0.8 %collective-permute-start.14 = (f32[192,128]{1,0:T(8,128)S(1)}, f32[192,128]{1,0:T(8,128)S(1)}, u32[]{:S(2)}, u32[]{:S(2)}) collective-permute-start(f32[192,128]{1,0:T(8,128)S(1)} %get-tuple-element.58), channel_id=1, source_target_pairs={{0,24},{2,26},{4,28},{6,30},{8,0},{10,2},{12,4},{14,6},{16,8},{18,... | collective-permute-start | bytes 294920 | tf_op jit(solution)/shard_map/ppermute | solution.py:623
  44.5 1.7 %first.1.after.rest_2_ = f32[2048,128]{1,0:T(8,128)S(1)} custom-call(s32[1]{0:T(128)} %bitcast.own, f32[384,128]{1,0:T(8,128)S(1)} %get-tuple-element.49.force, bf16[64,192]{1,0:T(8,128)(2,1)S(1)} %get-tuple-element.53.gstack, bf16[256,256]{1,0:T(8,128)(2,1)S(1)} %copy-done.5, bf16[2,32,192]{2,1,0:T(8,128)(2,1)S(1)} %copy-done.7, ...), custom_call_target="tpu_custom_call" | custom-call | flops 1000000000 | bytes 2097152 | tf_op jit(solution)/shard_map/first/pallas_call | solution.py:714
  46.2 0.9 %collective-permute-done.12.refs_1_ = f32[192,128]{1,0:T(8,128)S(1)} collective-permute-done((f32[192,128]{1,0:T(8,128)S(1)}, f32[192,128]{1,0:T(8,128)S(1)}, u32[]{:S(2)}, u32[]{:S(2)}) %collective-permute-start.12) | collective-permute-done | bytes 98336 | tf_op jit(solution)/shard_map/ppermute | solution.py:623
  47.0 3.4 %collective-permute-done.13.refs_2_ = f32[192,128]{1,0:T(8,128)S(1)} collective-permute-done((f32[192,128]{1,0:T(8,128)S(1)}, f32[192,128]{1,0:T(8,128)S(1)}, u32[]{:S(2)}, u32[]{:S(2)}) %collective-permute-start.13) | collective-permute-done | bytes 98336 | tf_op jit(solution)/shard_map/ppermute | solution.py:623
  50.5 0.9 %collective-permute-start.15 = (f32[192,128]{1,0:T(8,128)S(1)}, f32[192,128]{1,0:T(8,128)S(1)}, u32[]{:S(2)}, u32[]{:S(2)}) collective-permute-start(f32[192,128]{1,0:T(8,128)S(1)} %pick.3.rest_0_), channel_id=1, source_target_pairs={{0,1},{1,0},{2,3},{3,2},{4,5},{5,4},{6,7},{7,6},{8,9},{9,8},{10,11... | collective-permute-start | bytes 294920 | tf_op jit(solution)/shard_map/ppermute | solution.py:599
  52.1 9.2 %collective-permute-done.15.rest_1_ = f32[192,128]{1,0:T(8,128)S(1)} collective-permute-done((f32[192,128]{1,0:T(8,128)S(1)}, f32[192,128]{1,0:T(8,128)S(1)}, u32[]{:S(2)}, u32[]{:S(2)}) %collective-permute-start.15) | collective-permute-done | bytes 98336 | tf_op jit(solution)/shard_map/ppermute | solution.py:599
  61.2 3.4 %last.1 = (f32[32,64,128]{2,1,0:T(8,128)}, f32[2048,128]{1,0:T(8,128)}) custom-call(s32[1]{0:T(128)} %bitcast.own, f32[384,128]{1,0:T(8,128)S(1)} %near.1, f32[2,64,64]{2,1,0:T(8,128)S(1)} %get-tuple-element.43.tx, f32[2,128,128]{2,1,0:T(8,128)S(1)} %get-tuple-element.44.uy, f32[32,64,128]{2,1,0:T(8,128)S(1)} %get-tuple-element.50.after.onward, ...), custom_call_target="tpu_custom_call" | custom-call | flops 1000000000 | bytes 6291456 | tf_op jit(solution)/shard_map/last/pallas_call | solution.py:735
  (49 shorter events, 6.8 us)
Async XLA Ops:
  3.8 5.7 %copy-start.1 = (f32[32,64,128]{2,1,0:T(8,128)S(1)}, f32[32,64,128]{2,1,0:T(8,128)}, u32[]{:S(2)}) copy-start(f32[32,64,128]{2,1,0:T(8,128)} %now.7) | copy-start | bytes 3145732
  4.6 8.6 %collective-permute-start.2 = (f32[200,128]{1,0:T(8,128)S(1)}, f32[200,128]{1,0:T(8,128)S(1)}, u32[]{:S(2)}, u32[]{:S(2)}) collective-permute-start(f32[200,128]{1,0:T(8,128)S(1)} %get-tuple-element.36.refs_0_.rest_0_), channel_id=1, source_target_pairs={{0,6},{2,4},{4,2},{6,0},{8,14},{10,12},{12,10},{14,8},{16,22},{18,... | collective-permute-start | bytes 307208 | tf_op jit(solution)/shard_map/ppermute | solution.py:606
  7.1 6.2 %collective-permute-start.1 = (f32[200,128]{1,0:T(8,128)S(1)}, f32[200,128]{1,0:T(8,128)S(1)}, u32[]{:S(2)}, u32[]{:S(2)}) collective-permute-start(f32[200,128]{1,0:T(8,128)S(1)} %get-tuple-element.36.refs_0_.rest_0_), channel_id=1, source_target_pairs={{0,4},{2,6},{4,0},{6,2},{8,12},{10,14},{12,8},{14,10},{16,20},{18,... | collective-permute-start | bytes 307208 | tf_op jit(solution)/shard_map/ppermute | solution.py:606
  7.7 5.5 %collective-permute-start = (f32[200,128]{1,0:T(8,128)S(1)}, f32[200,128]{1,0:T(8,128)S(1)}, u32[]{:S(2)}, u32[]{:S(2)}) collective-permute-start(f32[200,128]{1,0:T(8,128)S(1)} %get-tuple-element.36.refs_0_.rest_0_), channel_id=1, source_target_pairs={{0,2},{2,0},{4,6},{6,4},{8,10},{10,8},{12,14},{14,12},{16,18},{18,... | collective-permute-start | bytes 307208 | tf_op jit(solution)/shard_map/ppermute | solution.py:606
  7.8 13.0 %collective-permute-start.3 = (f32[200,128]{1,0:T(8,128)S(1)}, f32[200,128]{1,0:T(8,128)S(1)}, u32[]{:S(2)}, u32[]{:S(2)}) collective-permute-start(f32[200,128]{1,0:T(8,128)S(1)} %get-tuple-element.36.refs_0_.rest_0_), channel_id=1, source_target_pairs={{0,1},{1,0},{2,3},{3,2},{4,5},{5,4},{6,7},{7,6},{8,9},{9,8},{10,11... | collective-permute-start | bytes 307208 | tf_op jit(solution)/shard_map/ppermute | solution.py:599
  13.3 7.5 %copy-start.4 = (f32[512,128]{1,0:T(8,128)S(1)}, f32[512,128]{1,0:T(8,128)}, u32[]{:S(2)}) copy-start(f32[512,128]{1,0:T(8,128)} %constant.25.clone.ytall) | copy-start | bytes 786436
  13.3 7.5 %copy-start.6 = (f32[256,64]{1,0:T(8,128)S(1)}, f32[256,64]{1,0:T(8,128)}, u32[]{:S(2)}) copy-start(f32[256,64]{1,0:T(8,128)} %constant.24.clone.xtall) | copy-start | bytes 196612
  13.3 7.5 %copy-start.10 = (s32[1,2]{1,0:T(1,128)S(1)}, s32[1,2]{1,0:T(1,128)}, u32[]{:S(2)}) copy-start(s32[1,2]{1,0:T(1,128)} %x_shift.1) | copy-start | bytes 28
  13.3 7.5 %copy-start.11 = (s32[1,2]{1,0:T(1,128)S(1)}, s32[1,2]{1,0:T(1,128)}, u32[]{:S(2)}) copy-start(s32[1,2]{1,0:T(1,128)} %y_shift.1) | copy-start | bytes 28
  13.4 12.9 %copy-start.3 = (f32[32,64,128]{2,1,0:T(8,128)S(1)}, f32[32,64,128]{2,1,0:T(8,128)}, u32[]{:S(2)}) copy-start(f32[32,64,128]{2,1,0:T(8,128)} %prev.5) | copy-start | bytes 3145732
  13.4 9.4 %collective-permute-start.4 = (f32[192,128]{1,0:T(8,128)S(1)}, f32[192,128]{1,0:T(8,128)S(1)}, u32[]{:S(2)}, u32[]{:S(2)}) collective-permute-start(f32[192,128]{1,0:T(8,128)S(1)} %get-tuple-element.39), channel_id=1, source_target_pairs={{0,8},{2,10},{4,12},{6,14},{8,16},{10,18},{12,20},{14,22},{16,24},... | collective-permute-start | bytes 294920 | tf_op jit(solution)/shard_map/ppermute | solution.py:623
  15.3 9.4 %collective-permute-start.5 = (f32[192,128]{1,0:T(8,128)S(1)}, f32[192,128]{1,0:T(8,128)S(1)}, u32[]{:S(2)}, u32[]{:S(2)}) collective-permute-start(f32[192,128]{1,0:T(8,128)S(1)} %get-tuple-element.40), channel_id=1, source_target_pairs={{0,16},{2,18},{4,20},{6,22},{8,24},{10,26},{12,28},{14,30},{16,0},... | collective-permute-start | bytes 294920 | tf_op jit(solution)/shard_map/ppermute | solution.py:623
  17.9 6.8 %collective-permute-start.6 = (f32[192,128]{1,0:T(8,128)S(1)}, f32[192,128]{1,0:T(8,128)S(1)}, u32[]{:S(2)}, u32[]{:S(2)}) collective-permute-start(f32[192,128]{1,0:T(8,128)S(1)} %get-tuple-element.41), channel_id=1, source_target_pairs={{0,24},{2,26},{4,28},{6,30},{8,0},{10,2},{12,4},{14,6},{16,8},{18,... | collective-permute-start | bytes 294920 | tf_op jit(solution)/shard_map/ppermute | solution.py:623
  19.2 11.9 %collective-permute-start.8 = (f32[192,128]{1,0:T(8,128)S(1)}, f32[192,128]{1,0:T(8,128)S(1)}, u32[]{:S(2)}, u32[]{:S(2)}) collective-permute-start(f32[192,128]{1,0:T(8,128)S(1)} %get-tuple-element.35.after.rest_2_), channel_id=1, source_target_pairs={{0,1},{1,0},{2,3},{3,2},{4,5},{5,4},{6,7},{7,6},{8,9},{9,8},{10,11... | collective-permute-start | bytes 294920 | tf_op jit(solution)/shard_map/ppermute | solution.py:599
  24.7 6.4 %collective-permute-start.7 = (f32[192,128]{1,0:T(8,128)S(1)}, f32[192,128]{1,0:T(8,128)S(1)}, u32[]{:S(2)}, u32[]{:S(2)}) collective-permute-start(f32[192,128]{1,0:T(8,128)S(1)} %pick.2.after.rest_0_), channel_id=1, source_target_pairs={{0,1},{1,0},{2,3},{3,2},{4,5},{5,4},{6,7},{7,6},{8,9},{9,8},{10,11... | collective-permute-start | bytes 294920 | tf_op jit(solution)/shard_map/ppermute | solution.py:599
  31.9 5.9 %collective-permute-start.11 = (f32[200,128]{1,0:T(8,128)S(1)}, f32[200,128]{1,0:T(8,128)S(1)}, u32[]{:S(2)}, u32[]{:S(2)}) collective-permute-start(f32[200,128]{1,0:T(8,128)S(1)} %get-tuple-element.54.refs_0_), channel_id=1, source_target_pairs={{0,6},{2,4},{4,2},{6,0},{8,14},{10,12},{12,10},{14,8},{16,22},{18,... | collective-permute-start | bytes 307208 | tf_op jit(solution)/shard_map/ppermute | solution.py:606
  32.7 6.6 %collective-permute-start.10 = (f32[200,128]{1,0:T(8,128)S(1)}, f32[200,128]{1,0:T(8,128)S(1)}, u32[]{:S(2)}, u32[]{:S(2)}) collective-permute-start(f32[200,128]{1,0:T(8,128)S(1)} %get-tuple-element.54.refs_0_), channel_id=1, source_target_pairs={{0,4},{2,6},{4,0},{6,2},{8,12},{10,14},{12,8},{14,10},{16,20},{18,... | collective-permute-start | bytes 307208 | tf_op jit(solution)/shard_map/ppermute | solution.py:606
  33.5 5.8 %collective-permute-start.9 = (f32[200,128]{1,0:T(8,128)S(1)}, f32[200,128]{1,0:T(8,128)S(1)}, u32[]{:S(2)}, u32[]{:S(2)}) collective-permute-start(f32[200,128]{1,0:T(8,128)S(1)} %get-tuple-element.54.refs_0_), channel_id=1, source_target_pairs={{0,2},{2,0},{4,6},{6,4},{8,10},{10,8},{12,14},{14,12},{16,18},{18,... | collective-permute-start | bytes 307208 | tf_op jit(solution)/shard_map/ppermute | solution.py:606
  33.8 27.4 %collective-permute-start.16 = (f32[2048,128]{1,0:T(8,128)S(1)}, f32[2048,128]{1,0:T(8,128)S(1)}, u32[]{:S(2)}, u32[]{:S(2)}) collective-permute-start(f32[2048,128]{1,0:T(8,128)S(1)} %get-tuple-element.59), channel_id=1, source_target_pairs={{0,1},{1,0},{2,3},{3,2},{4,5},{5,4},{6,7},{7,6},{8,9},{9,8},{10,11... | collective-permute-start | bytes 3145736 | tf_op jit(solution)/shard_map/ppermute | solution.py:681
  39.3 5.2 %copy-start.7 = (bf16[2,32,192]{2,1,0:T(8,128)(2,1)S(1)}, bf16[2,32,192]{2,1,0:T(8,128)(2,1)}, u32[]{:S(2)}) copy-start(bf16[2,32,192]{2,1,0:T(8,128)(2,1)} %constant.22.clone.xown) | copy-start | bytes 73732
  39.4 7.6 %collective-permute-start.12 = (f32[192,128]{1,0:T(8,128)S(1)}, f32[192,128]{1,0:T(8,128)S(1)}, u32[]{:S(2)}, u32[]{:S(2)}) collective-permute-start(f32[192,128]{1,0:T(8,128)S(1)} %get-tuple-element.56), channel_id=1, source_target_pairs={{0,8},{2,10},{4,12},{6,14},{8,16},{10,18},{12,20},{14,22},{16,24},... | collective-permute-start | bytes 294920 | tf_op jit(solution)/shard_map/ppermute | solution.py:623
  42.0 8.4 %collective-permute-start.13 = (f32[192,128]{1,0:T(8,128)S(1)}, f32[192,128]{1,0:T(8,128)S(1)}, u32[]{:S(2)}, u32[]{:S(2)}) collective-permute-start(f32[192,128]{1,0:T(8,128)S(1)} %get-tuple-element.57), channel_id=1, source_target_pairs={{0,16},{2,18},{4,20},{6,22},{8,24},{10,26},{12,28},{14,30},{16,0},... | collective-permute-start | bytes 294920 | tf_op jit(solution)/shard_map/ppermute | solution.py:623
  43.6 6.9 %collective-permute-start.14 = (f32[192,128]{1,0:T(8,128)S(1)}, f32[192,128]{1,0:T(8,128)S(1)}, u32[]{:S(2)}, u32[]{:S(2)}) collective-permute-start(f32[192,128]{1,0:T(8,128)S(1)} %get-tuple-element.58), channel_id=1, source_target_pairs={{0,24},{2,26},{4,28},{6,30},{8,0},{10,2},{12,4},{14,6},{16,8},{18,... | collective-permute-start | bytes 294920 | tf_op jit(solution)/shard_map/ppermute | solution.py:623
  50.5 10.7 %collective-permute-start.15 = (f32[192,128]{1,0:T(8,128)S(1)}, f32[192,128]{1,0:T(8,128)S(1)}, u32[]{:S(2)}, u32[]{:S(2)}) collective-permute-start(f32[192,128]{1,0:T(8,128)S(1)} %pick.3.rest_0_), channel_id=1, source_target_pairs={{0,1},{1,0},{2,3},{3,2},{4,5},{5,4},{6,7},{7,6},{8,9},{9,8},{10,11... | collective-permute-start | bytes 294920 | tf_op jit(solution)/shard_map/ppermute | solution.py:599
  (6 other events, 10.0 us)

commit v6 on v5

--- a/solution.py
+++ b/solution.py
@@ -230,7 +230,7 @@
 
 
 def ahead_kernel(
-    extent, own, now, prev, rows, consts, strip, coefs, *, full
+    extent, own, packet, now, prev, rows, consts, strip, coefs, same, *, full
 ):
     slab, zcap, width = now.shape
     ext = extent[0]
@@ -238,6 +238,7 @@
     shape = (zcap, width)
     pairs = face_rows(consts[2:3, :], consts[3:4, :], shape, ext)
     pairs = pairs * face_rows(consts[4:5, :], consts[5:6, :], shape, ext)
+    same[...] = packet[: same.shape[0], :]
     series = lane_series(consts, 8, len(SERIES), shape, ext)
     coefs[...] = exact_dot(series.T[: coefs.shape[0]], pairs)
 
@@ -638,16 +639,16 @@
         name="strip",
     )(z_extent, lower_nbr, upper_nbr, modes_now)
     held = spread(packet)
-    ahead, coefs = call(
+    ahead, coefs, strip = call(
         functools.partial(ahead_kernel, full=full),
-        [shape_of(size, width), shape_of(16, width)],
-        [SMEM] * 2 + [VMEM] * 4,
+        [shape_of(size, width), shape_of(16, width), shape_of(size, width)],
+        [SMEM] * 2 + [VMEM] * 5,
         flops=10**8,
         moved=2 * big,
         name="ahead",
-    )(z_extent, own, modes_now, modes_prev, rows, consts)
+    )(z_extent, own, packet, modes_now, modes_prev, rows, consts)
     chosen = choose(held, ahead)
-    mine = swap(packet)
+    mine = swap(strip)
     aheads = swap(ahead)
 
     tx, uy, vx, wy, near1, mixing, _ = call(

time: 65.1 us -> 65.1 us (level)
  no operation moved by 1% of the time
where the time goes in v6:
time: 65.1 us; the launch traced here: 64.9 us
  starting transfers between devices  22.5 us (35%)
  Pallas kernels  19.3 us (30%)
  waiting for transfers between devices  17 us (26%)
  local copies, waits for them, and re-layouts  3.24 us (5%)
  between operations  2.89 us (4%)
    ppermute x6, starting transfers between devices, deliver(): got.append(lax.ppermute(chosen[k], 'dom', to))  10.8 us
    ppermute x4, waiting for transfers between devices, swap(): lax.ppermute(piece, 'split', [(i, (i + k) % parts) for i in range(parts)])  9.18 us
    ppermute x6, waiting for transfers between devices, deliver(): got.append(lax.ppermute(chosen[k], 'dom', to))  6.22 us
    ppermute x4, starting transfers between devices, swap(): lax.ppermute(piece, 'split', [(i, (i + k) % parts) for i in range(parts)])  5.82 us
    ppermute x6, starting transfers between devices, spread(): held.append(lax.ppermute(packet, 'dom', to))  5.05 us
    pallas_call x1, Pallas kernels, on_device(): call(functools.partial(unforced_kernel, full=full), [shape_of(slab * zcap...  4.76 us
    pallas_call x1, Pallas kernels, on_device(): call(functools.partial(last_kernel, full=full, parts=parts), [shape_of(sl...  3.45 us
    unnamed x26, local copies, waits for them, and re-layouts  3.24 us
  transfers between devices with their start and end apart: 17, of which 6 were waited for; matrix products, arithmetic and copies ran while one was open for 0% of the time, Pallas kernels for 22%

profile of v6, /device:TPU:0, one launch (start us, length us, event | category | flops | bytes accessed | tf_op | source)
XLA Modules:
  0.0 64.9 jit_solution(12829476574445659064)
XLA Ops:
  2.6 1.2 %copy-done = f32[32,64,128]{2,1,0:T(8,128)S(1)} copy-done((f32[32,64,128]{2,1,0:T(8,128)S(1)}, f32[32,64,128]{2,1,0:T(8,128)}, u32[]{:S(2)}) %copy-start) | copy-done | bytes 1048600
  4.6 2.4 %collective-permute-start.2 = (f32[200,128]{1,0:T(8,128)S(1)}, f32[200,128]{1,0:T(8,128)S(1)}, u32[]{:S(2)}, u32[]{:S(2)}) collective-permute-start(f32[200,128]{1,0:T(8,128)S(1)} %get-tuple-element.34.packet.refs_0_), channel_id=1, source_target_pairs={{0,6},{2,4},{4,2},{6,0},{8,14},{10,12},{12,10},{14,8},{16,22},{18,... | collective-permute-start | bytes 307208 | tf_op jit(solution)/shard_map/ppermute | solution.py:607
  7.8 1.2 %copy-done.2 = f32[32,64,128]{2,1,0:T(8,128)S(1)} copy-done((f32[32,64,128]{2,1,0:T(8,128)S(1)}, f32[32,64,128]{2,1,0:T(8,128)}, u32[]{:S(2)}) %copy-start.2) | copy-done | bytes 1048600
  9.7 1.7 %ahead.1 = (f32[192,128]{1,0:T(8,128)S(1)}, f32[16,128]{1,0:T(8,128)S(1)}, f32[192,128]{1,0:T(8,128)S(1)}) custom-call(s32[1]{0:T(128)S(6)} %copy.16.extent, s32[1]{0:T(128)} %bitcast.own, f32[200,128]{1,0:T(8,128)S(1)} %get-tuple-element.34.packet.refs_0_, f32[32,64,128]{2,1,0:T(8,128)S(1)} %copy-done.1, f32[32,64,128]{2,1,0:T(8,128)S(1)} %copy-done.2, ...), custom_call_target="tpu_custom_call" | custom-call | flops 100000000 | bytes 2097152 | tf_op jit(solution)/shard_map/ahead/pallas_call | solution.py:642
  11.5 1.8 %collective-permute-start.3 = (f32[192,128]{1,0:T(8,128)S(1)}, f32[192,128]{1,0:T(8,128)S(1)}, u32[]{:S(2)}, u32[]{:S(2)}) collective-permute-start(f32[192,128]{1,0:T(8,128)S(1)} %get-tuple-element.39.rest_0_), channel_id=1, source_target_pairs={{0,1},{1,0},{2,3},{3,2},{4,5},{5,4},{6,7},{7,6},{8,9},{9,8},{10,11... | collective-permute-start | bytes 294920 | tf_op jit(solution)/shard_map/ppermute | solution.py:600
  13.5 1.8 %collective-permute-start.4 = (f32[192,128]{1,0:T(8,128)S(1)}, f32[192,128]{1,0:T(8,128)S(1)}, u32[]{:S(2)}, u32[]{:S(2)}) collective-permute-start(f32[192,128]{1,0:T(8,128)S(1)} %get-tuple-element.41), channel_id=1, source_target_pairs={{0,8},{2,10},{4,12},{6,14},{8,16},{10,18},{12,20},{14,22},{16,24},... | collective-permute-start | bytes 294920 | tf_op jit(solution)/shard_map/ppermute | solution.py:624
  15.3 2.6 %collective-permute-start.5 = (f32[192,128]{1,0:T(8,128)S(1)}, f32[192,128]{1,0:T(8,128)S(1)}, u32[]{:S(2)}, u32[]{:S(2)}) collective-permute-start(f32[192,128]{1,0:T(8,128)S(1)} %get-tuple-element.42), channel_id=1, source_target_pairs={{0,16},{2,18},{4,20},{6,22},{8,24},{10,26},{12,28},{14,30},{16,0},... | collective-permute-start | bytes 294920 | tf_op jit(solution)/shard_map/ppermute | solution.py:624
  17.9 1.3 %collective-permute-start.6 = (f32[192,128]{1,0:T(8,128)S(1)}, f32[192,128]{1,0:T(8,128)S(1)}, u32[]{:S(2)}, u32[]{:S(2)}) collective-permute-start(f32[192,128]{1,0:T(8,128)S(1)} %get-tuple-element.43), channel_id=1, source_target_pairs={{0,24},{2,26},{4,28},{6,30},{8,0},{10,2},{12,4},{14,6},{16,8},{18,... | collective-permute-start | bytes 294920 | tf_op jit(solution)/shard_map/ppermute | solution.py:624
  19.2 1.5 %collective-permute-start.8 = (f32[192,128]{1,0:T(8,128)S(1)}, f32[192,128]{1,0:T(8,128)S(1)}, u32[]{:S(2)}, u32[]{:S(2)}) collective-permute-start(f32[192,128]{1,0:T(8,128)S(1)} %get-tuple-element.37.after.rest_2_), channel_id=1, source_target_pairs={{0,1},{1,0},{2,3},{3,2},{4,5},{5,4},{6,7},{7,6},{8,9},{9,8},{10,11... | collective-permute-start | bytes 294920 | tf_op jit(solution)/shard_map/ppermute | solution.py:600
  20.8 2.0 %relation.1 = (f32[2,64,64]{2,1,0:T(8,128)S(1)}, f32[2,128,128]{2,1,0:T(8,128)S(1)}, f32[2,64,64]{2,1,0:T(8,128)S(1)}, f32[2,128,128]{2,1,0:T(8,128)S(1)}, f32[3...) custom-call(s32[1]{0:T(128)S(6)} %copy.17.below, s32[1]{0:T(128)S(6)} %copy.18.above, ...), custom_call_target="tpu_custom_call" | custom-call | flops 100000000 | bytes 2097152 | tf_op jit(solution)/shard_map/relation/pallas_call | solution.py:654
  22.8 1.9 %collective-permute-done.5.refs_2_ = f32[192,128]{1,0:T(8,128)S(1)} collective-permute-done((f32[192,128]{1,0:T(8,128)S(1)}, f32[192,128]{1,0:T(8,128)S(1)}, u32[]{:S(2)}, u32[]{:S(2)}) %collective-permute-start.5) | collective-permute-done | bytes 98336 | tf_op jit(solution)/shard_map/ppermute | solution.py:624
  24.7 1.6 %collective-permute-start.7 = (f32[192,128]{1,0:T(8,128)S(1)}, f32[192,128]{1,0:T(8,128)S(1)}, u32[]{:S(2)}, u32[]{:S(2)}) collective-permute-start(f32[192,128]{1,0:T(8,128)S(1)} %pick.2.after.rest_0_), channel_id=1, source_target_pairs={{0,1},{1,0},{2,3},{3,2},{4,5},{5,4},{6,7},{7,6},{8,9},{9,8},{10,11... | collective-permute-start | bytes 294920 | tf_op jit(solution)/shard_map/ppermute | solution.py:600
  26.3 4.8 %unforced.1 = (f32[2048,128]{1,0:T(8,128)S(1)}, f32[2048,128]{1,0:T(8,128)S(1)}) custom-call(s32[1]{0:T(128)S(6)} %copy.16.extent, s32[1]{0:T(128)} %bitcast.own, f32[192,128]{1,0:T(8,128)S(1)} %pick.2.after.rest_0_, f32[32,64,128]{2,1,0:T(8,128)S(1)} %copy-done.1, f32[32,64,128]{2,1,0:T(8,128)S(1)} %copy-done.3, bf16[256,256]{1,0:T(8,128)(2,1)S(1)} %copy-done.5, ...), custom_call_target="tpu_custom_call" | custom-call | flops 1000000000 | bytes 4194304 | tf_op jit(solution)/shard_map/unforced/pallas_call | solution.py:672
  34.6 3.2 %between.1 = (f32[32,64,128]{2,1,0:T(8,128)}, f32[32,64,128]{2,1,0:T(8,128)S(1)}, bf16[64,144]{1,0:T(8,128)(2,1)S(1)}, bf16[64,144]{1,0:T(8,128)(2,1)S(1)}, bf16[64,192]{1,0:T(8,128)(2,1)S(1)}) custom-call(s32[1]{0:T(128)S(6)} %copy.16.extent, s32[1]{0:T(128)} %bitcast.own, f32[32,64,128]{2,1,0:T(8,128)S(1)} %copy-done.1, f32[32,64,128]{2,1,0:T(8,128)S(1)} %copy-done.3, ...), custom_call_target="tpu_custom_call" | custom-call | flops 1000000000 | bytes 4194304 | tf_op jit(solution)/shard_map/between/pallas_call | solution.py:700
  37.8 1.5 %collective-permute-done.10.refs_2_ = f32[200,128]{1,0:T(8,128)S(1)} collective-permute-done((f32[200,128]{1,0:T(8,128)S(1)}, f32[200,128]{1,0:T(8,128)S(1)}, u32[]{:S(2)}, u32[]{:S(2)}) %collective-permute-start.10) | collective-permute-done | bytes 102432 | tf_op jit(solution)/shard_map/ppermute | solution.py:607
  39.4 2.6 %collective-permute-start.12 = (f32[192,128]{1,0:T(8,128)S(1)}, f32[192,128]{1,0:T(8,128)S(1)}, u32[]{:S(2)}, u32[]{:S(2)}) collective-permute-start(f32[192,128]{1,0:T(8,128)S(1)} %get-tuple-element.58), channel_id=1, source_target_pairs={{0,8},{2,10},{4,12},{6,14},{8,16},{10,18},{12,20},{14,22},{16,24},... | collective-permute-start | bytes 294920 | tf_op jit(solution)/shard_map/ppermute | solution.py:624
  42.0 1.6 %collective-permute-start.13 = (f32[192,128]{1,0:T(8,128)S(1)}, f32[192,128]{1,0:T(8,128)S(1)}, u32[]{:S(2)}, u32[]{:S(2)}) collective-permute-start(f32[192,128]{1,0:T(8,128)S(1)} %get-tuple-element.59), channel_id=1, source_target_pairs={{0,16},{2,18},{4,20},{6,22},{8,24},{10,26},{12,28},{14,30},{16,0},... | collective-permute-start | bytes 294920 | tf_op jit(solution)/shard_map/ppermute | solution.py:624
  43.6 0.8 %collective-permute-start.14 = (f32[192,128]{1,0:T(8,128)S(1)}, f32[192,128]{1,0:T(8,128)S(1)}, u32[]{:S(2)}, u32[]{:S(2)}) collective-permute-start(f32[192,128]{1,0:T(8,128)S(1)} %get-tuple-element.60), channel_id=1, source_target_pairs={{0,24},{2,26},{4,28},{6,30},{8,0},{10,2},{12,4},{14,6},{16,8},{18,... | collective-permute-start | bytes 294920 | tf_op jit(solution)/shard_map/ppermute | solution.py:624
  44.5 1.7 %first.1.after.rest_2_ = f32[2048,128]{1,0:T(8,128)S(1)} custom-call(s32[1]{0:T(128)} %bitcast.own, f32[384,128]{1,0:T(8,128)S(1)} %get-tuple-element.51.force, bf16[64,192]{1,0:T(8,128)(2,1)S(1)} %get-tuple-element.55.gstack, bf16[256,256]{1,0:T(8,128)(2,1)S(1)} %copy-done.5, bf16[2,32,192]{2,1,0:T(8,128)(2,1)S(1)} %copy-done.7, ...), custom_call_target="tpu_custom_call" | custom-call | flops 1000000000 | bytes 2097152 | tf_op jit(solution)/shard_map/first/pallas_call | solution.py:715
  46.2 0.9 %collective-permute-done.12.refs_1_ = f32[192,128]{1,0:T(8,128)S(1)} collective-permute-done((f32[192,128]{1,0:T(8,128)S(1)}, f32[192,128]{1,0:T(8,128)S(1)}, u32[]{:S(2)}, u32[]{:S(2)}) %collective-permute-start.12) | collective-permute-done | bytes 98336 | tf_op jit(solution)/shard_map/ppermute | solution.py:624
  47.0 3.4 %collective-permute-done.13.refs_2_ = f32[192,128]{1,0:T(8,128)S(1)} collective-permute-done((f32[192,128]{1,0:T(8,128)S(1)}, f32[192,128]{1,0:T(8,128)S(1)}, u32[]{:S(2)}, u32[]{:S(2)}) %collective-permute-start.13) | collective-permute-done | bytes 98336 | tf_op jit(solution)/shard_map/ppermute | solution.py:624
  50.6 0.8 %collective-permute-start.15 = (f32[192,128]{1,0:T(8,128)S(1)}, f32[192,128]{1,0:T(8,128)S(1)}, u32[]{:S(2)}, u32[]{:S(2)}) collective-permute-start(f32[192,128]{1,0:T(8,128)S(1)} %pick.3.rest_0_), channel_id=1, source_target_pairs={{0,1},{1,0},{2,3},{3,2},{4,5},{5,4},{6,7},{7,6},{8,9},{9,8},{10,11... | collective-permute-start | bytes 294920 | tf_op jit(solution)/shard_map/ppermute | solution.py:600
  52.1 9.2 %collective-permute-done.15.rest_1_ = f32[192,128]{1,0:T(8,128)S(1)} collective-permute-done((f32[192,128]{1,0:T(8,128)S(1)}, f32[192,128]{1,0:T(8,128)S(1)}, u32[]{:S(2)}, u32[]{:S(2)}) %collective-permute-start.15) | collective-permute-done | bytes 98336 | tf_op jit(solution)/shard_map/ppermute | solution.py:600
  61.2 3.5 %last.1 = (f32[32,64,128]{2,1,0:T(8,128)}, f32[2048,128]{1,0:T(8,128)}) custom-call(s32[1]{0:T(128)} %bitcast.own, f32[384,128]{1,0:T(8,128)S(1)} %near.1, f32[2,64,64]{2,1,0:T(8,128)S(1)} %get-tuple-element.45.tx, f32[2,128,128]{2,1,0:T(8,128)S(1)} %get-tuple-element.46.uy, f32[32,64,128]{2,1,0:T(8,128)S(1)} %get-tuple-element.52.after.onward, ...), custom_call_target="tpu_custom_call" | custom-call | flops 1000000000 | bytes 6291456 | tf_op jit(solution)/shard_map/last/pallas_call | solution.py:736
  (49 shorter events, 6.8 us)
Async XLA Ops:
  3.8 4.0 %copy-start.1 = (f32[32,64,128]{2,1,0:T(8,128)S(1)}, f32[32,64,128]{2,1,0:T(8,128)}, u32[]{:S(2)}) copy-start(f32[32,64,128]{2,1,0:T(8,128)} %now.7) | copy-start | bytes 3145732
  4.6 8.7 %collective-permute-start.2 = (f32[200,128]{1,0:T(8,128)S(1)}, f32[200,128]{1,0:T(8,128)S(1)}, u32[]{:S(2)}, u32[]{:S(2)}) collective-permute-start(f32[200,128]{1,0:T(8,128)S(1)} %get-tuple-element.34.packet.refs_0_), channel_id=1, source_target_pairs={{0,6},{2,4},{4,2},{6,0},{8,14},{10,12},{12,10},{14,8},{16,22},{18,... | collective-permute-start | bytes 307208 | tf_op jit(solution)/shard_map/ppermute | solution.py:607
  7.1 6.2 %collective-permute-start.1 = (f32[200,128]{1,0:T(8,128)S(1)}, f32[200,128]{1,0:T(8,128)S(1)}, u32[]{:S(2)}, u32[]{:S(2)}) collective-permute-start(f32[200,128]{1,0:T(8,128)S(1)} %get-tuple-element.34.packet.refs_0_), channel_id=1, source_target_pairs={{0,4},{2,6},{4,0},{6,2},{8,12},{10,14},{12,8},{14,10},{16,20},{18,... | collective-permute-start | bytes 307208 | tf_op jit(solution)/shard_map/ppermute | solution.py:607
  7.7 5.6 %collective-permute-start = (f32[200,128]{1,0:T(8,128)S(1)}, f32[200,128]{1,0:T(8,128)S(1)}, u32[]{:S(2)}, u32[]{:S(2)}) collective-permute-start(f32[200,128]{1,0:T(8,128)S(1)} %get-tuple-element.34.packet.refs_0_), channel_id=1, source_target_pairs={{0,2},{2,0},{4,6},{6,4},{8,10},{10,8},{12,14},{14,12},{16,18},{18,... | collective-permute-start | bytes 307208 | tf_op jit(solution)/shard_map/ppermute | solution.py:607
  11.5 9.3 %collective-permute-start.3 = (f32[192,128]{1,0:T(8,128)S(1)}, f32[192,128]{1,0:T(8,128)S(1)}, u32[]{:S(2)}, u32[]{:S(2)}) collective-permute-start(f32[192,128]{1,0:T(8,128)S(1)} %get-tuple-element.39.rest_0_), channel_id=1, source_target_pairs={{0,1},{1,0},{2,3},{3,2},{4,5},{5,4},{6,7},{7,6},{8,9},{9,8},{10,11... | collective-permute-start | bytes 294920 | tf_op jit(solution)/shard_map/ppermute | solution.py:600
  13.3 7.5 %copy-start.4 = (f32[512,128]{1,0:T(8,128)S(1)}, f32[512,128]{1,0:T(8,128)}, u32[]{:S(2)}) copy-start(f32[512,128]{1,0:T(8,128)} %constant.25.clone.ytall) | copy-start | bytes 786436
  13.3 7.4 %copy-start.6 = (f32[256,64]{1,0:T(8,128)S(1)}, f32[256,64]{1,0:T(8,128)}, u32[]{:S(2)}) copy-start(f32[256,64]{1,0:T(8,128)} %constant.24.clone.xtall) | copy-start | bytes 196612
  13.3 7.4 %copy-start.10 = (s32[1,2]{1,0:T(1,128)S(1)}, s32[1,2]{1,0:T(1,128)}, u32[]{:S(2)}) copy-start(s32[1,2]{1,0:T(1,128)} %x_shift.1) | copy-start | bytes 28
  13.4 7.4 %copy-start.11 = (s32[1,2]{1,0:T(1,128)S(1)}, s32[1,2]{1,0:T(1,128)}, u32[]{:S(2)}) copy-start(s32[1,2]{1,0:T(1,128)} %y_shift.1) | copy-start | bytes 28
  13.5 12.9 %copy-start.3 = (f32[32,64,128]{2,1,0:T(8,128)S(1)}, f32[32,64,128]{2,1,0:T(8,128)}, u32[]{:S(2)}) copy-start(f32[32,64,128]{2,1,0:T(8,128)} %prev.5) | copy-start | bytes 3145732
  13.5 9.3 %collective-permute-start.4 = (f32[192,128]{1,0:T(8,128)S(1)}, f32[192,128]{1,0:T(8,128)S(1)}, u32[]{:S(2)}, u32[]{:S(2)}) collective-permute-start(f32[192,128]{1,0:T(8,128)S(1)} %get-tuple-element.41), channel_id=1, source_target_pairs={{0,8},{2,10},{4,12},{6,14},{8,16},{10,18},{12,20},{14,22},{16,24},... | collective-permute-start | bytes 294920 | tf_op jit(solution)/shard_map/ppermute | solution.py:624
  15.3 9.4 %collective-permute-start.5 = (f32[192,128]{1,0:T(8,128)S(1)}, f32[192,128]{1,0:T(8,128)S(1)}, u32[]{:S(2)}, u32[]{:S(2)}) collective-permute-start(f32[192,128]{1,0:T(8,128)S(1)} %get-tuple-element.42), channel_id=1, source_target_pairs={{0,16},{2,18},{4,20},{6,22},{8,24},{10,26},{12,28},{14,30},{16,0},... | collective-permute-start | bytes 294920 | tf_op jit(solution)/shard_map/ppermute | solution.py:624
  17.9 6.8 %collective-permute-start.6 = (f32[192,128]{1,0:T(8,128)S(1)}, f32[192,128]{1,0:T(8,128)S(1)}, u32[]{:S(2)}, u32[]{:S(2)}) collective-permute-start(f32[192,128]{1,0:T(8,128)S(1)} %get-tuple-element.43), channel_id=1, source_target_pairs={{0,24},{2,26},{4,28},{6,30},{8,0},{10,2},{12,4},{14,6},{16,8},{18,... | collective-permute-start | bytes 294920 | tf_op jit(solution)/shard_map/ppermute | solution.py:624
  19.2 11.9 %collective-permute-start.8 = (f32[192,128]{1,0:T(8,128)S(1)}, f32[192,128]{1,0:T(8,128)S(1)}, u32[]{:S(2)}, u32[]{:S(2)}) collective-permute-start(f32[192,128]{1,0:T(8,128)S(1)} %get-tuple-element.37.after.rest_2_), channel_id=1, source_target_pairs={{0,1},{1,0},{2,3},{3,2},{4,5},{5,4},{6,7},{7,6},{8,9},{9,8},{10,11... | collective-permute-start | bytes 294920 | tf_op jit(solution)/shard_map/ppermute | solution.py:600
  24.7 6.4 %collective-permute-start.7 = (f32[192,128]{1,0:T(8,128)S(1)}, f32[192,128]{1,0:T(8,128)S(1)}, u32[]{:S(2)}, u32[]{:S(2)}) collective-permute-start(f32[192,128]{1,0:T(8,128)S(1)} %pick.2.after.rest_0_), channel_id=1, source_target_pairs={{0,1},{1,0},{2,3},{3,2},{4,5},{5,4},{6,7},{7,6},{8,9},{9,8},{10,11... | collective-permute-start | bytes 294920 | tf_op jit(solution)/shard_map/ppermute | solution.py:600
  31.9 5.9 %collective-permute-start.11 = (f32[200,128]{1,0:T(8,128)S(1)}, f32[200,128]{1,0:T(8,128)S(1)}, u32[]{:S(2)}, u32[]{:S(2)}) collective-permute-start(f32[200,128]{1,0:T(8,128)S(1)} %get-tuple-element.56.refs_0_), channel_id=1, source_target_pairs={{0,6},{2,4},{4,2},{6,0},{8,14},{10,12},{12,10},{14,8},{16,22},{18,... | collective-permute-start | bytes 307208 | tf_op jit(solution)/shard_map/ppermute | solution.py:607
  32.7 6.6 %collective-permute-start.10 = (f32[200,128]{1,0:T(8,128)S(1)}, f32[200,128]{1,0:T(8,128)S(1)}, u32[]{:S(2)}, u32[]{:S(2)}) collective-permute-start(f32[200,128]{1,0:T(8,128)S(1)} %get-tuple-element.56.refs_0_), channel_id=1, source_target_pairs={{0,4},{2,6},{4,0},{6,2},{8,12},{10,14},{12,8},{14,10},{16,20},{18,... | collective-permute-start | bytes 307208 | tf_op jit(solution)/shard_map/ppermute | solution.py:607
  33.6 5.8 %collective-permute-start.9 = (f32[200,128]{1,0:T(8,128)S(1)}, f32[200,128]{1,0:T(8,128)S(1)}, u32[]{:S(2)}, u32[]{:S(2)}) collective-permute-start(f32[200,128]{1,0:T(8,128)S(1)} %get-tuple-element.56.refs_0_), channel_id=1, source_target_pairs={{0,2},{2,0},{4,6},{6,4},{8,10},{10,8},{12,14},{14,12},{16,18},{18,... | collective-permute-start | bytes 307208 | tf_op jit(solution)/shard_map/ppermute | solution.py:607
  33.8 27.4 %collective-permute-start.16 = (f32[2048,128]{1,0:T(8,128)S(1)}, f32[2048,128]{1,0:T(8,128)S(1)}, u32[]{:S(2)}, u32[]{:S(2)}) collective-permute-start(f32[2048,128]{1,0:T(8,128)S(1)} %get-tuple-element.61), channel_id=1, source_target_pairs={{0,1},{1,0},{2,3},{3,2},{4,5},{5,4},{6,7},{7,6},{8,9},{9,8},{10,11... | collective-permute-start | bytes 3145736 | tf_op jit(solution)/shard_map/ppermute | solution.py:682
  39.3 5.2 %copy-start.7 = (bf16[2,32,192]{2,1,0:T(8,128)(2,1)S(1)}, bf16[2,32,192]{2,1,0:T(8,128)(2,1)}, u32[]{:S(2)}) copy-start(bf16[2,32,192]{2,1,0:T(8,128)(2,1)} %constant.22.clone.xown) | copy-start | bytes 73732
  39.4 7.6 %collective-permute-start.12 = (f32[192,128]{1,0:T(8,128)S(1)}, f32[192,128]{1,0:T(8,128)S(1)}, u32[]{:S(2)}, u32[]{:S(2)}) collective-permute-start(f32[192,128]{1,0:T(8,128)S(1)} %get-tuple-element.58), channel_id=1, source_target_pairs={{0,8},{2,10},{4,12},{6,14},{8,16},{10,18},{12,20},{14,22},{16,24},... | collective-permute-start | bytes 294920 | tf_op jit(solution)/shard_map/ppermute | solution.py:624
  42.0 8.4 %collective-permute-start.13 = (f32[192,128]{1,0:T(8,128)S(1)}, f32[192,128]{1,0:T(8,128)S(1)}, u32[]{:S(2)}, u32[]{:S(2)}) collective-permute-start(f32[192,128]{1,0:T(8,128)S(1)} %get-tuple-element.59), channel_id=1, source_target_pairs={{0,16},{2,18},{4,20},{6,22},{8,24},{10,26},{12,28},{14,30},{16,0},... | collective-permute-start | bytes 294920 | tf_op jit(solution)/shard_map/ppermute | solution.py:624
  43.6 6.9 %collective-permute-start.14 = (f32[192,128]{1,0:T(8,128)S(1)}, f32[192,128]{1,0:T(8,128)S(1)}, u32[]{:S(2)}, u32[]{:S(2)}) collective-permute-start(f32[192,128]{1,0:T(8,128)S(1)} %get-tuple-element.60), channel_id=1, source_target_pairs={{0,24},{2,26},{4,28},{6,30},{8,0},{10,2},{12,4},{14,6},{16,8},{18,... | collective-permute-start | bytes 294920 | tf_op jit(solution)/shard_map/ppermute | solution.py:624
  50.6 10.7 %collective-permute-start.15 = (f32[192,128]{1,0:T(8,128)S(1)}, f32[192,128]{1,0:T(8,128)S(1)}, u32[]{:S(2)}, u32[]{:S(2)}) collective-permute-start(f32[192,128]{1,0:T(8,128)S(1)} %pick.3.rest_0_), channel_id=1, source_target_pairs={{0,1},{1,0},{2,3},{3,2},{4,5},{5,4},{6,7},{7,6},{8,9},{9,8},{10,11... | collective-permute-start | bytes 294920 | tf_op jit(solution)/shard_map/ppermute | solution.py:600
  (6 other events, 10.0 us)
